TPU v7x, 32 devices: a whole 2x2x4 slice. The times are simulated.
32 devices in a mesh: video: 4 (over y, x), tm: 2 (over core), space: 4 (over z).
Axes of the slice: x: 2, y: 2, z: 4, core: 2. Of those that a mesh axis runs over, the one named last changes fastest.
Arguments:
- feature_maps: bfloat16 [8, 128, 240, 128], P(('video', 'tm'), 'space'), parts along dimension 0, may hold values from -27 to 27
- query_frame: int32 [2048], P('video'), parts along dimension 0, may hold values from 0 to 1
- query_row: int32 [2048], P('video'), parts along dimension 0, may hold values from 0 to 127
- query_col: int32 [2048], P('video'), parts along dimension 0, may hold values from 0 to 239
- ema_decay: float32 [8, 128], P(('video', 'tm')), parts along dimension 0, may hold values from 0.14 to 1
- dw_kernel: float32 [3, 128], replicated, may hold values from -3 to 3
- pw_weight: bfloat16 [128, 128], replicated, may hold values from -0.5 to 0.5
- out_weight: float32 [2, 128], replicated, may hold values from -2 to 2
Outputs:
- tracks: float32 [8, 2, 512], P(('video', 'tm')), parts along dimension 0
There are 4 independent parts, one for each index of `video`. A program takes and returns all parts, laid end to end along the dimension named above; an argument that names none is the same for every part. Nothing has to cross between parts.
All inputs are finite; a program needn't handle non-finite values.
Results may differ from a plain program's by a relative error of at most 0.0026.
Values may be sent and summed in bfloat16 or wider, within the bound.
No kernel may reach another device: no remote copies, remote signals or barrier semaphores. Data moves between devices by JAX's collectives and lax.ppermute only.
A program may use at most 128 MiB of HBM per device.

v0:
```python
import math

import jax
import jax.numpy as jnp
from jax import lax
from jax.sharding import PartitionSpec as P


def with_halo(cells, sides, width):
    for axis, dim in sides:
        count = lax.axis_size(axis)
        ends = count - 1
        head = lax.slice_in_dim(cells, 0, width, axis=dim)
        tail = lax.slice_in_dim(cells, cells.shape[dim] - width, cells.shape[dim], axis=dim)
        cells = jnp.concatenate(
            [
                lax.ppermute(tail, axis, [(i, (i + 1) % count) for i in range(ends)]),
                cells,
                lax.ppermute(head, axis, [((i + 1) % count, i) for i in range(ends)]),
            ],
            axis=dim,
        )
    return cells


def local(
    feature_maps, query_frame, query_row, query_col, ema_decay, dw_kernel, pw_weight, out_weight
):
    frames_here, rows_here, map_width, channels = feature_maps.shape
    num_queries = query_frame.shape[0]
    first_frame = lax.axis_index("tm") * frames_here
    first_row = lax.axis_index("space") * rows_here
    map_height = rows_here * lax.axis_size("space")
    local_frame = query_frame - first_frame
    local_row = query_row - first_row
    owned = (
        (local_frame >= 0)
        & (local_frame < frames_here)
        & (local_row >= 0)
        & (local_row < rows_here)
    )
    picked = feature_maps[
        jnp.clip(local_frame, 0, frames_here - 1), jnp.clip(local_row, 0, rows_here - 1), query_col
    ]
    contrib = jnp.where(owned[:, None], picked.astype(jnp.float32), 0.0)
    query_feats = lax.psum(contrib, ("tm", "space")).astype(jnp.bfloat16)
    scale = 1.0 / math.sqrt(channels)
    col_coord = jnp.arange(map_width, dtype=jnp.int32).astype(jnp.float32) / map_width
    row_coord = (first_row + jnp.arange(rows_here, dtype=jnp.int32)).astype(
        jnp.float32
    ) / map_height
    highest_list, total_list, pos_list, feat_list = ([], [], [], [])
    frame_index = 0
    frame_map = feature_maps[frame_index].reshape(rows_here * map_width, channels)
    scores = (
        lax.dot_general(
            query_feats, frame_map, (((1,), (1,)), ((), ())), preferred_element_type=jnp.float32
        )
        * scale
    )
    highest = jnp.max(scores, axis=1)
    weights_exp = jnp.exp(scores - highest[:, None])
    highest_list.append(highest)
    total_list.append(jnp.sum(weights_exp, axis=1))
    grid = weights_exp.reshape(num_queries, rows_here, map_width)
    col_part = jnp.sum(jnp.sum(grid, axis=1) * col_coord[None, :], axis=1)
    line_portion = jnp.sum(jnp.sum(grid, axis=2) * row_coord[None, :], axis=1)
    pos_list.append(jnp.stack([col_part, line_portion], 1))
    feat_list.append(
        jnp.dot(weights_exp.astype(jnp.bfloat16), frame_map, preferred_element_type=jnp.float32)
    )
    highest = jnp.stack(highest_list)
    totals = jnp.stack(total_list)
    pos_sum = jnp.stack(pos_list)
    feat_sum = jnp.stack(feat_list)
    top_value = lax.pmax(highest, "space")
    factor = jnp.exp(highest - top_value)
    grand_total, pos_all, feat_all = lax.psum(
        (factor * totals, factor[..., None] * pos_sum, factor[..., None] * feat_sum), "space"
    )
    position = pos_all / grand_total[..., None]
    focused_result = (feat_all / grand_total[..., None]).astype(jnp.bfloat16)
    padded = with_halo(focused_result, (("tm", 0),), 1).astype(jnp.float32)
    depth = jnp.zeros((frames_here, num_queries, channels), jnp.float32)
    for tap in range(dw_kernel.shape[0]):
        depth = depth + dw_kernel[tap][None, None, :] * padded[tap : tap + frames_here]
    hidden = jax.nn.gelu(depth).astype(jnp.bfloat16)
    mixed = jnp.dot(
        hidden.reshape(-1, channels), pw_weight, preferred_element_type=jnp.float32
    ).reshape(frames_here, num_queries, channels)
    refined = focused_result.astype(jnp.float32) + mixed
    carried = jnp.zeros((num_queries, channels), jnp.float32)
    retain_prod = jnp.ones((channels,), jnp.float32)
    local_states, local_prods = ([], [])
    frame_index = 0
    retain = ema_decay[frame_index]
    carried = retain[None, :] * carried + (1.0 - retain[None, :]) * refined[frame_index]
    retain_prod = retain_prod * retain
    local_states.append(carried)
    local_prods.append(retain_prod)
    all_prods, all_ends = (
        lax.all_gather(retain_prod[None], "tm", axis=0, tiled=True),
        lax.all_gather(carried[None], "tm", axis=0, tiled=True),
    )
    position_tm = lax.axis_index("tm")

    def fold_step(source, running):
        advanced = all_prods[source][None, :] * running + all_ends[source]
        return jnp.where(source < position_tm, advanced, running)

    incoming = lax.fori_loop(
        0, lax.axis_size("tm"), fold_step, jnp.zeros((num_queries, channels), jnp.float32)
    )
    memory = jnp.stack(local_states) + jnp.stack(local_prods)[:, None, :] * incoming[None]
    delta = jnp.einsum("tqc,kc->tkq", memory, out_weight, precision=lax.Precision.HIGHEST)
    return jnp.transpose(position, (0, 2, 1)) + delta


def solution(mesh):
    placed = (
        P(("video", "tm"), "space", None, None),
        P("video"),
        P("video"),
        P("video"),
        P(("video", "tm"), None),
        P(),
        P(),
        P(),
    )
    return jax.shard_map(
        local, mesh=mesh, in_specs=placed, out_specs=P(("video", "tm"), None, None), check_vma=False
    )
```

profile of v0, /device:TPU:0, one launch (start us, length us, event | category | flops | bytes accessed | tf_op | source)
XLA Modules:
  0.0 128.0 jit_solution(10686366909794556137)
XLA Ops:
  6.5 0.0 copy-start
  6.5 0.0 all-reduce.4.cloned.1.call-start
  6.5 0.8 compare_and_fusion
  7.4 0.7 fusion.41
  8.1 0.0 copy-done
  8.1 3.1 %gather_fusion = bf16[512,128]{1,0:T(8,128)(2,1)S(1)} fusion(bf16[1,32,240,128]{3,2,1,0:T(8,128)(2,1)S(1)} %copy-done, s32[512]{0:T(512)S(1)} %fusion.41), kind=kCustom, calls=%fused_computation | custom fusion | bytes 268288 | tf_op jit(solution)/shard_map/gather | solution.py:42
  11.3 0.1 convert_select_fusion
  11.4 37.3 %all-reduce.5 = bf16[512,128]{1,0:T(8,128)(2,1)S(1)} all-reduce(f32[512,128]{1,0:T(8,128)S(1)} %convert_select_fusion), channel_id=1, replica_groups=mesh['video'=4,'tm'=2,'space'=4] {'tm','space'}, use_global_device_ids=true, to_apply=%region_0.1 | all-reduce | flops 65536 | bytes 393216 | tf_op jit(solution)/shard_map/psum | solution.py:46
  48.7 2.3 %multiply_reduce_fusion = (f32[512]{0:T(512)S(1)}, f32[512,7680]{1,0:T(8,128)S(1)}) fusion(bf16[512,128]{1,0:T(8,128)(2,1)S(1)} %all-reduce.5, bf16[7680,128]{1,0:T(8,128)(2,1)S(1)} %bitcast.61), kind=kOutput, calls=%fused_computation.5 | convolution fusion | flops 1014496768 | bytes 17827840 | tf_op jit(solution)/shard_map/dot_general | solution.py:56
  51.0 7.0 %fusion.50 = (f32[512]{0:T(512)S(1)}, f32[512,7680]{1,0:T(8,128)}) fusion(f32[512]{0:T(512)S(1)} %get-tuple-element.139, f32[512,7680]{1,0:T(8,128)S(1)} %get-tuple-element.140), kind=kLoop, calls=%fused_computation.74 | loop fusion | flops 11795968 | bytes 31461376 | tf_op jit(solution)/shard_map/reduce_sum | solution.py:64
  58.0 8.8 %pmax.7 = f32[1,512]{1,0:T(1,128)S(1)} all-reduce(f32[1,512]{1,0:T(1,128)S(1)} %bitcast.66), channel_id=1, replica_groups=mesh['video'=4,'tm'=2,'space'=4] {'space'}, use_global_device_ids=true, to_apply=%region_2.3 | all-reduce | flops 512 | bytes 4096 | tf_op jit(solution)/shard_map/pmax | solution.py:76
  66.8 8.4 %fusion.7 = f32[1,512,128]{2,1,0:T(8,128)} fusion(bf16[7680,128]{1,0:T(8,128)(2,1)S(1)} %bitcast.62, f32[512,7680]{1,0:T(8,128)} %get-tuple-element.135, f32[512]{0:T(512)S(1)} %bitcast.64), kind=kOutput, calls=%fused_computation.11 | convolution fusion | flops 1010630656 | bytes 17958912 | tf_op jit(solution)/shard_map/dot_general | solution.py:70
  75.2 0.0 all-reduce.4.cloned.1.call-update
  75.2 15.7 %copy.10 = f32[512,7680]{0,1:T(8,128)} copy(f32[512,7680]{1,0:T(8,128)} %get-tuple-element.135) | data formatting | bytes 31457280 | tf_op jit(solution)/shard_map/exp | solution.py:62
  90.9 0.0 copy-start.3
  90.9 0.0 copy-start.1
  91.0 0.0 copy-start.4
  91.0 0.0 copy-start.2
  91.0 7.8 %fusion.48 = (f32[512,240]{0,1:T(8,128)S(1)}, f32[512,32]{0,1:T(8,128)S(1)}) fusion(f32[512,32,240]{0,2,1:T(8,128)} %bitcast.63), kind=kLoop, calls=%fused_computation.72 | loop fusion | flops 7725056 | bytes 16285696 | tf_op jit(solution)/shard_map/reduce_sum | solution.py:66
  98.8 0.1 multiply_reduce_fusion.2
  98.9 0.1 multiply_reduce_fusion.1
  99.1 0.0 copy-done.3
  99.1 1.8 %all-gather = f32[2,1,128]{2,1,0:T(1,128)S(1)} all-gather(f32[1,1,128]{2,1,0:T(1,128)S(1)} %bitcast.72), channel_id=1, replica_groups=mesh['video'=4,'tm'=2,'space'=4] {'tm'}, dimensions={0}, use_global_device_ids=true | all-gather | bytes 1536 | tf_op jit(solution)/shard_map/all_gather | solution.py:102
  100.8 10.1 %all-reduce = (f32[512]{0:T(512)S(1)}, f32[1,512,2]{1,2,0:T(2,128)S(1)}) all-reduce(f32[512]{0:T(512)S(1)} %bitcast.70, f32[1,512,2]{1,2,0:T(2,128)S(1)} %maximum_multiply_fusion), channel_id=1, replica_groups=mesh['video'=4,'tm'=2,'space'=4] {'space'}, use_global_device_ids=true, to_apply=%region_9.10 | all-reduce | flops 1536 | bytes 12288 | tf_op jit(solution)/shard_map/psum | solution.py:78
  111.0 0.0 copy-done.1
  111.0 0.0 all-reduce.4.cloned.1.call-done
  111.0 1.1 divide_convert_fusion
  112.1 1.3 %collective-permute-start.1 = (bf16[1,512,128]{2,1,0:T(8,128)(2,1)S(1)}, bf16[1,512,128]{2,1,0:T(8,128)(2,1)S(1)}, u32[]{:S(2)}, u32[]{:S(2)}) collective-permute-start(bf16[1,512,128]{2,1,0:T(8,128)(2,1)S(1)} %divide_convert_fusion), channel_id=1, source_target_pairs={{4,0},{5,1},{6,2},{7,3},{12,8},{13,9},{14,10},{15,11},{20,16},{21,... | collective-permute-start | bytes 393224 | tf_op jit(solution)/shard_map/ppermute | solution.py:19
  113.4 3.0 %collective-permute-start = (bf16[1,512,128]{2,1,0:T(8,128)(2,1)S(1)}, bf16[1,512,128]{2,1,0:T(8,128)(2,1)S(1)}, u32[]{:S(2)}, u32[]{:S(2)}) collective-permute-start(bf16[1,512,128]{2,1,0:T(8,128)(2,1)S(1)} %divide_convert_fusion), channel_id=1, source_target_pairs={{0,4},{1,5},{2,6},{3,7},{8,12},{9,13},{10,14},{11,15},{16,20},{17,... | collective-permute-start | bytes 393224 | tf_op jit(solution)/shard_map/ppermute | solution.py:17
  116.5 0.0 collective-permute-done.1
  116.5 0.9 collective-permute-done
  117.4 0.1 maximum_convert_fusion
  117.5 0.0 copy-done.4
  117.5 0.3 multiply_add_fusion
  117.8 2.2 %all_gather.7 = f32[2,512,128]{2,1,0:T(8,128)S(1)} all-gather(f32[1,512,128]{2,1,0:T(8,128)S(1)} %get-tuple-element.141), channel_id=1, replica_groups=mesh['video'=4,'tm'=2,'space'=4] {'tm'}, dimensions={0}, use_global_device_ids=true | all-gather | bytes 786432 | tf_op jit(solution)/shard_map/all_gather | solution.py:103
  119.9 0.3 while.14
  119.9 0.1 fusion.57
  120.1 0.1 fusion.57
  120.2 0.0 copy-done.2
  120.2 1.0 fusion.10
  (10 shorter events, 0.1 us)
Async XLA Ops:
  6.5 1.6 %copy-start = (bf16[1,32,240,128]{3,2,1,0:T(8,128)(2,1)S(1)}, bf16[1,32,240,128]{3,2,1,0:T(8,128)(2,1)}, u32[]{:S(2)}) copy-start(bf16[1,32,240,128]{3,2,1,0:T(8,128)(2,1)} %param.10) | copy-start | bytes 5898244
  6.5 104.5 %all-reduce.4.cloned.1.call-start = ((), (), s32[]{:S(2)}) async-start(), calls=%async_computation | async-start | bytes 524288 | tf_op jit(solution)/shard_map/psum | solution.py:78
  90.9 8.1 %copy-start.3 = (f32[1,128]{1,0:T(1,128)S(1)}, f32[1,128]{1,0:T(1,128)}, u32[]{:S(2)}) copy-start(f32[1,128]{1,0:T(1,128)} %param.14) | copy-start | bytes 1540
  90.9 20.0 %copy-start.1 = (f32[3,128]{1,0:T(4,128)S(1)}, f32[3,128]{1,0:T(4,128)}, u32[]{:S(2)}) copy-start(f32[3,128]{1,0:T(4,128)} %param.15) | copy-start | bytes 4612
  91.0 26.5 %copy-start.4 = (bf16[128,128]{1,0:T(8,128)(2,1)S(1)}, bf16[128,128]{1,0:T(8,128)(2,1)}, u32[]{:S(2)}) copy-start(bf16[128,128]{1,0:T(8,128)(2,1)} %param.16) | copy-start | bytes 98308
  91.0 29.3 %copy-start.2 = (f32[2,128]{1,0:T(2,128)S(1)}, f32[2,128]{1,0:T(2,128)}, u32[]{:S(2)}) copy-start(f32[2,128]{1,0:T(2,128)} %param.17) | copy-start | bytes 3076
  112.1 4.4 %collective-permute-start.1 = (bf16[1,512,128]{2,1,0:T(8,128)(2,1)S(1)}, bf16[1,512,128]{2,1,0:T(8,128)(2,1)S(1)}, u32[]{:S(2)}, u32[]{:S(2)}) collective-permute-start(bf16[1,512,128]{2,1,0:T(8,128)(2,1)S(1)} %divide_convert_fusion), channel_id=1, source_target_pairs={{4,0},{5,1},{6,2},{7,3},{12,8},{13,9},{14,10},{15,11},{20,16},{21,... | collective-permute-start | bytes 393224 | tf_op jit(solution)/shard_map/ppermute | solution.py:19
  113.4 4.0 %collective-permute-start = (bf16[1,512,128]{2,1,0:T(8,128)(2,1)S(1)}, bf16[1,512,128]{2,1,0:T(8,128)(2,1)S(1)}, u32[]{:S(2)}, u32[]{:S(2)}) collective-permute-start(bf16[1,512,128]{2,1,0:T(8,128)(2,1)S(1)} %divide_convert_fusion), channel_id=1, source_target_pairs={{0,4},{1,5},{2,6},{3,7},{8,12},{9,13},{10,14},{11,15},{16,20},{17,... | collective-permute-start | bytes 393224 | tf_op jit(solution)/shard_map/ppermute | solution.py:17
Sparse Core Ops, SparseCore 0:
  75.3 34.7 all-reduce.3
where the time goes:
time: 129 us; the launch traced here: 128 us
  blocking collectives  60.2 us (47%)
  local copies, waits for them, and re-layouts  18.9 us (15%)
  other arithmetic  18.2 us (14%)
  between operations  13.6 us (11%)
  matrix products  11.9 us (9%)
  starting transfers between devices  4.34 us (3%)
    psum x1, blocking collectives, local(): query_feats = lax.psum(contrib, ('tm', 'space')).astype(jnp.bfloat16)  37.3 us
    exp x1, local copies, waits for them, and re-layouts, local(): weights_exp = jnp.exp(scores - highest[:, None])  15.7 us
    psum x1, blocking collectives, local(): lax.psum((factor * totals, factor[..., None] * pos_sum, factor[..., None]...  10.1 us
    pmax x1, blocking collectives, local(): top_value = lax.pmax(highest, 'space')  8.79 us
    dot_general x1, matrix products, local(): jnp.dot(weights_exp.astype(jnp.bfloat16), frame_map, preferred_element_ty...  8.38 us
    reduce_sum x2, other arithmetic, local(): col_part = jnp.sum(jnp.sum(grid, axis=1) * col_coord[None, :], axis=1)  7.96 us
    reduce_sum x1, other arithmetic, local(): total_list.append(jnp.sum(weights_exp, axis=1))  6.99 us
    gather x1, local copies, waits for them, and re-layouts, local(): feature_maps[jnp.clip(local_frame, 0, frames_here - 1), jnp.clip(local_ro...  3.13 us
  transfers between devices with their start and end apart: 3, of which 1 were waited for; matrix products, arithmetic and copies ran while one was open for 19% of the time, Pallas kernels for 0%

commit v1 on v0

v1 whole, which is shorter than its diff:
```python
import functools
import math

import jax
import jax.numpy as jnp
from jax import lax
from jax.experimental import pallas as pl
from jax.experimental.pallas import tpu as pltpu
from jax.sharding import PartitionSpec as P

F32 = jnp.float32
BF16 = jnp.bfloat16
LANES = 128
AUX_ROWS = 8
VMEM_LIMIT = 40 * 1024 * 1024
NT = (((1,), (1,)), ((), ()))


def pick_chunk(total, limit):
    best = None
    for size in range(LANES, limit + 1, LANES):
        if total % size == 0 and (best is None or size % 256 == 0 or best % 256):
            best = size
    return best if best is not None else total


def gather_kernel(rows_here, map_width, frame_ref, row_ref, col_ref, map_ref, *out_refs):
    positions = map_ref.shape[0]
    queries = frame_ref.shape[1]
    tm = lax.axis_index("tm")
    row = row_ref[...] - lax.axis_index("space") * rows_here
    here = (frame_ref[...] == tm) & (row >= 0) & (row < rows_here)
    target = jnp.where(here, row * map_width + col_ref[...], -1)
    target = jnp.transpose(jnp.broadcast_to(target, (LANES, queries)))
    chunk = pick_chunk(positions, 1536)
    picked = None
    for base in range(0, positions, chunk):
        parts = []
        for lane_base in range(base, base + chunk, LANES):
            lane = lax.broadcasted_iota(jnp.int32, (queries, LANES), 1) + lane_base
            parts.append(jnp.where(lane == target, 1.0, 0.0).astype(BF16))
        hot = jnp.concatenate(parts, axis=1)
        term = jnp.dot(hot, map_ref[base : base + chunk, :], preferred_element_type=F32)
        picked = term if picked is None else picked + term
    if len(out_refs) == 1:
        out_refs[0][...] = picked.astype(BF16)
        return
    half = queries // 2
    first, second = picked[:half].astype(F32), picked[half:].astype(F32)
    out_refs[0][...] = jnp.where(tm == 0, first, second).astype(BF16)
    out_refs[1][...] = jnp.where(tm == 0, second, first).astype(BF16)


def volume_kernel(n_groups, rows_here, height, width, *refs):
    *query_refs, map_ref, coord_ref, decay_ref, out_ref = refs
    positions, channels = map_ref.shape
    factor = math.log2(math.e) / math.sqrt(channels)
    part_queries = query_refs[0].shape[0]
    n_parts = len(query_refs)
    group = part_queries * n_parts // n_groups
    feat_rows = out_ref.shape[1] - AUX_ROWS
    first_row = (lax.axis_index("space") * rows_here).astype(F32)
    tm = lax.axis_index("tm")
    chunk = pick_chunk(positions, 1280)
    state = [None] * n_parts
    for base in range(0, positions, chunk):
        keys = map_ref[base : base + chunk, :]
        values = jnp.concatenate([keys, coord_ref[base : base + chunk, :]], axis=1)
        for part in range(n_parts):
            scores = lax.dot_general(
                query_refs[part][...], keys, NT, preferred_element_type=F32
            )
            top = jnp.max(scores, axis=1, keepdims=True) * factor
            if state[part] is not None:
                old_top, old_sum = state[part]
                top = jnp.maximum(top, old_top)
            weights = jnp.exp2(scores * factor - top).astype(BF16)
            sums = jnp.dot(weights, values, preferred_element_type=F32)
            if state[part] is not None:
                sums = sums + jnp.exp2(old_top - top) * old_sum
            state[part] = (top, sums)
    decay = [decay_ref[...]]
    sub = lax.broadcasted_iota(jnp.int32, (AUX_ROWS, LANES), 0)
    for part in range(n_parts):
        top, sums = state[part]
        feats = sums[:, :channels] / sums[:, channels + 2 : channels + 3]
        extra = sums[:, channels:]
        lane = lax.broadcasted_iota(jnp.int32, extra.shape, 1)
        extra = jnp.transpose(jnp.where(lane == 3, top, extra))
        total = extra[2:3]
        rows = [extra[3:4]]
        rows += [total, extra[0:1] / total / width, (extra[1:2] / total + first_row) / height]
        aux = jnp.zeros((AUX_ROWS, part_queries), F32)
        wide = lax.broadcasted_iota(jnp.int32, aux.shape, 0)
        for index, values in enumerate(rows):
            aux = jnp.where(wide == index, values, aux)
        where = part if n_parts == 1 else jnp.where(tm == 0, part, 1 - part)
        groups_here = n_groups // n_parts
        for index in range(groups_here):
            shift = (part_queries - index * group) % part_queries
            block = pltpu.roll(aux, shift, 1) if shift else aux
            block = block[:, :LANES]
            for offset, piece in enumerate(decay):
                block = jnp.where(sub == len(rows) + offset, piece, block)
            pieces = [feats[index * group : (index + 1) * group]]
            if feat_rows > group:
                pieces.append(jnp.zeros((feat_rows - group, LANES), F32))
            pieces.append(block)
            out_ref[where * groups_here + index] = jnp.concatenate(pieces, axis=0).astype(
                out_ref.dtype
            )


def tail_kernel(n_tm, n_space, group, dw_ref, pw_ref, ow_ref, in_ref, out_ref):
    feat_rows = in_ref.shape[1] - AUX_ROWS
    n_blocks = n_tm * n_space
    blocks = [in_ref[index].astype(F32) for index in range(n_blocks)]
    aux = [block[feat_rows:] for block in blocks]
    positions, shares, decays = [], [], []
    for frame in range(n_tm):
        mine = aux[frame * n_space : (frame + 1) * n_space]
        top = mine[0][0:1]
        for block in mine[1:]:
            top = jnp.maximum(top, block[0:1])
        weight = [jnp.exp2(b[0:1] - top) * b[1:2] for b in mine]
        total = sum(weight[1:], weight[0])
        share = [w / total for w in weight]
        shares += share
        across = [s * b[2:3] for s, b in zip(share, mine)]
        down = [s * b[3:4] for s, b in zip(share, mine)]
        positions.append((sum(across[1:], across[0]), sum(down[1:], down[0])))
        decays.append(mine[0][4:5])
    pad_blocks = -(-n_blocks // 8) * 8
    table = jnp.zeros((pad_blocks, LANES), F32)
    sub = lax.broadcasted_iota(jnp.int32, table.shape, 0)
    for index, share in enumerate(shares):
        table = jnp.where(sub == index, share, table)
    table = jnp.transpose(table)
    attended = []
    for frame in range(n_tm):
        value = None
        for index in range(frame * n_space, (frame + 1) * n_space):
            term = table[:group, index : index + 1] * blocks[index][:group]
            value = term if value is None else value + term
        attended.append(value.astype(BF16).astype(F32))
    taps = dw_ref.shape[0]
    hidden = []
    for frame in range(n_tm):
        depth = None
        for tap in range(taps):
            source = frame + tap - taps // 2
            if 0 <= source < n_tm:
                term = dw_ref[tap : tap + 1, :] * attended[source]
                depth = term if depth is None else depth + term
        hidden.append(jax.nn.gelu(depth).astype(BF16).astype(F32))
    hidden = jnp.concatenate(hidden, axis=0).astype(BF16)
    mixed = jnp.dot(hidden, pw_ref[...], preferred_element_type=F32)
    memory = None
    out = jnp.zeros(out_ref.shape, F32)
    out_sub = lax.broadcasted_iota(jnp.int32, out.shape, 0)
    n_out = ow_ref.shape[0]
    for frame in range(n_tm):
        refined = attended[frame] + mixed[frame * group : (frame + 1) * group]
        fresh = (1.0 - decays[frame]) * refined
        memory = fresh if memory is None else decays[frame] * memory + fresh
        padded = memory
        if group < LANES:
            padded = jnp.concatenate([memory, jnp.zeros((LANES - group, LANES), F32)], axis=0)
        delta = lax.dot_general(
            ow_ref[...], padded, NT, preferred_element_type=F32, precision=lax.Precision.HIGHEST
        )
        for axis in range(n_out):
            line = positions[frame][axis] + delta[axis : axis + 1]
            out = jnp.where(out_sub == frame * n_out + axis, line, out)
    out_ref[...] = out


def call(kernel, out_shape, n_in, **cost):
    vmem = pl.BlockSpec(memory_space=pltpu.VMEM)
    return pl.pallas_call(
        kernel,
        out_shape=out_shape,
        in_specs=[vmem] * n_in,
        out_specs=jax.tree.map(lambda _: vmem, out_shape),
        compiler_params=pltpu.CompilerParams(vmem_limit_bytes=VMEM_LIMIT),
        cost_estimate=pl.CostEstimate(**cost),
    )


def swap(value, axis, bit):
    return lax.ppermute(value, axis, [(i, i ^ bit) for i in range(lax.axis_size(axis))])


def all_sum(value, axis):
    count = lax.axis_size(axis)
    if count & (count - 1):
        return lax.psum(value, axis)
    bit = 1
    while bit < count:
        value = value + swap(value, axis, bit)
        bit *= 2
    return value


def local(
    feature_maps, query_frame, query_row, query_col, ema_decay, dw_kernel, pw_weight, out_weight
):
    frames_here, rows_here, map_width, channels = feature_maps.shape
    assert frames_here == 1 and channels == LANES
    queries = query_frame.shape[0]
    n_tm, n_space = lax.axis_size("tm"), lax.axis_size("space")
    n_groups = n_tm * n_space
    group = queries // n_groups
    height = rows_here * n_space
    positions = rows_here * map_width
    maps = feature_maps.reshape(positions, channels)
    halves = 2 if n_tm == 2 else 1
    part = jax.ShapeDtypeStruct((queries // halves, channels), BF16)

    picked = call(
        functools.partial(gather_kernel, rows_here, map_width),
        [part] * halves,
        4,
        flops=2 * queries * positions * channels,
        bytes_accessed=2 * positions * channels,
        transcendentals=0,
    )(query_frame[None], query_row[None], query_col[None], maps)

    place = jnp.arange(positions, dtype=jnp.int32)[:, None]
    lane = jnp.arange(LANES, dtype=jnp.int32)[None, :]
    coords = jnp.where(
        lane == 0,
        place % map_width,
        jnp.where(lane == 1, place // map_width, jnp.where(lane == 2, 1, 0)),
    ).astype(BF16)

    if halves == 2:
        mine = picked[0] + swap(picked[1], "tm", 1)
        mine = all_sum(mine, "space")
        feats = [mine, swap(mine, "tm", 1)]
    else:
        feats = [all_sum(all_sum(picked[0], "tm"), "space")]

    feat_rows = -(-group // 8) * 8
    blocks = call(
        functools.partial(volume_kernel, n_groups, rows_here, height, map_width),
        jax.ShapeDtypeStruct((n_groups, feat_rows + AUX_ROWS, LANES), F32),
        halves + 3,
        flops=6 * queries * positions * channels,
        bytes_accessed=4 * positions * channels,
        transcendentals=queries * positions,
    )(*feats, maps, coords, ema_decay)

    blocks = lax.all_to_all(blocks, ("tm", "space"), 0, 0, tiled=True)

    n_out = out_weight.shape[0]
    out_rows = -(-n_tm * n_out // 8) * 8
    lines = call(
        functools.partial(tail_kernel, n_tm, n_space, group),
        jax.ShapeDtypeStruct((out_rows, LANES), F32),
        4,
        flops=2 * n_tm * group * channels * channels,
        bytes_accessed=4 * n_groups * (feat_rows + AUX_ROWS) * LANES,
        transcendentals=n_tm * group * channels,
    )(dw_kernel, pw_weight, out_weight, blocks)

    lines = lax.all_gather(lines, ("tm", "space"), axis=0)
    own = lax.dynamic_slice_in_dim(lines, lax.axis_index("tm") * n_out, n_out, axis=1)
    own = own[:, :, :group]
    return jnp.transpose(own, (1, 0, 2)).reshape(1, n_out, queries)


def solution(mesh):
    placed = (
        P(("video", "tm"), "space", None, None),
        P("video"),
        P("video"),
        P("video"),
        P(("video", "tm"), None),
        P(),
        P(),
        P(),
    )
    return jax.shard_map(
        local, mesh=mesh, in_specs=placed, out_specs=P(("video", "tm"), None, None), check_vma=False
    )
```

time: 129 us -> 70.4 us (0.55)
  blocking collectives: 60.2 us -> 23.7 us
  waiting for transfers between devices: 0.98 us -> 15.7 us
  local copies, waits for them, and re-layouts: 18.9 us -> 4.29 us
  between operations: 13.6 us -> 0.11 us
  other arithmetic: 18.2 us -> 4.81 us
  matrix products: 11.9 us -> 0 us
  Pallas kernels: 0 us -> 9.28 us
  starting transfers between devices: 4.34 us -> 12.2 us
    psum x2 -> x0, blocking collectives: 47.4 us -> none  [the longest x1 37.3 us: local(): query_feats = lax.psum(contrib, ('tm', 'space')).astype(jnp.bfloat16)]
    all_gather x2 -> x1, blocking collectives: 3.95 us -> 23.7 us  [local(): lines = lax.all_gather(lines, ('tm', 'space'), axis=0)]
    exp x1 -> x0, local copies, waits for them, and re-layouts: 15.7 us -> none  [local(): weights_exp = jnp.exp(scores - highest[:, None])]
    reduce_sum x4 -> x0, other arithmetic: 15 us -> none  [the longest x2 7.96 us: local(): col_part = jnp.sum(jnp.sum(grid, axis=1) * col_coord[None, :], axis=1)]
    dot_general x4 -> x0, matrix products: 11.9 us -> none  [the longest x1 8.38 us: local(): jnp.dot(weights_exp.astype(jnp.bfloat16), frame_map, preferred_element_ty...]
    all_to_all x0 -> x1, waiting for transfers between devices: none -> 10 us  [local(): blocks = lax.all_to_all(blocks, ('tm', 'space'), 0, 0, tiled=True)]
    pallas_call x0 -> x3, Pallas kernels: none -> 9.28 us  [the longest x1 6.39 us: local(): call(functools.partial(volume_kernel, n_groups, rows_here, height, map_wi...]
    pmax x1 -> x0, blocking collectives: 8.79 us -> none  [local(): top_value = lax.pmax(highest, 'space')]
  transfers between devices with their start and end apart: 3 -> 5, of which waited for: 1 -> 4; matrix products, arithmetic and copies ran while one was open for 19% -> 7% of each run, Pallas kernels for 0% -> 0%
where the time goes in v1:
time: 70.4 us; the launch traced here: 70.1 us
  blocking collectives  23.7 us (34%)
  waiting for transfers between devices  15.7 us (22%)
  starting transfers between devices  12.2 us (17%)
  Pallas kernels  9.28 us (13%)
  other arithmetic  4.81 us (7%)
  local copies, waits for them, and re-layouts  4.29 us (6%)
    all_gather x1, blocking collectives, local(): lines = lax.all_gather(lines, ('tm', 'space'), axis=0)  23.7 us
    all_to_all x1, waiting for transfers between devices, local(): blocks = lax.all_to_all(blocks, ('tm', 'space'), 0, 0, tiled=True)  10 us
    ppermute x4, starting transfers between devices, swap(): lax.ppermute(value, axis, [(i, i ^ bit) for i in range(lax.axis_size(axis...  6.51 us
    pallas_call x1, Pallas kernels, local(): call(functools.partial(volume_kernel, n_groups, rows_here, height, map_wi...  6.39 us
    all_to_all x1, starting transfers between devices, local(): blocks = lax.all_to_all(blocks, ('tm', 'space'), 0, 0, tiled=True)  5.73 us
    ppermute x4, waiting for transfers between devices, swap(): lax.ppermute(value, axis, [(i, i ^ bit) for i in range(lax.axis_size(axis...  5.67 us
    convert_element_type x1, other arithmetic, local(): coords = jnp.where(lane == 0, place % map_width, jnp.where(lane == 1, pla...  4.72 us
    unnamed x16, local copies, waits for them, and re-layouts  3.61 us
  transfers between devices with their start and end apart: 5, of which 4 were waited for; matrix products, arithmetic and copies ran while one was open for 7% of the time, Pallas kernels for 0%

profile of v1, /device:TPU:0, one launch (start us, length us, event | category | flops | bytes accessed | tf_op | source)
XLA Modules:
  0.0 70.1 jit_solution(6087285195240147887)
XLA Ops:
  0.0 0.0 copy-start.3
  0.0 1.5 %copy-done.3 = bf16[1,32,240,128]{3,2,1,0:T(8,128)(2,1)S(1)} copy-done((bf16[1,32,240,128]{3,2,1,0:T(8,128)(2,1)S(1)}, bf16[1,32,240,128]{3,2,1,0:T(8,128)(2,1)}, u32[]{:S(2)}) %copy-start.3) | copy-done | bytes 1966104
  1.5 0.0 copy-start.4
  1.5 0.7 copy-done.4
  2.2 0.0 copy-start.5
  2.2 0.7 copy-done.5
  2.9 0.0 copy-start.6
  2.9 0.7 copy-done.6
  3.6 2.2 %shard_map.82 = (bf16[256,128]{1,0:T(8,128)(2,1)S(1)}, bf16[256,128]{1,0:T(8,128)(2,1)S(1)}) custom-call(s32[1,512]{1,0:T(1,128)S(1)} %bitcast.9, s32[1,512]{1,0:T(1,128)S(1)} %bitcast.10, s32[1,512]{1,0:T(1,128)S(1)} %bitcast.11, bf16[7680,128]{1,0:T(8,128)(2,1)S(1)} %bitcast.7), custom_call_target="tpu_custom_call" | custom-call | flops 1006632960 | bytes 1966080 | tf_op jit(solution)/shard_map/pallas_call | solution.py:220
  5.8 0.0 copy-start.7
  5.9 0.5 collective-permute-start
  6.4 0.9 %collective-permute-done = bf16[256,128]{1,0:T(8,128)(2,1)S(1)} collective-permute-done((bf16[256,128]{1,0:T(8,128)(2,1)S(1)}, bf16[256,128]{1,0:T(8,128)(2,1)S(1)}, u32[]{:S(2)}, u32[]{:S(2)}) %collective-permute-start) | collective-permute-done | bytes 65568 | tf_op jit(solution)/shard_map/ppermute | solution.py:191
  7.3 3.0 %collective-permute-start.1 = (bf16[256,128]{1,0:T(8,128)(2,1)S(1)}, bf16[256,128]{1,0:T(8,128)(2,1)S(1)}, u32[]{:S(2)}, u32[]{:S(2)}) collective-permute-start(bf16[256,128]{1,0:T(8,128)(2,1)S(1)} %add.29), channel_id=1, source_target_pairs={{0,1},{1,0},{2,3},{3,2},{4,5},{5,4},{6,7},{7,6},{8,9},{9,8},{10,11... | collective-permute-start | bytes 196616 | tf_op jit(solution)/shard_map/ppermute | solution.py:191
  10.3 2.4 %collective-permute-done.1 = bf16[256,128]{1,0:T(8,128)(2,1)S(1)} collective-permute-done((bf16[256,128]{1,0:T(8,128)(2,1)S(1)}, bf16[256,128]{1,0:T(8,128)(2,1)S(1)}, u32[]{:S(2)}, u32[]{:S(2)}) %collective-permute-start.1) | collective-permute-done | bytes 65568 | tf_op jit(solution)/shard_map/ppermute | solution.py:191
  12.7 2.9 %collective-permute-start.2 = (bf16[256,128]{1,0:T(8,128)(2,1)S(1)}, bf16[256,128]{1,0:T(8,128)(2,1)S(1)}, u32[]{:S(2)}, u32[]{:S(2)}) collective-permute-start(bf16[256,128]{1,0:T(8,128)(2,1)S(1)} %add.30), channel_id=1, source_target_pairs={{0,2},{1,3},{2,0},{3,1},{4,6},{5,7},{6,4},{7,5},{8,10},{9,11},{10,... | collective-permute-start | bytes 196616 | tf_op jit(solution)/shard_map/ppermute | solution.py:191
  15.7 2.4 %collective-permute-done.2 = bf16[256,128]{1,0:T(8,128)(2,1)S(1)} collective-permute-done((bf16[256,128]{1,0:T(8,128)(2,1)S(1)}, bf16[256,128]{1,0:T(8,128)(2,1)S(1)}, u32[]{:S(2)}, u32[]{:S(2)}) %collective-permute-start.2) | collective-permute-done | bytes 65568 | tf_op jit(solution)/shard_map/ppermute | solution.py:191
  18.1 0.1 collective-permute-start.3
  18.1 4.7 %select_convert_fusion.refs_3_ = bf16[7680,128]{1,0:T(8,128)(2,1)S(1)} fusion(s32[128]{0:T(128)S(1)} %compare_select_fusion, s32[7680]{0:T(1024)S(1)} %get-tuple-element.9, s32[7680]{0:T(1024)S(1)} %get-tuple-element.10, pred[128]{0:T(512)(128)(4,1)S(1)} %get-tuple-element.11, pred[128]{0:T(512)(128)(4,1)S(1)} %get-tuple-element.12), kind=kLoop, calls=%fused_computation | loop fusion | flops 2949120 | bytes 2028288 | tf_op jit(solution)/shard_map/convert_element_type | solution.py:235
  22.9 0.0 copy-start
  22.9 0.0 copy-start.1
  22.9 0.0 copy-start.2
  22.9 0.0 collective-permute-done.3.refs_1_
  22.9 0.0 copy-done.7
  22.9 6.4 %shard_map.83 = f32[8,72,128]{2,1,0:T(8,128)} custom-call(bf16[256,128]{1,0:T(8,128)(2,1)S(1)} %add.31.refs_0_, bf16[256,128]{1,0:T(8,128)(2,1)S(1)} %collective-permute-done.3.refs_1_, bf16[7680,128]{1,0:T(8,128)(2,1)S(1)} %bitcast.8, bf16[7680,128]{1,0:T(8,128)(2,1)S(1)} %select_convert_fusion.refs_3_, f32[1,128]{1,0:T(1,128)S(1)} %copy-done.7), custom_call_target="tpu_custom_call" | custom-call | flops 3019898880 | bytes 3932160 | tf_op jit(solution)/shard_map/pallas_call | solution.py:245
  29.3 5.7 %all-to-all-start = ((f32[8,72,128]{2,1,0:T(8,128)}), f32[8,72,128]{2,1,0:T(8,128)S(1)}, u32[]{:S(2)}, u32[]{:S(2)}) async-start(f32[8,72,128]{2,1,0:T(8,128)} %shard_map.83), calls=%async_computation | async-start | bytes 589824 | tf_op jit(solution)/shard_map/all_to_all | solution.py:254
  35.1 10.0 %all-to-all-done.in_ref = f32[8,72,128]{2,1,0:T(8,128)S(1)} async-done(((f32[8,72,128]{2,1,0:T(8,128)}), f32[8,72,128]{2,1,0:T(8,128)S(1)}, u32[]{:S(2)}, u32[]{:S(2)}) %all-to-all-start) | async-done | bytes 294944 | tf_op jit(solution)/shard_map/all_to_all | solution.py:254
  45.1 0.0 copy-done
  45.1 0.0 copy-done.1
  45.1 0.0 copy-done.2
  45.1 0.6 shard_map.84
  45.8 23.7 %all-gather = f32[64,128]{1,0:T(8,128)S(1)} all-gather(f32[8,128]{1,0:T(8,128)S(1)} %shard_map.84), channel_id=2, replica_groups=mesh['video'=4,'tm'=2,'space'=4] {'tm','space'}, dimensions={0}, use_global_device_ids=true | all-gather | bytes 36864 | tf_op jit(solution)/shard_map/all_gather | solution.py:267
  69.4 0.7 reshape.59
  (8 shorter events, 0.1 us)
Async XLA Ops:
  0.0 1.5 %copy-start.3 = (bf16[1,32,240,128]{3,2,1,0:T(8,128)(2,1)S(1)}, bf16[1,32,240,128]{3,2,1,0:T(8,128)(2,1)}, u32[]{:S(2)}) copy-start(bf16[1,32,240,128]{3,2,1,0:T(8,128)(2,1)} %param.8) | copy-start | bytes 5898244
  1.5 0.7 copy-start.4
  2.2 0.7 copy-start.5
  2.9 0.7 copy-start.6
  5.8 17.1 %copy-start.7 = (f32[1,128]{1,0:T(1,128)S(1)}, f32[1,128]{1,0:T(1,128)}, u32[]{:S(2)}) copy-start(f32[1,128]{1,0:T(1,128)} %refs_4_.1) | copy-start | bytes 1540
  5.9 1.4 %collective-permute-start = (bf16[256,128]{1,0:T(8,128)(2,1)S(1)}, bf16[256,128]{1,0:T(8,128)(2,1)S(1)}, u32[]{:S(2)}, u32[]{:S(2)}) collective-permute-start(bf16[256,128]{1,0:T(8,128)(2,1)S(1)} %get-tuple-element.8), channel_id=1, source_target_pairs={{0,4},{4,0},{1,5},{5,1},{2,6},{6,2},{3,7},{7,3},{8,12},{12,8},{9,1... | collective-permute-start | bytes 196616 | tf_op jit(solution)/shard_map/ppermute | solution.py:191
  7.3 5.4 %collective-permute-start.1 = (bf16[256,128]{1,0:T(8,128)(2,1)S(1)}, bf16[256,128]{1,0:T(8,128)(2,1)S(1)}, u32[]{:S(2)}, u32[]{:S(2)}) collective-permute-start(bf16[256,128]{1,0:T(8,128)(2,1)S(1)} %add.29), channel_id=1, source_target_pairs={{0,1},{1,0},{2,3},{3,2},{4,5},{5,4},{6,7},{7,6},{8,9},{9,8},{10,11... | collective-permute-start | bytes 196616 | tf_op jit(solution)/shard_map/ppermute | solution.py:191
  12.7 5.3 %collective-permute-start.2 = (bf16[256,128]{1,0:T(8,128)(2,1)S(1)}, bf16[256,128]{1,0:T(8,128)(2,1)S(1)}, u32[]{:S(2)}, u32[]{:S(2)}) collective-permute-start(bf16[256,128]{1,0:T(8,128)(2,1)S(1)} %add.30), channel_id=1, source_target_pairs={{0,2},{1,3},{2,0},{3,1},{4,6},{5,7},{6,4},{7,5},{8,10},{9,11},{10,... | collective-permute-start | bytes 196616 | tf_op jit(solution)/shard_map/ppermute | solution.py:191
  18.1 4.8 %collective-permute-start.3 = (bf16[256,128]{1,0:T(8,128)(2,1)S(1)}, bf16[256,128]{1,0:T(8,128)(2,1)S(1)}, u32[]{:S(2)}, u32[]{:S(2)}) collective-permute-start(bf16[256,128]{1,0:T(8,128)(2,1)S(1)} %add.31.refs_0_), channel_id=1, source_target_pairs={{0,4},{4,0},{1,5},{5,1},{2,6},{6,2},{3,7},{7,3},{8,12},{12,8},{9,1... | collective-permute-start | bytes 196616 | tf_op jit(solution)/shard_map/ppermute | solution.py:191
  22.9 22.2 %copy-start = (bf16[128,128]{1,0:T(8,128)(2,1)S(1)}, bf16[128,128]{1,0:T(8,128)(2,1)}, u32[]{:S(2)}) copy-start(bf16[128,128]{1,0:T(8,128)(2,1)} %pw_ref.1) | copy-start | bytes 98308
  22.9 22.2 %copy-start.1 = (f32[3,128]{1,0:T(4,128)S(1)}, f32[3,128]{1,0:T(4,128)}, u32[]{:S(2)}) copy-start(f32[3,128]{1,0:T(4,128)} %dw_ref.1) | copy-start | bytes 4612
  22.9 22.2 %copy-start.2 = (f32[2,128]{1,0:T(2,128)S(1)}, f32[2,128]{1,0:T(2,128)}, u32[]{:S(2)}) copy-start(f32[2,128]{1,0:T(2,128)} %ow_ref.1) | copy-start | bytes 3076
  29.3 15.8 %all-to-all-start = ((f32[8,72,128]{2,1,0:T(8,128)}), f32[8,72,128]{2,1,0:T(8,128)S(1)}, u32[]{:S(2)}, u32[]{:S(2)}) async-start(f32[8,72,128]{2,1,0:T(8,128)} %shard_map.83), calls=%async_computation | async-start | bytes 589824 | tf_op jit(solution)/shard_map/all_to_all | solution.py:254

commit v2 on v1

--- a/solution.py
+++ b/solution.py
@@ -187,6 +187,234 @@
     )
 
 
+def hot_rows(target, map_ref, base, chunk):
+    rows = target.shape[0]
+    lane = lax.broadcasted_iota(jnp.int32, (rows, LANES), 1)
+    parts = []
+    for lane_base in range(base, base + chunk, LANES):
+        parts.append(jnp.where(lane + lane_base == target, 1.0, 0.0).astype(BF16))
+    hot = jnp.concatenate(parts, axis=1)
+    return jnp.dot(hot, map_ref[base : base + chunk, :], preferred_element_type=F32)
+
+
+def store_by_partner(picked, scratch_ref, out_ref):
+    n_space = lax.axis_size("space")
+    space = lax.axis_index("space")
+    group = picked.shape[0] // n_space
+    scratch_ref[...] = picked
+    for k in range(n_space):
+        start = pl.multiple_of((space ^ k) * group, group)
+        out_ref[k * group : (k + 1) * group, :] = scratch_ref[pl.ds(start, group), :].astype(BF16)
+
+
+def pick_send_kernel(
+    rows_here,
+    map_width,
+    frame_hbm,
+    row_hbm,
+    col_hbm,
+    map_hbm,
+    send_ref,
+    target_ref,
+    map_ref,
+    index_ref,
+    scratch_ref,
+    index_sem,
+    map_sem,
+):
+    index_copies = []
+    for i, ref in enumerate((frame_hbm, row_hbm, col_hbm)):
+        copy = pltpu.make_async_copy(ref, index_ref.at[i], index_sem.at[i])
+        copy.start()
+        index_copies.append(copy)
+    positions = map_ref.shape[0]
+    chunk = pick_chunk(positions, 1536)
+    map_copies = []
+    for i in range(positions // chunk):
+        window = pl.ds(i * chunk, chunk)
+        copy = pltpu.make_async_copy(map_hbm.at[window], map_ref.at[window], map_sem.at[i])
+        copy.start()
+        map_copies.append(copy)
+    for copy in index_copies:
+        copy.wait()
+    tm = lax.axis_index("tm")
+    row = index_ref[1] - lax.axis_index("space") * rows_here
+    here = (index_ref[0] == tm) & (row >= 0) & (row < rows_here)
+    target = jnp.where(here, row * map_width + index_ref[2], -1)
+    half = target.shape[1] // 2
+    first, second = target[:, :half], target[:, half:]
+    target_ref[...] = jnp.where(tm == 0, first, second)
+    target = jnp.where(tm == 0, second, first)
+    target = jnp.transpose(jnp.broadcast_to(target, (LANES, half)))
+    picked = None
+    for i, copy in enumerate(map_copies):
+        copy.wait()
+        term = hot_rows(target, map_ref, i * chunk, chunk)
+        picked = term if picked is None else picked + term
+    store_by_partner(picked, scratch_ref, send_ref)
+
+
+def pick_keep_kernel(target_ref, map_ref, keep_ref, scratch_ref):
+    half = target_ref.shape[1]
+    positions = map_ref.shape[0]
+    chunk = pick_chunk(positions, 1536)
+    target = jnp.transpose(jnp.broadcast_to(target_ref[...], (LANES, half)))
+    picked = None
+    for base in range(0, positions, chunk):
+        term = hot_rows(target, map_ref, base, chunk)
+        picked = term if picked is None else picked + term
+    store_by_partner(picked, scratch_ref, keep_ref)
+
+
+def coord_kernel(map_width, after_ref, out_ref):
+    positions = out_ref.shape[0]
+    chunk = pick_chunk(positions, 512)
+    lane = lax.broadcasted_iota(jnp.int32, (chunk, LANES), 1)
+    local_place = lax.broadcasted_iota(jnp.int32, (chunk, LANES), 0).astype(F32)
+
+    @pl.loop(0, positions // chunk)
+    def _(step):
+        place = local_place + (step * chunk).astype(F32)
+        row = jnp.floor((place + 0.5) * (1.0 / map_width))
+        rest = jnp.where(lane == 2, 1.0, 0.0)
+        value = jnp.where(lane == 0, place - row * map_width, jnp.where(lane == 1, row, rest))
+        out_ref[pl.ds(pl.multiple_of(step * chunk, chunk), chunk), :] = value.astype(BF16)
+
+
+def half_kernel(n_space, rows_here, height, width, *refs):
+    query_refs, (map_ref, coord_ref, decay_ref) = refs[:n_space], refs[n_space : n_space + 3]
+    out_refs = refs[n_space + 3 :]
+    positions, channels = map_ref.shape
+    factor = math.log2(math.e) / math.sqrt(channels)
+    group = query_refs[0].shape[0]
+    query = jnp.concatenate([ref[...] for ref in query_refs], axis=0)
+    first_row = (lax.axis_index("space") * rows_here).astype(F32)
+    chunk = pick_chunk(positions, 1280)
+
+    def score(base):
+        keys = map_ref[base : base + chunk, :]
+        return lax.dot_general(query, keys, NT, preferred_element_type=F32)
+
+    top = sums = None
+    ahead = score(0)
+    for base in range(0, positions, chunk):
+        scores = ahead
+        if base + chunk < positions:
+            ahead = score(base + chunk)
+        window = slice(base, base + chunk)
+        values = jnp.concatenate([map_ref[window, :], coord_ref[window, :]], axis=1)
+        new_top = jnp.max(scores, axis=1, keepdims=True) * factor
+        if top is not None:
+            new_top = jnp.maximum(new_top, top)
+        weights = jnp.exp2(scores * factor - new_top).astype(BF16)
+        terms = jnp.dot(weights, values, preferred_element_type=F32)
+        sums = terms if sums is None else terms + jnp.exp2(top - new_top) * sums
+        top = new_top
+    feats = sums[:, :channels] / sums[:, channels + 2 : channels + 3]
+    extra = sums[:, channels:]
+    lane = lax.broadcasted_iota(jnp.int32, extra.shape, 1)
+    extra = jnp.transpose(jnp.where(lane == 3, top, extra))
+    total = extra[2:3]
+    across = extra[0:1] / total / width
+    down = (extra[1:2] / total + first_row) / height
+    aux = jnp.zeros((AUX_ROWS, extra.shape[1]), F32)
+    sub = lax.broadcasted_iota(jnp.int32, aux.shape, 0)
+    for index, values in enumerate([extra[3:4], total, across, down]):
+        aux = jnp.where(sub == index, values, aux)
+    sub = lax.broadcasted_iota(jnp.int32, (AUX_ROWS, LANES), 0)
+    for index, out_ref in enumerate(out_refs):
+        shift = (aux.shape[1] - index * group) % aux.shape[1]
+        block = pltpu.roll(aux, shift, 1) if shift else aux
+        out_ref[:group, :] = feats[index * group : (index + 1) * group]
+        out_ref[group:, :] = jnp.where(sub == 4, decay_ref[...], block[:, :LANES])
+
+
+def merge(blocks, group):
+    aux = [block[group:] for block in blocks]
+    top = aux[0][0:1]
+    for block in aux[1:]:
+        top = jnp.maximum(top, block[0:1])
+    weight = [jnp.exp2(b[0:1] - top) * b[1:2] for b in aux]
+    total = sum(weight[1:], weight[0])
+    share = [w / total for w in weight]
+    across = [s * b[2:3] for s, b in zip(share, aux)]
+    down = [s * b[3:4] for s, b in zip(share, aux)]
+    across, down = sum(across[1:], across[0]), sum(down[1:], down[0])
+    table = jnp.zeros((8, LANES), F32)
+    sub = lax.broadcasted_iota(jnp.int32, table.shape, 0)
+    for index, value in enumerate(share):
+        table = jnp.where(sub == index, value, table)
+    table = jnp.transpose(table)
+    attended = None
+    for index, block in enumerate(blocks):
+        term = table[:group, index : index + 1] * block[:group]
+        attended = term if attended is None else attended + term
+    return across, down, attended.astype(BF16).astype(F32), aux[0][4:5]
+
+
+def pair_tail_kernel(n_space, group, *refs):
+    dw_ref, pw_ref, ow_ref = refs[:3]
+    same = merge([ref[...].astype(F32) for ref in refs[3 : 3 + n_space]], group)
+    other = merge([ref[...].astype(F32) for ref in refs[3 + n_space : 3 + 2 * n_space]], group)
+    same_ref, other_ref = refs[3 + 2 * n_space :]
+    early = lax.axis_index("tm") == 0
+    frames = [
+        [jnp.where(early, a, b) for a, b in zip(same, other)],
+        [jnp.where(early, b, a) for a, b in zip(same, other)],
+    ]
+    taps = dw_ref.shape[0]
+    hidden = []
+    for frame in range(2):
+        depth = None
+        for tap in range(taps):
+            source = frame + tap - taps // 2
+            if 0 <= source < 2:
+                term = dw_ref[tap : tap + 1, :] * frames[source][2]
+                depth = term if depth is None else depth + term
+        hidden.append(jax.nn.gelu(depth).astype(BF16))
+    hidden = jnp.concatenate(hidden, axis=0)
+    mixed = jnp.dot(hidden, pw_ref[...], preferred_element_type=F32)
+    memory = None
+    lines = []
+    for frame, (across, down, attended, decay) in enumerate(frames):
+        refined = attended + mixed[frame * group : (frame + 1) * group]
+        fresh = (1.0 - decay) * refined
+        memory = fresh if memory is None else decay * memory + fresh
+        padded = memory
+        if group < LANES:
+            padded = jnp.concatenate([memory, jnp.zeros((LANES - group, LANES), F32)], axis=0)
+        delta = lax.dot_general(
+            ow_ref[...], padded, NT, preferred_element_type=F32, precision=lax.Precision.HIGHEST
+        )
+        sub = lax.broadcasted_iota(jnp.int32, delta.shape, 0)
+        lines.append(delta + jnp.where(sub == 0, across, down))
+    same_ref[...] = jnp.where(early, lines[0], lines[1])
+    other_ref[...] = jnp.where(early, lines[1], lines[0])
+
+
+def lay_kernel(n_space, group, *refs):
+    same = [ref[...] for ref in refs[:n_space]]
+    other = [ref[...] for ref in refs[n_space : 2 * n_space]]
+    out_ref = refs[2 * n_space]
+    early = lax.axis_index("tm") == 0
+    space = lax.axis_index("space")
+    lines = [jnp.where(early, a, b) for a, b in zip(same, other)]
+    lines += [jnp.where(early, b, a) for a, b in zip(same, other)]
+    bit = 1
+    while bit < n_space:
+        turn = (space & bit) != 0
+        lines = [jnp.where(turn, lines[i ^ bit], lines[i]) for i in range(2 * n_space)]
+        bit *= 2
+    per_tile = LANES // group
+    lane = lax.broadcasted_iota(jnp.int32, lines[0].shape, 1)
+    for tile in range(2 * n_space // per_tile):
+        value = lines[tile * per_tile]
+        for index in range(1, per_tile):
+            moved = pltpu.roll(lines[tile * per_tile + index], index * group, 1)
+            value = jnp.where(lane >= index * group, moved, value)
+        out_ref[0, :, tile * LANES : (tile + 1) * LANES] = value
+
+
 def swap(value, axis, bit):
     return lax.ppermute(value, axis, [(i, i ^ bit) for i in range(lax.axis_size(axis))])
 
@@ -202,7 +430,7 @@
     return value
 
 
-def local(
+def local_general(
     feature_maps, query_frame, query_row, query_col, ema_decay, dw_kernel, pw_weight, out_weight
 ):
     frames_here, rows_here, map_width, channels = feature_maps.shape
@@ -268,6 +496,135 @@
     own = lax.dynamic_slice_in_dim(lines, lax.axis_index("tm") * n_out, n_out, axis=1)
     own = own[:, :, :group]
     return jnp.transpose(own, (1, 0, 2)).reshape(1, n_out, queries)
+
+
+def partner(value, flip, bits):
+    n_space = lax.axis_size("space")
+    pairs = []
+    for tm in range(2):
+        for space in range(n_space):
+            pairs.append((tm * n_space + space, (tm ^ flip) * n_space + (space ^ bits)))
+    return lax.ppermute(value, ("tm", "space"), pairs)
+
+
+def local_pair(
+    feature_maps, query_frame, query_row, query_col, ema_decay, dw_kernel, pw_weight, out_weight
+):
+    _, rows_here, map_width, channels = feature_maps.shape
+    queries = query_frame.shape[0]
+    n_space = lax.axis_size("space")
+    half = queries // 2
+    group = half // n_space
+    height = rows_here * n_space
+    positions = rows_here * map_width
+    maps = feature_maps.reshape(positions, channels)
+    vmem = pl.BlockSpec(memory_space=pltpu.VMEM)
+    hbm = pl.BlockSpec(memory_space=pltpu.HBM)
+    params = pltpu.CompilerParams(vmem_limit_bytes=VMEM_LIMIT)
+    n_chunks = positions // pick_chunk(positions, 1536)
+
+    half_shape = jax.ShapeDtypeStruct((half, channels), BF16)
+    send, target, maps_near = pl.pallas_call(
+        functools.partial(pick_send_kernel, rows_here, map_width),
+        out_shape=[
+            half_shape,
+            jax.ShapeDtypeStruct((1, half), jnp.int32),
+            jax.ShapeDtypeStruct(maps.shape, BF16),
+        ],
+        in_specs=[hbm] * 4,
+        out_specs=[vmem] * 3,
+        scratch_shapes=[
+            pltpu.VMEM((3, 1, queries), jnp.int32),
+            pltpu.VMEM((half, channels), F32),
+            pltpu.SemaphoreType.DMA((3,)),
+            pltpu.SemaphoreType.DMA((n_chunks,)),
+        ],
+        compiler_params=params,
+        cost_estimate=pl.CostEstimate(
+            flops=queries * positions * channels,
+            bytes_accessed=4 * positions * channels,
+            transcendentals=0,
+        ),
+    )(query_frame[None], query_row[None], query_col[None], maps)
+    arrived = partner(send, 1, 0)
+    keep = pl.pallas_call(
+        pick_keep_kernel,
+        out_shape=half_shape,
+        in_specs=[vmem] * 2,
+        out_specs=vmem,
+        scratch_shapes=[pltpu.VMEM((half, channels), F32)],
+        compiler_params=params,
+        cost_estimate=pl.CostEstimate(
+            flops=queries * positions * channels,
+            bytes_accessed=2 * positions * channels,
+            transcendentals=0,
+        ),
+    )(target, maps_near)
+    coords = call(
+        functools.partial(coord_kernel, map_width),
+        jax.ShapeDtypeStruct((positions, LANES), BF16),
+        1,
+        flops=8 * positions * LANES,
+        bytes_accessed=2 * positions * LANES,
+        transcendentals=0,
+    )(target)
+
+    def piece(k):
+        window = slice(k * group, (k + 1) * group)
+        return keep[window] + arrived[window]
+
+    own = piece(0)
+    shares = [partner(piece(k), 0, k) for k in range(1, n_space)]
+    for share in shares:
+        own = own + share
+    mine = [own] + [partner(own, 0, k) for k in range(1, n_space)]
+    theirs = [partner(value, 1, 0) for value in mine]
+
+    def blocks_of(feats):
+        shape = jax.ShapeDtypeStruct((group + AUX_ROWS, LANES), F32)
+        return call(
+            functools.partial(half_kernel, n_space, rows_here, height, map_width),
+            [shape] * n_space,
+            n_space + 3,
+            flops=3 * queries * positions * channels,
+            bytes_accessed=4 * positions * channels,
+            transcendentals=half * positions,
+        )(*feats, maps_near, coords, ema_decay)
+
+    near = blocks_of(mine)
+    near = [near[0]] + [partner(near[k], 0, k) for k in range(1, n_space)]
+    far = blocks_of(theirs)
+    far = [partner(far[k], 1, k) for k in range(n_space)]
+
+    n_out = out_weight.shape[0]
+    line = jax.ShapeDtypeStruct((n_out, LANES), F32)
+    same, other = call(
+        functools.partial(pair_tail_kernel, n_space, group),
+        [line, line],
+        3 + 2 * n_space,
+        flops=8 * group * channels * channels,
+        bytes_accessed=8 * n_space * (group + AUX_ROWS) * LANES,
+        transcendentals=2 * group * channels,
+    )(dw_kernel, pw_weight, out_weight, *near, *far)
+    lines = [same] + [partner(same, 0, k) for k in range(1, n_space)]
+    lines += [partner(other, 1, k) for k in range(n_space)]
+    return call(
+        functools.partial(lay_kernel, n_space, group),
+        jax.ShapeDtypeStruct((1, n_out, queries), F32),
+        2 * n_space,
+        flops=n_out * queries,
+        bytes_accessed=8 * n_out * queries,
+        transcendentals=0,
+    )(*lines)
+
+
+def local(feature_maps, query_frame, *rest):
+    n_tm, n_space = lax.axis_size("tm"), lax.axis_size("space")
+    group = query_frame.shape[0] // (n_tm * n_space)
+    paired = n_tm == 2 and n_space & (n_space - 1) == 0 and n_space <= 8
+    if paired and group % 16 == 0 and LANES % group == 0:
+        return local_pair(feature_maps, query_frame, *rest)
+    return local_general(feature_maps, query_frame, *rest)
 
 
 def solution(mesh):

time: 70.4 us -> 57.7 us (0.82)
  blocking collectives: 23.7 us -> 0 us
  starting transfers between devices: 12.2 us -> 28.7 us
  other arithmetic: 4.81 us -> 0.02 us
  Pallas kernels: 9.28 us -> 12.7 us
  waiting for transfers between devices: 15.7 us -> 12.3 us
    all_gather x1 -> x0, blocking collectives: 23.7 us -> none  [local(): lines = lax.all_gather(lines, ('tm', 'space'), axis=0)]
    ppermute x4 -> x25, starting transfers between devices: 6.51 us -> 28.7 us  [partner(): return lax.ppermute(value, ('tm', 'space'), pairs)]
    all_to_all x1 -> x0, waiting for transfers between devices: 10 us -> none  [local(): blocks = lax.all_to_all(blocks, ('tm', 'space'), 0, 0, tiled=True)]
    ppermute x4 -> x25, waiting for transfers between devices: 5.67 us -> 12.3 us  [partner(): return lax.ppermute(value, ('tm', 'space'), pairs)]
    all_to_all x1 -> x0, starting transfers between devices: 5.73 us -> none  [local(): blocks = lax.all_to_all(blocks, ('tm', 'space'), 0, 0, tiled=True)]
    convert_element_type x1 -> x0, other arithmetic: 4.72 us -> none  [local(): coords = jnp.where(lane == 0, place % map_width, jnp.where(lane == 1, pla...]
    pallas_call x3 -> x7, Pallas kernels: 9.28 us -> 12.7 us  [the longest x2 5.94 us: blocks_of(): call(functools.partial(half_kernel, n_space, rows_here, height, map_width...]
  transfers between devices with their start and end apart: 5 -> 25, of which waited for: 4 -> 5; matrix products, arithmetic and copies ran while one was open for 7% -> 0% of each run, Pallas kernels for 0% -> 15%
where the time goes in v2:
time: 57.7 us; the launch traced here: 57.5 us
  starting transfers between devices  28.7 us (50%)
  Pallas kernels  12.7 us (22%)
  waiting for transfers between devices  12.3 us (21%)
  local copies, waits for them, and re-layouts  3.6 us (6%)
    ppermute x25, starting transfers between devices, partner(): return lax.ppermute(value, ('tm', 'space'), pairs)  28.7 us
    ppermute x25, waiting for transfers between devices, partner(): return lax.ppermute(value, ('tm', 'space'), pairs)  12.3 us
    pallas_call x2, Pallas kernels, blocks_of(): call(functools.partial(half_kernel, n_space, rows_here, height, map_width...  5.94 us
    unnamed x16, local copies, waits for them, and re-layouts  3.6 us
    pallas_call x1, Pallas kernels, local_pair(): pl.pallas_call(functools.partial(pick_send_kernel, rows_here, map_width),...  3 us
    pallas_call x1, Pallas kernels, local_pair(): pl.pallas_call(pick_keep_kernel, out_shape=half_shape, in_specs=[vmem] *...  1.24 us
    pallas_call x1, Pallas kernels, local_pair(): call(functools.partial(coord_kernel, map_width), jax.ShapeDtypeStruct((po...  1.19 us
  transfers between devices with their start and end apart: 25, of which 5 were waited for; matrix products, arithmetic and copies ran while one was open for 0% of the time, Pallas kernels for 15%

profile of v2, /device:TPU:0, one launch (start us, length us, event | category | flops | bytes accessed | tf_op | source)
XLA Modules:
  0.0 57.5 jit_solution(1328311753551110366)
XLA Ops:
  0.0 1.5 %copy-done = bf16[1,32,240,128]{3,2,1,0:T(8,128)(2,1)S(1)} copy-done((bf16[1,32,240,128]{3,2,1,0:T(8,128)(2,1)S(1)}, bf16[1,32,240,128]{3,2,1,0:T(8,128)(2,1)}, u32[]{:S(2)}) %copy-start) | copy-done | bytes 1966104
  1.5 0.7 %copy-done.2 = s32[512]{0:T(512)S(1)} copy-done((s32[512]{0:T(512)S(1)}, s32[512]{0:T(512)}, u32[]{:S(2)}) %copy-start.2) | copy-done | bytes 2072
  2.2 0.7 %copy-done.3 = s32[512]{0:T(512)S(1)} copy-done((s32[512]{0:T(512)S(1)}, s32[512]{0:T(512)}, u32[]{:S(2)}) %copy-start.3) | copy-done | bytes 2072
  2.9 0.7 %copy-done.4 = s32[512]{0:T(512)S(1)} copy-done((s32[512]{0:T(512)S(1)}, s32[512]{0:T(512)}, u32[]{:S(2)}) %copy-start.4) | copy-done | bytes 2072
  3.6 3.0 %shard_map.82 = (bf16[256,128]{1,0:T(8,128)(2,1)S(1)}, s32[1,256]{1,0:T(1,128)S(1)}, bf16[7680,128]{1,0:T(8,128)(2,1)S(1)}) custom-call(s32[1,512]{1,0:T(1,128)S(1)} %bitcast.5, s32[1,512]{1,0:T(1,128)S(1)} %bitcast.6, s32[1,512]{1,0:T(1,128)S(1)} %bitcast.7, bf16[7680,128]{1,0:T(8,128)(2,1)S(1)} %bitcast.4), custom_call_target="tpu_custom_call" | custom-call | flops 503316480 | bytes 3932160 | tf_op jit(solution)/shard_map/pallas_call | solution.py:527
  6.6 0.5 collective-permute-start
  7.1 1.2 %shard_map.83 = bf16[256,128]{1,0:T(8,128)(2,1)S(1)} custom-call(s32[1,256]{1,0:T(1,128)S(1)} %get-tuple-element.18.target_ref.after_ref, bf16[7680,128]{1,0:T(8,128)(2,1)S(1)} %get-tuple-element.19.map_ref.refs_4_), custom_call_target="tpu_custom_call" | custom-call | flops 503316480 | bytes 1966080 | tf_op jit(solution)/shard_map/pallas_call | solution.py:550
  8.4 0.0 collective-permute-done
  8.4 2.7 %collective-permute-start.1 = (bf16[64,128]{1,0:T(8,128)(2,1)S(1)}, bf16[64,128]{1,0:T(8,128)(2,1)S(1)}, u32[]{:S(2)}, u32[]{:S(2)}) collective-permute-start(bf16[64,128]{1,0:T(8,128)(2,1)S(1)} %get-tuple-element.31), channel_id=1, source_target_pairs={{0,1},{1,0},{2,3},{3,2},{4,5},{5,4},{6,7},{7,6},{8,9},{9,8},{10,11... | collective-permute-start | bytes 49160 | tf_op jit(solution)/shard_map/ppermute | solution.py:507
  11.1 2.6 %collective-permute-start.2 = (bf16[64,128]{1,0:T(8,128)(2,1)S(1)}, bf16[64,128]{1,0:T(8,128)(2,1)S(1)}, u32[]{:S(2)}, u32[]{:S(2)}) collective-permute-start(bf16[64,128]{1,0:T(8,128)(2,1)S(1)} %get-tuple-element.33), channel_id=1, source_target_pairs={{0,2},{1,3},{2,0},{3,1},{4,6},{5,7},{6,4},{7,5},{8,10},{9,11},{10,... | collective-permute-start | bytes 49160 | tf_op jit(solution)/shard_map/ppermute | solution.py:507
  13.7 0.0 collective-permute-start.3
  13.7 0.0 collective-permute-done.1
  13.7 2.0 %collective-permute-done.2 = bf16[64,128]{1,0:T(8,128)(2,1)S(1)} collective-permute-done((bf16[64,128]{1,0:T(8,128)(2,1)S(1)}, bf16[64,128]{1,0:T(8,128)(2,1)S(1)}, u32[]{:S(2)}, u32[]{:S(2)}) %collective-permute-start.2) | collective-permute-done | bytes 16416 | tf_op jit(solution)/shard_map/ppermute | solution.py:507
  15.7 3.5 %collective-permute-done.3 = bf16[64,128]{1,0:T(8,128)(2,1)S(1)} collective-permute-done((bf16[64,128]{1,0:T(8,128)(2,1)S(1)}, bf16[64,128]{1,0:T(8,128)(2,1)S(1)}, u32[]{:S(2)}, u32[]{:S(2)}) %collective-permute-start.3) | collective-permute-done | bytes 16416 | tf_op jit(solution)/shard_map/ppermute | solution.py:507
  19.2 0.1 collective-permute-start.4
  19.3 0.7 %collective-permute-start.5 = (bf16[64,128]{1,0:T(8,128)(2,1)S(1)}, bf16[64,128]{1,0:T(8,128)(2,1)S(1)}, u32[]{:S(2)}, u32[]{:S(2)}) collective-permute-start(bf16[64,128]{1,0:T(8,128)(2,1)S(1)} %fusion.2.refs_0_), channel_id=1, source_target_pairs={{0,2},{1,3},{2,0},{3,1},{4,6},{5,7},{6,4},{7,5},{8,10},{9,11},{10,... | collective-permute-start | bytes 49160 | tf_op jit(solution)/shard_map/ppermute | solution.py:507
  20.0 3.6 %collective-permute-start.6 = (bf16[64,128]{1,0:T(8,128)(2,1)S(1)}, bf16[64,128]{1,0:T(8,128)(2,1)S(1)}, u32[]{:S(2)}, u32[]{:S(2)}) collective-permute-start(bf16[64,128]{1,0:T(8,128)(2,1)S(1)} %fusion.2.refs_0_), channel_id=1, source_target_pairs={{0,3},{1,2},{2,1},{3,0},{4,7},{5,6},{6,5},{7,4},{8,11},{9,10},{10,... | collective-permute-start | bytes 49160 | tf_op jit(solution)/shard_map/ppermute | solution.py:507
  23.7 1.2 %shard_map.84.refs_5_ = bf16[7680,128]{1,0:T(8,128)(2,1)S(1)} custom-call(s32[1,256]{1,0:T(1,128)S(1)} %get-tuple-element.18.target_ref.after_ref), custom_call_target="tpu_custom_call" | custom-call | flops 7864320 | bytes 1966080 | tf_op jit(solution)/shard_map/pallas_call | solution.py:563
  24.9 0.1 collective-permute-start.10
  24.9 0.0 collective-permute-done.4.refs_1_
  24.9 0.5 collective-permute-start.11
  25.4 0.0 collective-permute-done.5.refs_2_
  25.4 0.1 collective-permute-start.12
  25.5 0.0 collective-permute-done.6.refs_3_
  25.5 0.4 collective-permute-start.13
  26.0 0.0 copy-done.7
  26.0 3.0 %shard_map.85 = (f32[72,128]{1,0:T(8,128)S(1)}, f32[72,128]{1,0:T(8,128)S(1)}, f32[72,128]{1,0:T(8,128)S(1)}, f32[72,128]{1,0:T(8,128)S(1)}) custom-call(bf16[64,128]{1,0:T(8,128)(2,1)S(1)} %fusion.2.refs_0_, bf16[64,128]{1,0:T(8,128)(2,1)S(1)} %collective-permute-done.4.refs_1_, bf16[64,128]{1,0:T(8,128)(2,1)S(1)} %collective-permute-done.5.refs_2_, ...), custom_call_target="tpu_custom_call" | custom-call | flops 1509949440 | bytes 3932160 | tf_op jit(solution)/shard_map/pallas_call | solution.py:585
  28.9 0.6 collective-permute-start.7
  29.5 0.0 collective-permute-done.10.refs_0_
  29.5 3.3 %collective-permute-start.8 = (f32[72,128]{1,0:T(8,128)S(1)}, f32[72,128]{1,0:T(8,128)S(1)}, u32[]{:S(2)}, u32[]{:S(2)}) collective-permute-start(f32[72,128]{1,0:T(8,128)S(1)} %get-tuple-element.23), channel_id=1, source_target_pairs={{0,2},{1,3},{2,0},{3,1},{4,6},{5,7},{6,4},{7,5},{8,10},{9,11},{10,... | collective-permute-start | bytes 110600 | tf_op jit(solution)/shard_map/ppermute | solution.py:507
  32.8 0.0 collective-permute-done.11.refs_1_
  32.8 0.6 %collective-permute-start.9 = (f32[72,128]{1,0:T(8,128)S(1)}, f32[72,128]{1,0:T(8,128)S(1)}, u32[]{:S(2)}, u32[]{:S(2)}) collective-permute-start(f32[72,128]{1,0:T(8,128)S(1)} %get-tuple-element.24), channel_id=1, source_target_pairs={{0,3},{1,2},{2,1},{3,0},{4,7},{5,6},{6,5},{7,4},{8,11},{9,10},{10,... | collective-permute-start | bytes 110600 | tf_op jit(solution)/shard_map/ppermute | solution.py:507
  33.4 0.0 collective-permute-done.12.refs_2_
  33.4 0.0 collective-permute-done.13.refs_3_
  33.4 3.0 %shard_map.86 = (f32[72,128]{1,0:T(8,128)S(1)}, f32[72,128]{1,0:T(8,128)S(1)}, f32[72,128]{1,0:T(8,128)S(1)}, f32[72,128]{1,0:T(8,128)S(1)}) custom-call(bf16[64,128]{1,0:T(8,128)(2,1)S(1)} %collective-permute-done.10.refs_0_, bf16[64,128]{1,0:T(8,128)(2,1)S(1)} %collective-permute-done.11.refs_1_, bf16[64,128]{1,0:T(8,128)(2,1)S(1)} %collective-permute-done.12.refs_2_, ...), custom_call_target="tpu_custom_call" | custom-call | flops 1509949440 | bytes 3932160 | tf_op jit(solution)/shard_map/pallas_call | solution.py:585
  36.4 0.1 collective-permute-start.14
  36.5 0.1 collective-permute-start.15
  36.6 0.0 collective-permute-done.7.refs_4_
  36.6 3.5 %collective-permute-start.16 = (f32[72,128]{1,0:T(8,128)S(1)}, f32[72,128]{1,0:T(8,128)S(1)}, u32[]{:S(2)}, u32[]{:S(2)}) collective-permute-start(f32[72,128]{1,0:T(8,128)S(1)} %get-tuple-element.27), channel_id=1, source_target_pairs={{0,6},{1,7},{2,4},{3,5},{4,2},{5,3},{6,0},{7,1},{8,14},{9,15},{10,... | collective-permute-start | bytes 110600 | tf_op jit(solution)/shard_map/ppermute | solution.py:507
  40.1 0.0 collective-permute-done.8.refs_5_
  40.1 0.6 %collective-permute-start.17 = (f32[72,128]{1,0:T(8,128)S(1)}, f32[72,128]{1,0:T(8,128)S(1)}, u32[]{:S(2)}, u32[]{:S(2)}) collective-permute-start(f32[72,128]{1,0:T(8,128)S(1)} %get-tuple-element.28), channel_id=1, source_target_pairs={{0,7},{1,6},{2,5},{3,4},{4,3},{5,2},{6,1},{7,0},{8,15},{9,14},{10,... | collective-permute-start | bytes 110600 | tf_op jit(solution)/shard_map/ppermute | solution.py:507
  40.7 0.0 collective-permute-done.9.refs_6_
  40.7 0.0 collective-permute-done.14.refs_7_
  40.7 0.0 collective-permute-done.15.refs_8_
  40.7 1.2 %collective-permute-done.16.refs_9_ = f32[72,128]{1,0:T(8,128)S(1)} collective-permute-done((f32[72,128]{1,0:T(8,128)S(1)}, f32[72,128]{1,0:T(8,128)S(1)}, u32[]{:S(2)}, u32[]{:S(2)}) %collective-permute-start.16) | collective-permute-done | bytes 36896 | tf_op jit(solution)/shard_map/ppermute | solution.py:507
  42.0 3.3 %collective-permute-done.17.refs_10_ = f32[72,128]{1,0:T(8,128)S(1)} collective-permute-done((f32[72,128]{1,0:T(8,128)S(1)}, f32[72,128]{1,0:T(8,128)S(1)}, u32[]{:S(2)}, u32[]{:S(2)}) %collective-permute-start.17) | collective-permute-done | bytes 36896 | tf_op jit(solution)/shard_map/ppermute | solution.py:507
  45.3 0.0 copy-done.1
  45.3 0.0 copy-done.5
  45.3 0.6 %shard_map.87 = (f32[2,128]{1,0:T(2,128)S(1)}, f32[2,128]{1,0:T(2,128)S(1)}) custom-call(f32[3,128]{1,0:T(4,128)S(1)} %copy-done.5, bf16[128,128]{1,0:T(8,128)(2,1)S(1)} %copy-done.1, f32[2,128]{1,0:T(2,128)S(1)} %copy-done.6, f32[72,128]{1,0:T(8,128)S(1)} %get-tuple-element.21.refs_3_, f32[72,128]{1,0:T(8,128)S(1)} %collective-permute-done.7.refs_4_, ...), custom_call_target="tpu_custom_call" | custom-call | flops 8388608 | bytes 294912 | tf_op jit(solution)/shard_map/pallas_call | solution.py:601
  45.9 0.0 collective-permute-start.18
  45.9 1.9 %collective-permute-start.19 = (f32[2,128]{1,0:T(2,128)S(1)}, f32[2,128]{1,0:T(2,128)S(1)}, u32[]{:S(2)}, u32[]{:S(2)}) collective-permute-start(f32[2,128]{1,0:T(2,128)S(1)} %get-tuple-element.29.refs_0_), channel_id=1, source_target_pairs={{0,2},{1,3},{2,0},{3,1},{4,6},{5,7},{6,4},{7,5},{8,10},{9,11},{10,... | collective-permute-start | bytes 3080 | tf_op jit(solution)/shard_map/ppermute | solution.py:507
  47.9 2.5 %collective-permute-start.20 = (f32[2,128]{1,0:T(2,128)S(1)}, f32[2,128]{1,0:T(2,128)S(1)}, u32[]{:S(2)}, u32[]{:S(2)}) collective-permute-start(f32[2,128]{1,0:T(2,128)S(1)} %get-tuple-element.29.refs_0_), channel_id=1, source_target_pairs={{0,3},{1,2},{2,1},{3,0},{4,7},{5,6},{6,5},{7,4},{8,11},{9,10},{10,... | collective-permute-start | bytes 3080 | tf_op jit(solution)/shard_map/ppermute | solution.py:507
  50.3 0.0 collective-permute-start.21
  50.3 0.0 collective-permute-start.22
  50.3 0.0 collective-permute-done.18.refs_1_
  50.4 1.6 %collective-permute-start.23 = (f32[2,128]{1,0:T(2,128)S(1)}, f32[2,128]{1,0:T(2,128)S(1)}, u32[]{:S(2)}, u32[]{:S(2)}) collective-permute-start(f32[2,128]{1,0:T(2,128)S(1)} %get-tuple-element.30), channel_id=1, source_target_pairs={{0,6},{1,7},{2,4},{3,5},{4,2},{5,3},{6,0},{7,1},{8,14},{9,15},{10,... | collective-permute-start | bytes 3080 | tf_op jit(solution)/shard_map/ppermute | solution.py:507
  52.0 0.0 collective-permute-done.19.refs_2_
  52.0 2.6 %collective-permute-start.24 = (f32[2,128]{1,0:T(2,128)S(1)}, f32[2,128]{1,0:T(2,128)S(1)}, u32[]{:S(2)}, u32[]{:S(2)}) collective-permute-start(f32[2,128]{1,0:T(2,128)S(1)} %get-tuple-element.30), channel_id=1, source_target_pairs={{0,7},{1,6},{2,5},{3,4},{4,3},{5,2},{6,1},{7,0},{8,15},{9,14},{10,... | collective-permute-start | bytes 3080 | tf_op jit(solution)/shard_map/ppermute | solution.py:507
  54.6 0.0 collective-permute-done.20.refs_3_
  54.6 0.0 collective-permute-done.21.refs_4_
  54.6 0.0 collective-permute-done.22.refs_5_
  54.6 0.0 collective-permute-done.23.refs_6_
  54.6 2.2 %collective-permute-done.24.refs_7_ = f32[2,128]{1,0:T(2,128)S(1)} collective-permute-done((f32[2,128]{1,0:T(2,128)S(1)}, f32[2,128]{1,0:T(2,128)S(1)}, u32[]{:S(2)}, u32[]{:S(2)}) %collective-permute-start.24) | collective-permute-done | bytes 1056 | tf_op jit(solution)/shard_map/ppermute | solution.py:507
  56.8 0.7 %shard_map.88 = f32[1,2,512]{2,1,0:T(2,128)} custom-call(f32[2,128]{1,0:T(2,128)S(1)} %get-tuple-element.29.refs_0_, f32[2,128]{1,0:T(2,128)S(1)} %collective-permute-done.18.refs_1_, f32[2,128]{1,0:T(2,128)S(1)} %collective-permute-done.19.refs_2_, f32[2,128]{1,0:T(2,128)S(1)} %collective-permute-done.20.refs_3_, ...), custom_call_target="tpu_custom_call" | custom-call | flops 1024 | bytes 8192 | tf_op jit(solution)/shard_map/pallas_call | solution.py:611
  (11 shorter events, 0.0 us)
Async XLA Ops:
  0.0 1.5 %copy-start = (bf16[1,32,240,128]{3,2,1,0:T(8,128)(2,1)S(1)}, bf16[1,32,240,128]{3,2,1,0:T(8,128)(2,1)}, u32[]{:S(2)}) copy-start(bf16[1,32,240,128]{3,2,1,0:T(8,128)(2,1)} %param.8) | copy-start | bytes 5898244
  1.5 0.7 %copy-start.2 = (s32[512]{0:T(512)S(1)}, s32[512]{0:T(512)}, u32[]{:S(2)}) copy-start(s32[512]{0:T(512)} %param.9) | copy-start | bytes 6148
  2.2 0.7 %copy-start.3 = (s32[512]{0:T(512)S(1)}, s32[512]{0:T(512)}, u32[]{:S(2)}) copy-start(s32[512]{0:T(512)} %param.10) | copy-start | bytes 6148
  2.9 0.7 %copy-start.4 = (s32[512]{0:T(512)S(1)}, s32[512]{0:T(512)}, u32[]{:S(2)}) copy-start(s32[512]{0:T(512)} %param.11) | copy-start | bytes 6148
  6.6 1.8 %collective-permute-start = (bf16[256,128]{1,0:T(8,128)(2,1)S(1)}, bf16[256,128]{1,0:T(8,128)(2,1)S(1)}, u32[]{:S(2)}, u32[]{:S(2)}) collective-permute-start(bf16[256,128]{1,0:T(8,128)(2,1)S(1)} %get-tuple-element.20), channel_id=1, source_target_pairs={{0,4},{1,5},{2,6},{3,7},{4,0},{5,1},{6,2},{7,3},{8,12},{9,13},{10,... | collective-permute-start | bytes 196616 | tf_op jit(solution)/shard_map/ppermute | solution.py:507
  7.1 18.8 %copy-start.7 = (f32[1,128]{1,0:T(1,128)S(1)}, f32[1,128]{1,0:T(1,128)}, u32[]{:S(2)}) copy-start(f32[1,128]{1,0:T(1,128)} %refs_6_.3) | copy-start | bytes 1540
  8.4 5.3 %collective-permute-start.1 = (bf16[64,128]{1,0:T(8,128)(2,1)S(1)}, bf16[64,128]{1,0:T(8,128)(2,1)S(1)}, u32[]{:S(2)}, u32[]{:S(2)}) collective-permute-start(bf16[64,128]{1,0:T(8,128)(2,1)S(1)} %get-tuple-element.31), channel_id=1, source_target_pairs={{0,1},{1,0},{2,3},{3,2},{4,5},{5,4},{6,7},{7,6},{8,9},{9,8},{10,11... | collective-permute-start | bytes 49160 | tf_op jit(solution)/shard_map/ppermute | solution.py:507
  11.1 4.6 %collective-permute-start.2 = (bf16[64,128]{1,0:T(8,128)(2,1)S(1)}, bf16[64,128]{1,0:T(8,128)(2,1)S(1)}, u32[]{:S(2)}, u32[]{:S(2)}) collective-permute-start(bf16[64,128]{1,0:T(8,128)(2,1)S(1)} %get-tuple-element.33), channel_id=1, source_target_pairs={{0,2},{1,3},{2,0},{3,1},{4,6},{5,7},{6,4},{7,5},{8,10},{9,11},{10,... | collective-permute-start | bytes 49160 | tf_op jit(solution)/shard_map/ppermute | solution.py:507
  13.7 5.5 %collective-permute-start.3 = (bf16[64,128]{1,0:T(8,128)(2,1)S(1)}, bf16[64,128]{1,0:T(8,128)(2,1)S(1)}, u32[]{:S(2)}, u32[]{:S(2)}) collective-permute-start(bf16[64,128]{1,0:T(8,128)(2,1)S(1)} %get-tuple-element.32), channel_id=1, source_target_pairs={{0,3},{1,2},{2,1},{3,0},{4,7},{5,6},{6,5},{7,4},{8,11},{9,10},{10,... | collective-permute-start | bytes 49160 | tf_op jit(solution)/shard_map/ppermute | solution.py:507
  19.2 5.7 %collective-permute-start.4 = (bf16[64,128]{1,0:T(8,128)(2,1)S(1)}, bf16[64,128]{1,0:T(8,128)(2,1)S(1)}, u32[]{:S(2)}, u32[]{:S(2)}) collective-permute-start(bf16[64,128]{1,0:T(8,128)(2,1)S(1)} %fusion.2.refs_0_), channel_id=1, source_target_pairs={{0,1},{1,0},{2,3},{3,2},{4,5},{5,4},{6,7},{7,6},{8,9},{9,8},{10,11... | collective-permute-start | bytes 49160 | tf_op jit(solution)/shard_map/ppermute | solution.py:507
  19.3 6.2 %collective-permute-start.5 = (bf16[64,128]{1,0:T(8,128)(2,1)S(1)}, bf16[64,128]{1,0:T(8,128)(2,1)S(1)}, u32[]{:S(2)}, u32[]{:S(2)}) collective-permute-start(bf16[64,128]{1,0:T(8,128)(2,1)S(1)} %fusion.2.refs_0_), channel_id=1, source_target_pairs={{0,2},{1,3},{2,0},{3,1},{4,6},{5,7},{6,4},{7,5},{8,10},{9,11},{10,... | collective-permute-start | bytes 49160 | tf_op jit(solution)/shard_map/ppermute | solution.py:507
  20.0 5.5 %collective-permute-start.6 = (bf16[64,128]{1,0:T(8,128)(2,1)S(1)}, bf16[64,128]{1,0:T(8,128)(2,1)S(1)}, u32[]{:S(2)}, u32[]{:S(2)}) collective-permute-start(bf16[64,128]{1,0:T(8,128)(2,1)S(1)} %fusion.2.refs_0_), channel_id=1, source_target_pairs={{0,3},{1,2},{2,1},{3,0},{4,7},{5,6},{6,5},{7,4},{8,11},{9,10},{10,... | collective-permute-start | bytes 49160 | tf_op jit(solution)/shard_map/ppermute | solution.py:507
  24.9 4.6 %collective-permute-start.10 = (bf16[64,128]{1,0:T(8,128)(2,1)S(1)}, bf16[64,128]{1,0:T(8,128)(2,1)S(1)}, u32[]{:S(2)}, u32[]{:S(2)}) collective-permute-start(bf16[64,128]{1,0:T(8,128)(2,1)S(1)} %fusion.2.refs_0_), channel_id=1, source_target_pairs={{0,4},{1,5},{2,6},{3,7},{4,0},{5,1},{6,2},{7,3},{8,12},{9,13},{10,... | collective-permute-start | bytes 49160 | tf_op jit(solution)/shard_map/ppermute | solution.py:507
  24.9 7.9 %collective-permute-start.11 = (bf16[64,128]{1,0:T(8,128)(2,1)S(1)}, bf16[64,128]{1,0:T(8,128)(2,1)S(1)}, u32[]{:S(2)}, u32[]{:S(2)}) collective-permute-start(bf16[64,128]{1,0:T(8,128)(2,1)S(1)} %collective-permute-done.4.refs_1_), channel_id=1, source_target_pairs={{0,4},{1,5},{2,6},{3,7},{4,0},{5,1},{6,2},{7,3},{8,12},{9,13},{10,... | collective-permute-start | bytes 49160 | tf_op jit(solution)/shard_map/ppermute | solution.py:507
  25.4 8.0 %collective-permute-start.12 = (bf16[64,128]{1,0:T(8,128)(2,1)S(1)}, bf16[64,128]{1,0:T(8,128)(2,1)S(1)}, u32[]{:S(2)}, u32[]{:S(2)}) collective-permute-start(bf16[64,128]{1,0:T(8,128)(2,1)S(1)} %collective-permute-done.5.refs_2_), channel_id=1, source_target_pairs={{0,4},{1,5},{2,6},{3,7},{4,0},{5,1},{6,2},{7,3},{8,12},{9,13},{10,... | collective-permute-start | bytes 49160 | tf_op jit(solution)/shard_map/ppermute | solution.py:507
  25.5 7.9 %collective-permute-start.13 = (bf16[64,128]{1,0:T(8,128)(2,1)S(1)}, bf16[64,128]{1,0:T(8,128)(2,1)S(1)}, u32[]{:S(2)}, u32[]{:S(2)}) collective-permute-start(bf16[64,128]{1,0:T(8,128)(2,1)S(1)} %collective-permute-done.6.refs_3_), channel_id=1, source_target_pairs={{0,4},{1,5},{2,6},{3,7},{4,0},{5,1},{6,2},{7,3},{8,12},{9,13},{10,... | collective-permute-start | bytes 49160 | tf_op jit(solution)/shard_map/ppermute | solution.py:507
  28.9 7.7 %collective-permute-start.7 = (f32[72,128]{1,0:T(8,128)S(1)}, f32[72,128]{1,0:T(8,128)S(1)}, u32[]{:S(2)}, u32[]{:S(2)}) collective-permute-start(f32[72,128]{1,0:T(8,128)S(1)} %get-tuple-element.22), channel_id=1, source_target_pairs={{0,1},{1,0},{2,3},{3,2},{4,5},{5,4},{6,7},{7,6},{8,9},{9,8},{10,11... | collective-permute-start | bytes 110600 | tf_op jit(solution)/shard_map/ppermute | solution.py:507
  29.5 10.6 %collective-permute-start.8 = (f32[72,128]{1,0:T(8,128)S(1)}, f32[72,128]{1,0:T(8,128)S(1)}, u32[]{:S(2)}, u32[]{:S(2)}) collective-permute-start(f32[72,128]{1,0:T(8,128)S(1)} %get-tuple-element.23), channel_id=1, source_target_pairs={{0,2},{1,3},{2,0},{3,1},{4,6},{5,7},{6,4},{7,5},{8,10},{9,11},{10,... | collective-permute-start | bytes 110600 | tf_op jit(solution)/shard_map/ppermute | solution.py:507
  32.8 12.5 %copy-start.1 = (bf16[128,128]{1,0:T(8,128)(2,1)S(1)}, bf16[128,128]{1,0:T(8,128)(2,1)}, u32[]{:S(2)}) copy-start(bf16[128,128]{1,0:T(8,128)(2,1)} %refs_1_.1) | copy-start | bytes 98308
  32.8 12.5 %copy-start.5 = (f32[3,128]{1,0:T(4,128)S(1)}, f32[3,128]{1,0:T(4,128)}, u32[]{:S(2)}) copy-start(f32[3,128]{1,0:T(4,128)} %refs_0_.1) | copy-start | bytes 4612
  32.8 12.5 %copy-start.6 = (f32[2,128]{1,0:T(2,128)S(1)}, f32[2,128]{1,0:T(2,128)}, u32[]{:S(2)}) copy-start(f32[2,128]{1,0:T(2,128)} %refs_2_.1) | copy-start | bytes 3076
  32.8 7.9 %collective-permute-start.9 = (f32[72,128]{1,0:T(8,128)S(1)}, f32[72,128]{1,0:T(8,128)S(1)}, u32[]{:S(2)}, u32[]{:S(2)}) collective-permute-start(f32[72,128]{1,0:T(8,128)S(1)} %get-tuple-element.24), channel_id=1, source_target_pairs={{0,3},{1,2},{2,1},{3,0},{4,7},{5,6},{6,5},{7,4},{8,11},{9,10},{10,... | collective-permute-start | bytes 110600 | tf_op jit(solution)/shard_map/ppermute | solution.py:507
  36.4 4.3 %collective-permute-start.14 = (f32[72,128]{1,0:T(8,128)S(1)}, f32[72,128]{1,0:T(8,128)S(1)}, u32[]{:S(2)}, u32[]{:S(2)}) collective-permute-start(f32[72,128]{1,0:T(8,128)S(1)} %get-tuple-element.25), channel_id=1, source_target_pairs={{0,4},{1,5},{2,6},{3,7},{4,0},{5,1},{6,2},{7,3},{8,12},{9,13},{10,... | collective-permute-start | bytes 110600 | tf_op jit(solution)/shard_map/ppermute | solution.py:507
  36.5 4.2 %collective-permute-start.15 = (f32[72,128]{1,0:T(8,128)S(1)}, f32[72,128]{1,0:T(8,128)S(1)}, u32[]{:S(2)}, u32[]{:S(2)}) collective-permute-start(f32[72,128]{1,0:T(8,128)S(1)} %get-tuple-element.26), channel_id=1, source_target_pairs={{0,5},{1,4},{2,7},{3,6},{4,1},{5,0},{6,3},{7,2},{8,13},{9,12},{10,... | collective-permute-start | bytes 110600 | tf_op jit(solution)/shard_map/ppermute | solution.py:507
  36.6 5.3 %collective-permute-start.16 = (f32[72,128]{1,0:T(8,128)S(1)}, f32[72,128]{1,0:T(8,128)S(1)}, u32[]{:S(2)}, u32[]{:S(2)}) collective-permute-start(f32[72,128]{1,0:T(8,128)S(1)} %get-tuple-element.27), channel_id=1, source_target_pairs={{0,6},{1,7},{2,4},{3,5},{4,2},{5,3},{6,0},{7,1},{8,14},{9,15},{10,... | collective-permute-start | bytes 110600 | tf_op jit(solution)/shard_map/ppermute | solution.py:507
  40.1 5.2 %collective-permute-start.17 = (f32[72,128]{1,0:T(8,128)S(1)}, f32[72,128]{1,0:T(8,128)S(1)}, u32[]{:S(2)}, u32[]{:S(2)}) collective-permute-start(f32[72,128]{1,0:T(8,128)S(1)} %get-tuple-element.28), channel_id=1, source_target_pairs={{0,7},{1,6},{2,5},{3,4},{4,3},{5,2},{6,1},{7,0},{8,15},{9,14},{10,... | collective-permute-start | bytes 110600 | tf_op jit(solution)/shard_map/ppermute | solution.py:507
  45.9 4.4 %collective-permute-start.18 = (f32[2,128]{1,0:T(2,128)S(1)}, f32[2,128]{1,0:T(2,128)S(1)}, u32[]{:S(2)}, u32[]{:S(2)}) collective-permute-start(f32[2,128]{1,0:T(2,128)S(1)} %get-tuple-element.29.refs_0_), channel_id=1, source_target_pairs={{0,1},{1,0},{2,3},{3,2},{4,5},{5,4},{6,7},{7,6},{8,9},{9,8},{10,11... | collective-permute-start | bytes 3080 | tf_op jit(solution)/shard_map/ppermute | solution.py:507
  45.9 6.1 %collective-permute-start.19 = (f32[2,128]{1,0:T(2,128)S(1)}, f32[2,128]{1,0:T(2,128)S(1)}, u32[]{:S(2)}, u32[]{:S(2)}) collective-permute-start(f32[2,128]{1,0:T(2,128)S(1)} %get-tuple-element.29.refs_0_), channel_id=1, source_target_pairs={{0,2},{1,3},{2,0},{3,1},{4,6},{5,7},{6,4},{7,5},{8,10},{9,11},{10,... | collective-permute-start | bytes 3080 | tf_op jit(solution)/shard_map/ppermute | solution.py:507
  47.9 6.7 %collective-permute-start.20 = (f32[2,128]{1,0:T(2,128)S(1)}, f32[2,128]{1,0:T(2,128)S(1)}, u32[]{:S(2)}, u32[]{:S(2)}) collective-permute-start(f32[2,128]{1,0:T(2,128)S(1)} %get-tuple-element.29.refs_0_), channel_id=1, source_target_pairs={{0,3},{1,2},{2,1},{3,0},{4,7},{5,6},{6,5},{7,4},{8,11},{9,10},{10,... | collective-permute-start | bytes 3080 | tf_op jit(solution)/shard_map/ppermute | solution.py:507
  50.3 4.2 %collective-permute-start.21 = (f32[2,128]{1,0:T(2,128)S(1)}, f32[2,128]{1,0:T(2,128)S(1)}, u32[]{:S(2)}, u32[]{:S(2)}) collective-permute-start(f32[2,128]{1,0:T(2,128)S(1)} %get-tuple-element.30), channel_id=1, source_target_pairs={{0,4},{1,5},{2,6},{3,7},{4,0},{5,1},{6,2},{7,3},{8,12},{9,13},{10,... | collective-permute-start | bytes 3080 | tf_op jit(solution)/shard_map/ppermute | solution.py:507
  50.3 4.2 %collective-permute-start.22 = (f32[2,128]{1,0:T(2,128)S(1)}, f32[2,128]{1,0:T(2,128)S(1)}, u32[]{:S(2)}, u32[]{:S(2)}) collective-permute-start(f32[2,128]{1,0:T(2,128)S(1)} %get-tuple-element.30), channel_id=1, source_target_pairs={{0,5},{1,4},{2,7},{3,6},{4,1},{5,0},{6,3},{7,2},{8,13},{9,12},{10,... | collective-permute-start | bytes 3080 | tf_op jit(solution)/shard_map/ppermute | solution.py:507
  50.4 4.2 %collective-permute-start.23 = (f32[2,128]{1,0:T(2,128)S(1)}, f32[2,128]{1,0:T(2,128)S(1)}, u32[]{:S(2)}, u32[]{:S(2)}) collective-permute-start(f32[2,128]{1,0:T(2,128)S(1)} %get-tuple-element.30), channel_id=1, source_target_pairs={{0,6},{1,7},{2,4},{3,5},{4,2},{5,3},{6,0},{7,1},{8,14},{9,15},{10,... | collective-permute-start | bytes 3080 | tf_op jit(solution)/shard_map/ppermute | solution.py:507
  52.0 4.8 %collective-permute-start.24 = (f32[2,128]{1,0:T(2,128)S(1)}, f32[2,128]{1,0:T(2,128)S(1)}, u32[]{:S(2)}, u32[]{:S(2)}) collective-permute-start(f32[2,128]{1,0:T(2,128)S(1)} %get-tuple-element.30), channel_id=1, source_target_pairs={{0,7},{1,6},{2,5},{3,4},{4,3},{5,2},{6,1},{7,0},{8,15},{9,14},{10,... | collective-permute-start | bytes 3080 | tf_op jit(solution)/shard_map/ppermute | solution.py:507

commit v3 on v1

--- a/solution.py
+++ b/solution.py
@@ -12,6 +12,7 @@
 BF16 = jnp.bfloat16
 LANES = 128
 AUX_ROWS = 8
+PIECE_ROWS = 16
 VMEM_LIMIT = 40 * 1024 * 1024
 NT = (((1,), (1,)), ((), ()))
 
@@ -187,6 +188,195 @@
     )
 
 
+def hot_rows(target, map_ref, base, chunk):
+    rows = target.shape[0]
+    lane = lax.broadcasted_iota(jnp.int32, (rows, LANES), 1)
+    parts = []
+    for lane_base in range(base, base + chunk, LANES):
+        parts.append(jnp.where(lane + lane_base == target, 1.0, 0.0).astype(BF16))
+    hot = jnp.concatenate(parts, axis=1)
+    return jnp.dot(hot, map_ref[base : base + chunk, :], preferred_element_type=F32)
+
+
+def pick_kernel(core_flip, target_ref, map_ref, out_ref):
+    half = target_ref.shape[1] // 2
+    positions = map_ref.shape[0]
+    chunk = pick_chunk(positions, 1536)
+    second = lax.axis_index("tm") != core_flip
+    target = jnp.where(second, target_ref[:, half:], target_ref[:, :half])
+    target = jnp.transpose(jnp.broadcast_to(target, (LANES, half)))
+    picked = None
+    for base in range(0, positions, chunk):
+        term = hot_rows(target, map_ref, base, chunk)
+        picked = term if picked is None else picked + term
+    out_ref[...] = picked.astype(BF16)
+
+
+def coord_kernel(map_width, after_ref, out_ref):
+    positions = out_ref.shape[0]
+    chunk = pick_chunk(positions, 512)
+    lane = lax.broadcasted_iota(jnp.int32, (chunk, LANES), 1)
+    local_place = lax.broadcasted_iota(jnp.int32, (chunk, LANES), 0).astype(F32)
+
+    @pl.loop(0, positions // chunk)
+    def _(step):
+        place = local_place + (step * chunk).astype(F32)
+        row = jnp.floor((place + 0.5) * (1.0 / map_width))
+        rest = jnp.where(lane == 2, 1.0, 0.0)
+        value = jnp.where(lane == 0, place - row * map_width, jnp.where(lane == 1, row, rest))
+        out_ref[pl.ds(pl.multiple_of(step * chunk, chunk), chunk), :] = value.astype(BF16)
+
+
+def split(value):
+    pieces = []
+    for _ in range(3):
+        piece = value.astype(BF16).astype(F32)
+        pieces.append(piece)
+        value = value - piece
+    return pieces
+
+
+def by_partner(values, n_space):
+    space = lax.axis_index("space")
+    bit = 1
+    while bit < n_space:
+        turn = (space & bit) != 0
+        values = [jnp.where(turn, values[i ^ bit], values[i]) for i in range(len(values))]
+        bit *= 2
+    return values
+
+
+def half_kernel(n_space, rows_here, height, width, query_ref, map_ref, coord_ref, *out_refs):
+    positions, channels = map_ref.shape
+    factor = math.log2(math.e) / math.sqrt(channels)
+    query = query_ref[...]
+    group = query.shape[0] // n_space
+    first_row = (lax.axis_index("space") * rows_here).astype(F32)
+    chunk = pick_chunk(positions, 1280)
+
+    def score(base):
+        keys = map_ref[base : base + chunk, :]
+        return lax.dot_general(query, keys, NT, preferred_element_type=F32)
+
+    top = sums = None
+    ahead = score(0)
+    for base in range(0, positions, chunk):
+        scores = ahead
+        if base + chunk < positions:
+            ahead = score(base + chunk)
+        window = slice(base, base + chunk)
+        values = jnp.concatenate([map_ref[window, :], coord_ref[window, :]], axis=1)
+        new_top = jnp.max(scores, axis=1, keepdims=True) * factor
+        if top is not None:
+            new_top = jnp.maximum(new_top, top)
+        weights = jnp.exp2(scores * factor - new_top).astype(BF16)
+        terms = jnp.dot(weights, values, preferred_element_type=F32)
+        sums = terms if sums is None else terms + jnp.exp2(top - new_top) * sums
+        top = new_top
+    feats = sums[:, :channels] / sums[:, channels + 2 : channels + 3]
+    extra = sums[:, channels:]
+    lane = lax.broadcasted_iota(jnp.int32, extra.shape, 1)
+    extra = jnp.transpose(jnp.where(lane == 3, top, extra))
+    total = extra[2:3]
+    across = extra[0:1] / total / width
+    down = (extra[1:2] / total + first_row) / height
+    rows = [piece for value in (extra[3:4], total, across, down) for piece in split(value)]
+    aux = jnp.zeros((PIECE_ROWS, extra.shape[1]), F32)
+    sub = lax.broadcasted_iota(jnp.int32, aux.shape, 0)
+    for index, values in enumerate(rows):
+        aux = jnp.where(sub == index, values, aux)
+    blocks = []
+    for index in range(n_space):
+        shift = (aux.shape[1] - index * group) % aux.shape[1]
+        block = pltpu.roll(aux, shift, 1) if shift else aux
+        blocks.append(
+            jnp.concatenate([feats[index * group : (index + 1) * group], block[:, :LANES]], axis=0)
+        )
+    for out_ref, block in zip(out_refs, by_partner(blocks, n_space)):
+        out_ref[...] = block
+
+
+def merge(blocks, group):
+    aux = [block[group:] for block in blocks]
+    tops = [b[0:1] + b[1:2] + b[2:3] for b in aux]
+    top = functools.reduce(jnp.maximum, tops)
+    weight = [jnp.exp2(t - top) * (b[3:4] + b[4:5] + b[5:6]) for t, b in zip(tops, aux)]
+    total = sum(weight[1:], weight[0])
+    share = [w / total for w in weight]
+    across = [s * (b[6:7] + b[7:8] + b[8:9]) for s, b in zip(share, aux)]
+    down = [s * (b[9:10] + b[10:11] + b[11:12]) for s, b in zip(share, aux)]
+    across, down = sum(across[1:], across[0]), sum(down[1:], down[0])
+    table = jnp.zeros((8, LANES), F32)
+    sub = lax.broadcasted_iota(jnp.int32, table.shape, 0)
+    for index, value in enumerate(share):
+        table = jnp.where(sub == index, value, table)
+    table = jnp.transpose(table)
+    attended = None
+    for index, block in enumerate(blocks):
+        term = table[:group, index : index + 1] * block[:group]
+        attended = term if attended is None else attended + term
+    return across, down, attended.astype(BF16).astype(F32)
+
+
+def merge_kernel(group, decay_ref, *refs):
+    block_refs, (out_ref, place_ref) = refs[:-2], refs[-2:]
+    blocks = [ref[...] for ref in block_refs]
+    size = group + PIECE_ROWS
+    near = merge([block[:size] for block in blocks], group)
+    far = merge([block[size:] for block in blocks], group)
+    out_ref[:group, :] = near[2]
+    out_ref[group : 2 * group, :] = far[2]
+    out_ref[2 * group :, :] = jnp.broadcast_to(decay_ref[...], (8, LANES))
+    lane = lax.broadcasted_iota(jnp.int32, (1, LANES), 1)
+    for index in range(2):
+        moved = pltpu.roll(jnp.broadcast_to(far[index], (8, LANES)), group, 1)[0:1]
+        place_ref[index : index + 1, :] = jnp.where(lane < group, near[index], moved)
+
+
+def track_kernel(group, dw_ref, pw_ref, ow_ref, place_ref, mine_ref, theirs_ref, out_ref):
+    early = lax.axis_index("tm") == 0
+    mine = mine_ref[: 2 * group]
+    theirs = jnp.concatenate([theirs_ref[group : 2 * group], theirs_ref[:group]], axis=0)
+    attended = [jnp.where(early, mine, theirs), jnp.where(early, theirs, mine)]
+    decay_mine, decay_theirs = mine_ref[2 * group : 2 * group + 1], theirs_ref[2 * group : 2 * group + 1]
+    decay = [
+        jnp.where(early, decay_mine, decay_theirs),
+        jnp.where(early, decay_theirs, decay_mine),
+    ]
+    taps = dw_ref.shape[0]
+    hidden = []
+    for frame in range(2):
+        depth = None
+        for tap in range(taps):
+            source = frame + tap - taps // 2
+            if 0 <= source < 2:
+                term = dw_ref[tap : tap + 1, :] * attended[source]
+                depth = term if depth is None else depth + term
+        hidden.append(jax.nn.gelu(depth).astype(BF16))
+    hidden = jnp.concatenate(hidden, axis=0)
+    mixed = jnp.dot(hidden, pw_ref[...], preferred_element_type=F32)
+    first = (1.0 - decay[0]) * (attended[0] + mixed[: 2 * group])
+    second = decay[1] * first + (1.0 - decay[1]) * (attended[1] + mixed[2 * group :])
+    memory = jnp.where(early, first, second)
+    delta = lax.dot_general(
+        ow_ref[...], memory, NT, preferred_element_type=F32, precision=lax.Precision.HIGHEST
+    )
+    out_ref[...] = place_ref[...] + delta
+
+
+def lay_kernel(n_space, group, *refs):
+    out_ref = refs[n_space]
+    lines = by_partner([ref[...] for ref in refs[:n_space]], n_space)
+    early = lax.axis_index("tm") == 0
+    swapped = [pltpu.roll(line, group, 1) for line in lines]
+    halves = [jnp.where(early, a, b) for a, b in zip(lines, swapped)]
+    halves += [jnp.where(early, b, a) for a, b in zip(lines, swapped)]
+    lane = lax.broadcasted_iota(jnp.int32, lines[0].shape, 1)
+    for tile in range(n_space):
+        low, high = halves[2 * tile], pltpu.roll(halves[2 * tile + 1], group, 1)
+        out_ref[0, :, tile * LANES : (tile + 1) * LANES] = jnp.where(lane < group, low, high)
+
+
 def swap(value, axis, bit):
     return lax.ppermute(value, axis, [(i, i ^ bit) for i in range(lax.axis_size(axis))])
 
@@ -202,7 +392,7 @@
     return value
 
 
-def local(
+def local_general(
     feature_maps, query_frame, query_row, query_col, ema_decay, dw_kernel, pw_weight, out_weight
 ):
     frames_here, rows_here, map_width, channels = feature_maps.shape
@@ -268,6 +458,109 @@
     own = lax.dynamic_slice_in_dim(lines, lax.axis_index("tm") * n_out, n_out, axis=1)
     own = own[:, :, :group]
     return jnp.transpose(own, (1, 0, 2)).reshape(1, n_out, queries)
+
+
+def partner(value, flip, bits):
+    n_space = lax.axis_size("space")
+    pairs = []
+    for tm in range(2):
+        for space in range(n_space):
+            pairs.append((tm * n_space + space, (tm ^ flip) * n_space + (space ^ bits)))
+    return lax.ppermute(value, ("tm", "space"), pairs)
+
+
+def local_pair(
+    feature_maps, query_frame, query_row, query_col, ema_decay, dw_kernel, pw_weight, out_weight
+):
+    _, rows_here, map_width, channels = feature_maps.shape
+    queries = query_frame.shape[0]
+    n_space = lax.axis_size("space")
+    half = queries // 2
+    group = half // n_space
+    height = rows_here * n_space
+    positions = rows_here * map_width
+    maps = feature_maps.reshape(positions, channels)
+
+    row = query_row - lax.axis_index("space") * rows_here
+    here = (query_frame == lax.axis_index("tm")) & (row >= 0) & (row < rows_here)
+    target = jnp.where(here, row * map_width + query_col, -1)[None]
+
+    def pick(core_flip):
+        return call(
+            functools.partial(pick_kernel, core_flip),
+            jax.ShapeDtypeStruct((half, channels), BF16),
+            2,
+            flops=queries * positions * channels,
+            bytes_accessed=2 * positions * channels,
+            transcendentals=0,
+        )(target, maps)
+
+    arrived = partner(pick(1), 1, 0)
+    coords = call(
+        functools.partial(coord_kernel, map_width),
+        jax.ShapeDtypeStruct((positions, LANES), BF16),
+        1,
+        flops=8 * positions * LANES,
+        bytes_accessed=2 * positions * LANES,
+        transcendentals=0,
+    )(target)
+    mine = all_sum(pick(0) + arrived, "space")
+    theirs = partner(mine, 1, 0)
+
+    def blocks_of(feats):
+        shape = jax.ShapeDtypeStruct((group + PIECE_ROWS, LANES), F32)
+        return call(
+            functools.partial(half_kernel, n_space, rows_here, height, map_width),
+            [shape] * n_space,
+            3,
+            flops=3 * queries * positions * channels,
+            bytes_accessed=4 * positions * channels,
+            transcendentals=half * positions,
+        )(feats, maps, coords)
+
+    near, far = blocks_of(mine), blocks_of(theirs)
+    blocks = [jnp.concatenate([a, b], axis=0) for a, b in zip(near, far)]
+    for k in reversed(range(1, n_space)):
+        blocks[k] = partner(blocks[k].astype(jnp.float16), 0, k).astype(F32)
+
+    n_out = out_weight.shape[0]
+    attended, place = call(
+        functools.partial(merge_kernel, group),
+        [
+            jax.ShapeDtypeStruct((2 * group + 8, LANES), F32),
+            jax.ShapeDtypeStruct((n_out, LANES), F32),
+        ],
+        1 + n_space,
+        flops=4 * n_space * group * channels,
+        bytes_accessed=8 * n_space * group * channels,
+        transcendentals=0,
+    )(ema_decay, *blocks)
+    line = call(
+        functools.partial(track_kernel, group),
+        jax.ShapeDtypeStruct((n_out, LANES), F32),
+        6,
+        flops=16 * group * channels * channels,
+        bytes_accessed=16 * group * channels,
+        transcendentals=4 * group * channels,
+    )(dw_kernel, pw_weight, out_weight, place, attended, partner(attended, 1, 0))
+    lines = [line] + [partner(line, 0, k) for k in range(1, n_space)]
+    return call(
+        functools.partial(lay_kernel, n_space, group),
+        jax.ShapeDtypeStruct((1, n_out, queries), F32),
+        n_space,
+        flops=n_out * queries,
+        bytes_accessed=8 * n_out * queries,
+        transcendentals=0,
+    )(*lines)
+
+
+def local(feature_maps, query_frame, *rest):
+    n_tm, n_space = lax.axis_size("tm"), lax.axis_size("space")
+    group = query_frame.shape[0] // (n_tm * n_space)
+    paired = n_tm == 2 and n_space & (n_space - 1) == 0 and n_space <= 8
+    if paired and 2 * group == LANES:
+        return local_pair(feature_maps, query_frame, *rest)
+    return local_general(feature_maps, query_frame, *rest)
 
 
 def solution(mesh):

time: 70.4 us -> 41.5 us (0.59)
  blocking collectives: 23.7 us -> 0 us
  other arithmetic: 4.81 us -> 0.9 us
  starting transfers between devices: 12.2 us -> 15.1 us
  waiting for transfers between devices: 15.7 us -> 12.9 us
  local copies, waits for them, and re-layouts: 4.29 us -> 1.58 us
  Pallas kernels: 9.28 us -> 10.6 us
    all_gather x1 -> x0, blocking collectives: 23.7 us -> none  [local(): lines = lax.all_gather(lines, ('tm', 'space'), axis=0)]
    all_to_all x1 -> x0, waiting for transfers between devices: 10 us -> none  [local(): blocks = lax.all_to_all(blocks, ('tm', 'space'), 0, 0, tiled=True)]
    ppermute x0 -> x9, starting transfers between devices: none -> 9.64 us  [partner(): return lax.ppermute(value, ('tm', 'space'), pairs)]
    ppermute x0 -> x9, waiting for transfers between devices: none -> 7.59 us  [partner(): return lax.ppermute(value, ('tm', 'space'), pairs)]
    all_to_all x1 -> x0, starting transfers between devices: 5.73 us -> none  [local(): blocks = lax.all_to_all(blocks, ('tm', 'space'), 0, 0, tiled=True)]
    convert_element_type x1 -> x3, other arithmetic: 4.72 us -> 0.02 us  [local_pair(): blocks[k] = partner(blocks[k].astype(jnp.float16), 0, k).astype(F32)]
    unnamed x16 -> x12, local copies, waits for them, and re-layouts: 3.61 us -> 1.58 us
    pallas_call x3 -> x8, Pallas kernels: 9.28 us -> 10.6 us  [the longest x2 5.51 us: blocks_of(): call(functools.partial(half_kernel, n_space, rows_here, height, map_width...]
  transfers between devices with their start and end apart: 5 -> 11, of which waited for: 4 -> 8; matrix products, arithmetic and copies ran while one was open for 7% -> 0% of each run, Pallas kernels for 0% -> 13%
where the time goes in v3:
time: 41.5 us; the launch traced here: 41.3 us
  starting transfers between devices  15.1 us (36%)
  waiting for transfers between devices  12.9 us (31%)
  Pallas kernels  10.6 us (26%)
  local copies, waits for them, and re-layouts  1.58 us (4%)
  other arithmetic  0.9 us (2%)
    ppermute x9, starting transfers between devices, partner(): return lax.ppermute(value, ('tm', 'space'), pairs)  9.64 us
    ppermute x9, waiting for transfers between devices, partner(): return lax.ppermute(value, ('tm', 'space'), pairs)  7.59 us
    pallas_call x2, Pallas kernels, blocks_of(): call(functools.partial(half_kernel, n_space, rows_here, height, map_width...  5.51 us
    ppermute x2, starting transfers between devices, swap(): lax.ppermute(value, axis, [(i, i ^ bit) for i in range(lax.axis_size(axis...  5.47 us
    ppermute x2, waiting for transfers between devices, swap(): lax.ppermute(value, axis, [(i, i ^ bit) for i in range(lax.axis_size(axis...  5.3 us
    pallas_call x2, Pallas kernels, pick(): call(functools.partial(pick_kernel, core_flip), jax.ShapeDtypeStruct((hal...  2.49 us
    unnamed x12, local copies, waits for them, and re-layouts  1.58 us
    pallas_call x1, Pallas kernels, local_pair(): call(functools.partial(coord_kernel, map_width), jax.ShapeDtypeStruct((po...  1.19 us
  transfers between devices with their start and end apart: 11, of which 8 were waited for; matrix products, arithmetic and copies ran while one was open for 0% of the time, Pallas kernels for 13%

profile of v3, /device:TPU:0, one launch (start us, length us, event | category | flops | bytes accessed | tf_op | source)
XLA Modules:
  0.0 41.3 jit_solution(8682831499923320836)
XLA Ops:
  0.0 0.7 %add_select_fusion = s32[512]{0:T(512)S(1)} fusion(s32[512]{0:T(512)} %param.11, s32[512]{0:T(512)} %param.10, s32[512]{0:T(512)} %param.9, s32[]{:T(128)S(6)} %mul.9, s32[]{:T(128)S(6)} %axis_index.23), kind=kLoop, calls=%fused_computation.4 | loop fusion | flops 4608 | bytes 8200 | tf_op jit(solution)/shard_map/jit(_where)/select_n | solution.py:486
  0.7 0.0 copy-start
  0.7 1.5 %copy-done = bf16[1,32,240,128]{3,2,1,0:T(8,128)(2,1)S(1)} copy-done((bf16[1,32,240,128]{3,2,1,0:T(8,128)(2,1)S(1)}, bf16[1,32,240,128]{3,2,1,0:T(8,128)(2,1)}, u32[]{:S(2)}) %copy-start) | copy-done | bytes 1966104
  2.3 1.2 %shard_map.83 = bf16[256,128]{1,0:T(8,128)(2,1)S(1)} custom-call(s32[1,512]{1,0:T(1,128)S(1)} %bitcast.6, bf16[7680,128]{1,0:T(8,128)(2,1)S(1)} %bitcast.2), custom_call_target="tpu_custom_call" | custom-call | flops 503316480 | bytes 1966080 | tf_op jit(solution)/shard_map/pallas_call | solution.py:489
  3.5 0.0 copy-start.1
  3.5 0.5 %collective-permute-start = (bf16[256,128]{1,0:T(8,128)(2,1)S(1)}, bf16[256,128]{1,0:T(8,128)(2,1)S(1)}, u32[]{:S(2)}, u32[]{:S(2)}) collective-permute-start(bf16[256,128]{1,0:T(8,128)(2,1)S(1)} %shard_map.83), channel_id=1, source_target_pairs={{0,4},{1,5},{2,6},{3,7},{4,0},{5,1},{6,2},{7,3},{8,12},{9,13},{10,... | collective-permute-start | bytes 196616 | tf_op jit(solution)/shard_map/ppermute | solution.py:469
  4.0 1.2 %shard_map.82 = bf16[256,128]{1,0:T(8,128)(2,1)S(1)} custom-call(s32[1,512]{1,0:T(1,128)S(1)} %bitcast.7, bf16[7680,128]{1,0:T(8,128)(2,1)S(1)} %bitcast.3), custom_call_target="tpu_custom_call" | custom-call | flops 503316480 | bytes 1966080 | tf_op jit(solution)/shard_map/pallas_call | solution.py:489
  5.3 0.0 collective-permute-done
  5.3 2.6 %collective-permute-start.1 = (bf16[256,128]{1,0:T(8,128)(2,1)S(1)}, bf16[256,128]{1,0:T(8,128)(2,1)S(1)}, u32[]{:S(2)}, u32[]{:S(2)}) collective-permute-start(bf16[256,128]{1,0:T(8,128)(2,1)S(1)} %add.13), channel_id=1, source_target_pairs={{0,1},{1,0},{2,3},{3,2},{4,5},{5,4},{6,7},{7,6},{8,9},{9,8},{10,11... | collective-permute-start | bytes 196616 | tf_op jit(solution)/shard_map/ppermute | solution.py:381
  8.0 2.8 %collective-permute-done.1 = bf16[256,128]{1,0:T(8,128)(2,1)S(1)} collective-permute-done((bf16[256,128]{1,0:T(8,128)(2,1)S(1)}, bf16[256,128]{1,0:T(8,128)(2,1)S(1)}, u32[]{:S(2)}, u32[]{:S(2)}) %collective-permute-start.1) | collective-permute-done | bytes 65568 | tf_op jit(solution)/shard_map/ppermute | solution.py:381
  10.8 2.8 %collective-permute-start.2 = (bf16[256,128]{1,0:T(8,128)(2,1)S(1)}, bf16[256,128]{1,0:T(8,128)(2,1)S(1)}, u32[]{:S(2)}, u32[]{:S(2)}) collective-permute-start(bf16[256,128]{1,0:T(8,128)(2,1)S(1)} %add.14), channel_id=1, source_target_pairs={{0,2},{1,3},{2,0},{3,1},{4,6},{5,7},{6,4},{7,5},{8,10},{9,11},{10,... | collective-permute-start | bytes 196616 | tf_op jit(solution)/shard_map/ppermute | solution.py:381
  13.6 1.2 %shard_map.84.coord_ref = bf16[7680,128]{1,0:T(8,128)(2,1)S(1)} custom-call(s32[1,512]{1,0:T(1,128)S(1)} %bitcast.8), custom_call_target="tpu_custom_call" | custom-call | flops 7864320 | bytes 1966080 | tf_op jit(solution)/shard_map/pallas_call | solution.py:499
  14.8 2.5 %collective-permute-done.2 = bf16[256,128]{1,0:T(8,128)(2,1)S(1)} collective-permute-done((bf16[256,128]{1,0:T(8,128)(2,1)S(1)}, bf16[256,128]{1,0:T(8,128)(2,1)S(1)}, u32[]{:S(2)}, u32[]{:S(2)}) %collective-permute-start.2) | collective-permute-done | bytes 65568 | tf_op jit(solution)/shard_map/ppermute | solution.py:381
  17.4 0.1 collective-permute-start.3
  17.4 0.0 copy-done.1
  17.4 2.7 %shard_map.85 = (f32[80,128]{1,0:T(8,128)S(1)}, f32[80,128]{1,0:T(8,128)S(1)}, f32[80,128]{1,0:T(8,128)S(1)}, f32[80,128]{1,0:T(8,128)S(1)}) custom-call(bf16[256,128]{1,0:T(8,128)(2,1)S(1)} %add.15.query_ref, bf16[7680,128]{1,0:T(8,128)(2,1)S(1)} %bitcast.4, bf16[7680,128]{1,0:T(8,128)(2,1)S(1)} %shard_map.84.coord_ref), custom_call_target="tpu_custom_call" | custom-call | flops 1509949440 | bytes 3932160 | tf_op jit(solution)/shard_map/pallas_call | solution.py:512
  20.2 0.0 copy-start.5
  20.2 0.0 copy-start.2
  20.2 0.0 copy-start.3
  20.2 0.0 copy-start.4
  20.3 0.0 collective-permute-done.3.query_ref
  20.3 2.8 %shard_map.86 = (f32[80,128]{1,0:T(8,128)S(1)}, f32[80,128]{1,0:T(8,128)S(1)}, f32[80,128]{1,0:T(8,128)S(1)}, f32[80,128]{1,0:T(8,128)S(1)}) custom-call(bf16[256,128]{1,0:T(8,128)(2,1)S(1)} %collective-permute-done.3.query_ref, bf16[7680,128]{1,0:T(8,128)(2,1)S(1)} %bitcast.5, bf16[7680,128]{1,0:T(8,128)(2,1)S(1)} %shard_map.84.coord_ref), custom_call_target="tpu_custom_call" | custom-call | flops 1509949440 | bytes 3932160 | tf_op jit(solution)/shard_map/pallas_call | solution.py:512
  23.1 3.2 %collective-permute-start.6 = (f16[160,128]{1,0:T(8,128)(2,1)S(1)}, f16[160,128]{1,0:T(8,128)(2,1)S(1)}, u32[]{:S(2)}, u32[]{:S(2)}) collective-permute-start(f16[160,128]{1,0:T(8,128)(2,1)S(1)} %pad_maximum_fusion.3), channel_id=1, source_target_pairs={{0,3},{1,2},{2,1},{3,0},{4,7},{5,6},{6,5},{7,4},{8,11},{9,10},{10,... | collective-permute-start | bytes 122888 | tf_op jit(solution)/shard_map/ppermute | solution.py:469
  26.4 0.1 collective-permute-start.5
  26.5 1.2 %collective-permute-start.4 = (f16[160,128]{1,0:T(8,128)(2,1)S(1)}, f16[160,128]{1,0:T(8,128)(2,1)S(1)}, u32[]{:S(2)}, u32[]{:S(2)}) collective-permute-start(f16[160,128]{1,0:T(8,128)(2,1)S(1)} %pad_maximum_fusion.1), channel_id=1, source_target_pairs={{0,1},{1,0},{2,3},{3,2},{4,5},{5,4},{6,7},{7,6},{8,9},{9,8},{10,11... | collective-permute-start | bytes 122888 | tf_op jit(solution)/shard_map/ppermute | solution.py:469
  27.7 1.6 %collective-permute-done.6 = f16[160,128]{1,0:T(8,128)(2,1)S(1)} collective-permute-done((f16[160,128]{1,0:T(8,128)(2,1)S(1)}, f16[160,128]{1,0:T(8,128)(2,1)S(1)}, u32[]{:S(2)}, u32[]{:S(2)}) %collective-permute-start.6) | collective-permute-done | bytes 40992 | tf_op jit(solution)/shard_map/ppermute | solution.py:469
  29.3 2.1 %collective-permute-done.5 = f16[160,128]{1,0:T(8,128)(2,1)S(1)} collective-permute-done((f16[160,128]{1,0:T(8,128)(2,1)S(1)}, f16[160,128]{1,0:T(8,128)(2,1)S(1)}, u32[]{:S(2)}, u32[]{:S(2)}) %collective-permute-start.5) | collective-permute-done | bytes 40992 | tf_op jit(solution)/shard_map/ppermute | solution.py:469
  31.4 0.0 collective-permute-done.4
  31.4 0.0 copy-done.5
  31.5 0.3 shard_map.87
  31.8 0.1 collective-permute-start.7
  31.8 1.2 %collective-permute-done.7.theirs_ref = f32[136,128]{1,0:T(8,128)S(1)} collective-permute-done((f32[136,128]{1,0:T(8,128)S(1)}, f32[136,128]{1,0:T(8,128)S(1)}, u32[]{:S(2)}, u32[]{:S(2)}) %collective-permute-start.7) | collective-permute-done | bytes 69664 | tf_op jit(solution)/shard_map/ppermute | solution.py:469
  33.1 0.0 copy-done.2
  33.1 0.0 copy-done.3
  33.1 0.0 copy-done.4
  33.1 0.4 shard_map.88.refs_0_
  33.5 2.1 %collective-permute-start.10 = (f32[2,128]{1,0:T(2,128)S(1)}, f32[2,128]{1,0:T(2,128)S(1)}, u32[]{:S(2)}, u32[]{:S(2)}) collective-permute-start(f32[2,128]{1,0:T(2,128)S(1)} %shard_map.88.refs_0_), channel_id=1, source_target_pairs={{0,3},{1,2},{2,1},{3,0},{4,7},{5,6},{6,5},{7,4},{8,11},{9,10},{10,... | collective-permute-start | bytes 3080 | tf_op jit(solution)/shard_map/ppermute | solution.py:469
  35.5 0.6 %collective-permute-start.8 = (f32[2,128]{1,0:T(2,128)S(1)}, f32[2,128]{1,0:T(2,128)S(1)}, u32[]{:S(2)}, u32[]{:S(2)}) collective-permute-start(f32[2,128]{1,0:T(2,128)S(1)} %shard_map.88.refs_0_), channel_id=1, source_target_pairs={{0,1},{1,0},{2,3},{3,2},{4,5},{5,4},{6,7},{7,6},{8,9},{9,8},{10,11... | collective-permute-start | bytes 3080 | tf_op jit(solution)/shard_map/ppermute | solution.py:469
  36.1 1.8 %collective-permute-start.9 = (f32[2,128]{1,0:T(2,128)S(1)}, f32[2,128]{1,0:T(2,128)S(1)}, u32[]{:S(2)}, u32[]{:S(2)}) collective-permute-start(f32[2,128]{1,0:T(2,128)S(1)} %shard_map.88.refs_0_), channel_id=1, source_target_pairs={{0,2},{1,3},{2,0},{3,1},{4,6},{5,7},{6,4},{7,5},{8,10},{9,11},{10,... | collective-permute-start | bytes 3080 | tf_op jit(solution)/shard_map/ppermute | solution.py:469
  37.9 1.0 %collective-permute-done.10.refs_3_ = f32[2,128]{1,0:T(2,128)S(1)} collective-permute-done((f32[2,128]{1,0:T(2,128)S(1)}, f32[2,128]{1,0:T(2,128)S(1)}, u32[]{:S(2)}, u32[]{:S(2)}) %collective-permute-start.10) | collective-permute-done | bytes 1056 | tf_op jit(solution)/shard_map/ppermute | solution.py:469
  38.9 0.2 collective-permute-done.8.refs_1_
  39.1 1.5 %collective-permute-done.9.refs_2_ = f32[2,128]{1,0:T(2,128)S(1)} collective-permute-done((f32[2,128]{1,0:T(2,128)S(1)}, f32[2,128]{1,0:T(2,128)S(1)}, u32[]{:S(2)}, u32[]{:S(2)}) %collective-permute-start.9) | collective-permute-done | bytes 1056 | tf_op jit(solution)/shard_map/ppermute | solution.py:469
  40.6 0.7 %shard_map.89 = f32[1,2,512]{2,1,0:T(2,128)} custom-call(f32[2,128]{1,0:T(2,128)S(1)} %shard_map.88.refs_0_, f32[2,128]{1,0:T(2,128)S(1)} %collective-permute-done.8.refs_1_, f32[2,128]{1,0:T(2,128)S(1)} %collective-permute-done.9.refs_2_, f32[2,128]{1,0:T(2,128)S(1)} %collective-permute-done.10.refs_3_), custom_call_target="tpu_custom_call" | custom-call | flops 1024 | bytes 8192 | tf_op jit(solution)/shard_map/pallas_call | solution.py:547
  (16 shorter events, 0.2 us)
Async XLA Ops:
  0.7 1.5 %copy-start = (bf16[1,32,240,128]{3,2,1,0:T(8,128)(2,1)S(1)}, bf16[1,32,240,128]{3,2,1,0:T(8,128)(2,1)}, u32[]{:S(2)}) copy-start(bf16[1,32,240,128]{3,2,1,0:T(8,128)(2,1)} %param.8) | copy-start | bytes 5898244
  3.5 13.9 %copy-start.1 = (bf16[1,32,240,128]{3,2,1,0:T(8,128)(2,1)S(1)}, bf16[1,32,240,128]{3,2,1,0:T(8,128)(2,1)}, u32[]{:S(2)}) copy-start(bf16[1,32,240,128]{3,2,1,0:T(8,128)(2,1)} %param.8) | copy-start | bytes 5898244
  3.5 1.8 %collective-permute-start = (bf16[256,128]{1,0:T(8,128)(2,1)S(1)}, bf16[256,128]{1,0:T(8,128)(2,1)S(1)}, u32[]{:S(2)}, u32[]{:S(2)}) collective-permute-start(bf16[256,128]{1,0:T(8,128)(2,1)S(1)} %shard_map.83), channel_id=1, source_target_pairs={{0,4},{1,5},{2,6},{3,7},{4,0},{5,1},{6,2},{7,3},{8,12},{9,13},{10,... | collective-permute-start | bytes 196616 | tf_op jit(solution)/shard_map/ppermute | solution.py:469
  5.3 5.4 %collective-permute-start.1 = (bf16[256,128]{1,0:T(8,128)(2,1)S(1)}, bf16[256,128]{1,0:T(8,128)(2,1)S(1)}, u32[]{:S(2)}, u32[]{:S(2)}) collective-permute-start(bf16[256,128]{1,0:T(8,128)(2,1)S(1)} %add.13), channel_id=1, source_target_pairs={{0,1},{1,0},{2,3},{3,2},{4,5},{5,4},{6,7},{7,6},{8,9},{9,8},{10,11... | collective-permute-start | bytes 196616 | tf_op jit(solution)/shard_map/ppermute | solution.py:381
  10.8 6.6 %collective-permute-start.2 = (bf16[256,128]{1,0:T(8,128)(2,1)S(1)}, bf16[256,128]{1,0:T(8,128)(2,1)S(1)}, u32[]{:S(2)}, u32[]{:S(2)}) collective-permute-start(bf16[256,128]{1,0:T(8,128)(2,1)S(1)} %add.14), channel_id=1, source_target_pairs={{0,2},{1,3},{2,0},{3,1},{4,6},{5,7},{6,4},{7,5},{8,10},{9,11},{10,... | collective-permute-start | bytes 196616 | tf_op jit(solution)/shard_map/ppermute | solution.py:381
  17.4 2.9 %collective-permute-start.3 = (bf16[256,128]{1,0:T(8,128)(2,1)S(1)}, bf16[256,128]{1,0:T(8,128)(2,1)S(1)}, u32[]{:S(2)}, u32[]{:S(2)}) collective-permute-start(bf16[256,128]{1,0:T(8,128)(2,1)S(1)} %add.15.query_ref), channel_id=1, source_target_pairs={{0,4},{1,5},{2,6},{3,7},{4,0},{5,1},{6,2},{7,3},{8,12},{9,13},{10,... | collective-permute-start | bytes 196616 | tf_op jit(solution)/shard_map/ppermute | solution.py:469
  20.2 11.2 %copy-start.5 = (f32[1,128]{1,0:T(1,128)S(1)}, f32[1,128]{1,0:T(1,128)}, u32[]{:S(2)}) copy-start(f32[1,128]{1,0:T(1,128)} %decay_ref.1) | copy-start | bytes 1540
  20.2 12.9 %copy-start.2 = (bf16[128,128]{1,0:T(8,128)(2,1)S(1)}, bf16[128,128]{1,0:T(8,128)(2,1)}, u32[]{:S(2)}) copy-start(bf16[128,128]{1,0:T(8,128)(2,1)} %pw_ref.1) | copy-start | bytes 98308
  20.2 12.9 %copy-start.3 = (f32[3,128]{1,0:T(4,128)S(1)}, f32[3,128]{1,0:T(4,128)}, u32[]{:S(2)}) copy-start(f32[3,128]{1,0:T(4,128)} %dw_ref.1) | copy-start | bytes 4612
  20.2 12.8 %copy-start.4 = (f32[2,128]{1,0:T(2,128)S(1)}, f32[2,128]{1,0:T(2,128)}, u32[]{:S(2)}) copy-start(f32[2,128]{1,0:T(2,128)} %ow_ref.1) | copy-start | bytes 3076
  23.1 6.2 %collective-permute-start.6 = (f16[160,128]{1,0:T(8,128)(2,1)S(1)}, f16[160,128]{1,0:T(8,128)(2,1)S(1)}, u32[]{:S(2)}, u32[]{:S(2)}) collective-permute-start(f16[160,128]{1,0:T(8,128)(2,1)S(1)} %pad_maximum_fusion.3), channel_id=1, source_target_pairs={{0,3},{1,2},{2,1},{3,0},{4,7},{5,6},{6,5},{7,4},{8,11},{9,10},{10,... | collective-permute-start | bytes 122888 | tf_op jit(solution)/shard_map/ppermute | solution.py:469
  26.4 5.0 %collective-permute-start.5 = (f16[160,128]{1,0:T(8,128)(2,1)S(1)}, f16[160,128]{1,0:T(8,128)(2,1)S(1)}, u32[]{:S(2)}, u32[]{:S(2)}) collective-permute-start(f16[160,128]{1,0:T(8,128)(2,1)S(1)} %pad_maximum_fusion.2), channel_id=1, source_target_pairs={{0,2},{1,3},{2,0},{3,1},{4,6},{5,7},{6,4},{7,5},{8,10},{9,11},{10,... | collective-permute-start | bytes 122888 | tf_op jit(solution)/shard_map/ppermute | solution.py:469
  26.5 4.9 %collective-permute-start.4 = (f16[160,128]{1,0:T(8,128)(2,1)S(1)}, f16[160,128]{1,0:T(8,128)(2,1)S(1)}, u32[]{:S(2)}, u32[]{:S(2)}) collective-permute-start(f16[160,128]{1,0:T(8,128)(2,1)S(1)} %pad_maximum_fusion.1), channel_id=1, source_target_pairs={{0,1},{1,0},{2,3},{3,2},{4,5},{5,4},{6,7},{7,6},{8,9},{9,8},{10,11... | collective-permute-start | bytes 122888 | tf_op jit(solution)/shard_map/ppermute | solution.py:469
  31.8 1.3 %collective-permute-start.7 = (f32[136,128]{1,0:T(8,128)S(1)}, f32[136,128]{1,0:T(8,128)S(1)}, u32[]{:S(2)}, u32[]{:S(2)}) collective-permute-start(f32[136,128]{1,0:T(8,128)S(1)} %get-tuple-element.24.mine_ref), channel_id=1, source_target_pairs={{0,4},{1,5},{2,6},{3,7},{4,0},{5,1},{6,2},{7,3},{8,12},{9,13},{10,... | collective-permute-start | bytes 208904 | tf_op jit(solution)/shard_map/ppermute | solution.py:469
  33.5 5.4 %collective-permute-start.10 = (f32[2,128]{1,0:T(2,128)S(1)}, f32[2,128]{1,0:T(2,128)S(1)}, u32[]{:S(2)}, u32[]{:S(2)}) collective-permute-start(f32[2,128]{1,0:T(2,128)S(1)} %shard_map.88.refs_0_), channel_id=1, source_target_pairs={{0,3},{1,2},{2,1},{3,0},{4,7},{5,6},{6,5},{7,4},{8,11},{9,10},{10,... | collective-permute-start | bytes 3080 | tf_op jit(solution)/shard_map/ppermute | solution.py:469
  35.5 3.6 %collective-permute-start.8 = (f32[2,128]{1,0:T(2,128)S(1)}, f32[2,128]{1,0:T(2,128)S(1)}, u32[]{:S(2)}, u32[]{:S(2)}) collective-permute-start(f32[2,128]{1,0:T(2,128)S(1)} %shard_map.88.refs_0_), channel_id=1, source_target_pairs={{0,1},{1,0},{2,3},{3,2},{4,5},{5,4},{6,7},{7,6},{8,9},{9,8},{10,11... | collective-permute-start | bytes 3080 | tf_op jit(solution)/shard_map/ppermute | solution.py:469
  36.1 4.5 %collective-permute-start.9 = (f32[2,128]{1,0:T(2,128)S(1)}, f32[2,128]{1,0:T(2,128)S(1)}, u32[]{:S(2)}, u32[]{:S(2)}) collective-permute-start(f32[2,128]{1,0:T(2,128)S(1)} %shard_map.88.refs_0_), channel_id=1, source_target_pairs={{0,2},{1,3},{2,0},{3,1},{4,6},{5,7},{6,4},{7,5},{8,10},{9,11},{10,... | collective-permute-start | bytes 3080 | tf_op jit(solution)/shard_map/ppermute | solution.py:469

commit v4 on v3

--- a/solution.py
+++ b/solution.py
@@ -236,21 +236,10 @@
     return pieces
 
 
-def by_partner(values, n_space):
-    space = lax.axis_index("space")
-    bit = 1
-    while bit < n_space:
-        turn = (space & bit) != 0
-        values = [jnp.where(turn, values[i ^ bit], values[i]) for i in range(len(values))]
-        bit *= 2
-    return values
-
-
-def half_kernel(n_space, rows_here, height, width, query_ref, map_ref, coord_ref, *out_refs):
+def half_kernel(rows_here, height, width, query_ref, map_ref, coord_ref, out_ref):
     positions, channels = map_ref.shape
     factor = math.log2(math.e) / math.sqrt(channels)
     query = query_ref[...]
-    group = query.shape[0] // n_space
     first_row = (lax.axis_index("space") * rows_here).astype(F32)
     chunk = pick_chunk(positions, 1280)
 
@@ -280,71 +269,96 @@
     total = extra[2:3]
     across = extra[0:1] / total / width
     down = (extra[1:2] / total + first_row) / height
-    rows = [piece for value in (extra[3:4], total, across, down) for piece in split(value)]
-    aux = jnp.zeros((PIECE_ROWS, extra.shape[1]), F32)
-    sub = lax.broadcasted_iota(jnp.int32, aux.shape, 0)
-    for index, values in enumerate(rows):
-        aux = jnp.where(sub == index, values, aux)
-    blocks = []
-    for index in range(n_space):
-        shift = (aux.shape[1] - index * group) % aux.shape[1]
-        block = pltpu.roll(aux, shift, 1) if shift else aux
-        blocks.append(
-            jnp.concatenate([feats[index * group : (index + 1) * group], block[:, :LANES]], axis=0)
-        )
-    for out_ref, block in zip(out_refs, by_partner(blocks, n_space)):
-        out_ref[...] = block
-
-
-def merge(blocks, group):
-    aux = [block[group:] for block in blocks]
-    tops = [b[0:1] + b[1:2] + b[2:3] for b in aux]
-    top = functools.reduce(jnp.maximum, tops)
-    weight = [jnp.exp2(t - top) * (b[3:4] + b[4:5] + b[5:6]) for t, b in zip(tops, aux)]
-    total = sum(weight[1:], weight[0])
-    share = [w / total for w in weight]
-    across = [s * (b[6:7] + b[7:8] + b[8:9]) for s, b in zip(share, aux)]
-    down = [s * (b[9:10] + b[10:11] + b[11:12]) for s, b in zip(share, aux)]
-    across, down = sum(across[1:], across[0]), sum(down[1:], down[0])
-    table = jnp.zeros((8, LANES), F32)
-    sub = lax.broadcasted_iota(jnp.int32, table.shape, 0)
-    for index, value in enumerate(share):
-        table = jnp.where(sub == index, value, table)
-    table = jnp.transpose(table)
-    attended = None
-    for index, block in enumerate(blocks):
-        term = table[:group, index : index + 1] * block[:group]
-        attended = term if attended is None else attended + term
-    return across, down, attended.astype(BF16).astype(F32)
-
-
-def merge_kernel(group, decay_ref, *refs):
-    block_refs, (out_ref, place_ref) = refs[:-2], refs[-2:]
-    blocks = [ref[...] for ref in block_refs]
-    size = group + PIECE_ROWS
-    near = merge([block[:size] for block in blocks], group)
-    far = merge([block[size:] for block in blocks], group)
-    out_ref[:group, :] = near[2]
-    out_ref[group : 2 * group, :] = far[2]
-    out_ref[2 * group :, :] = jnp.broadcast_to(decay_ref[...], (8, LANES))
-    lane = lax.broadcasted_iota(jnp.int32, (1, LANES), 1)
-    for index in range(2):
-        moved = pltpu.roll(jnp.broadcast_to(far[index], (8, LANES)), group, 1)[0:1]
-        place_ref[index : index + 1, :] = jnp.where(lane < group, near[index], moved)
-
-
-def track_kernel(group, dw_ref, pw_ref, ow_ref, place_ref, mine_ref, theirs_ref, out_ref):
+    store_block(out_ref, feats, [extra[3:4], total, across, down])
+
+
+def store_block(out_ref, feats, lines):
+    queries = feats.shape[0]
+    out_ref[:queries, :] = feats
+    rows = [piece for line in lines for piece in split(line)]
+    sub = lax.broadcasted_iota(jnp.int32, (PIECE_ROWS, queries), 0)
+    aux = jnp.zeros((PIECE_ROWS, queries), F32)
+    for index, row in enumerate(rows):
+        aux = jnp.where(sub == index, row, aux)
+    for tile in range(queries // LANES):
+        base = queries + tile * PIECE_ROWS
+        out_ref[base : base + PIECE_ROWS, :] = aux[:, tile * LANES : (tile + 1) * LANES]
+
+
+def merged(bit, own_ref, came_ref):
+    queries = own_ref.shape[0] * LANES // (LANES + PIECE_ROWS)
+    high = (lax.axis_index("space") & bit) != 0
+    own, came = own_ref[...].astype(F32), came_ref[...].astype(F32)
+    pair = [jnp.where(high, came, own), jnp.where(high, own, came)]
+    feats, lines = [], []
+    for tile in range(queries // LANES):
+        base = queries + tile * PIECE_ROWS
+        parts = []
+        for block in pair:
+            aux = block[base : base + PIECE_ROWS]
+            parts.append(
+                [aux[i : i + 1] + aux[i + 1 : i + 2] + aux[i + 2 : i + 3] for i in (0, 3, 6, 9)]
+            )
+        (top_a, total_a, *place_a), (top_b, total_b, *place_b) = parts
+        top = jnp.maximum(top_a, top_b)
+        weight_a, weight_b = jnp.exp2(top_a - top) * total_a, jnp.exp2(top_b - top) * total_b
+        total = weight_a + weight_b
+        share_a, share_b = weight_a / total, weight_b / total
+        places = [share_a * a + share_b * b for a, b in zip(place_a, place_b)]
+        lines.append([top, total, *places])
+        sub = lax.broadcasted_iota(jnp.int32, (8, LANES), 0)
+        table = jnp.transpose(jnp.where(sub == 0, share_a, jnp.where(sub == 1, share_b, 0.0)))
+        window = slice(tile * LANES, (tile + 1) * LANES)
+        feats.append(table[:, 0:1] * pair[0][window] + table[:, 1:2] * pair[1][window])
+    return jnp.concatenate(feats, axis=0), [jnp.concatenate(v, axis=1) for v in zip(*lines)]
+
+
+def my_bit(step, n_space):
+    bits = n_space.bit_length() - 1
+    return jnp.left_shift(1, lax.rem(lax.axis_index("tm") + step, bits))
+
+
+def merge_kernel(n_space, step, own_ref, came_ref, out_ref):
+    store_block(out_ref, *merged(my_bit(step, n_space), own_ref, came_ref))
+
+
+def last_merge_kernel(n_space, step, decay_ref, near_own, near_came, far_own, far_came, *outs):
+    out_ref, place_ref = outs
+    bit = my_bit(step, n_space)
+    base = 0
+    for own_ref, came_ref in ((near_own, near_came), (far_own, far_came)):
+        feats, lines = merged(bit, own_ref, came_ref)
+        window = slice(base, base + feats.shape[0])
+        out_ref[window, :] = feats.astype(BF16)
+        place_ref[0:1, window] = lines[2]
+        place_ref[1:2, window] = lines[3]
+        base += feats.shape[0]
+    sub = lax.broadcasted_iota(jnp.int32, (PIECE_ROWS, LANES), 0)
+    rows = jnp.zeros((PIECE_ROWS, LANES), F32)
+    for index, piece in enumerate(split(decay_ref[...])):
+        rows = jnp.where(sub == index, piece, rows)
+    out_ref[base:, :] = rows.astype(BF16)
+
+
+def track_kernel(dw_ref, pw_ref, ow_ref, place_ref, mine_ref, theirs_ref, out_ref):
     early = lax.axis_index("tm") == 0
-    mine = mine_ref[: 2 * group]
-    theirs = jnp.concatenate([theirs_ref[group : 2 * group], theirs_ref[:group]], axis=0)
+    queries = place_ref.shape[1]
+    half = queries // 2
+    mine, theirs = mine_ref[...].astype(F32), theirs_ref[...].astype(F32)
+
+    def retention(rows):
+        return rows[queries : queries + 1] + rows[queries + 1 : queries + 2] + rows[queries + 2 : queries + 3]
+
+    decay_mine, decay_theirs = retention(mine), retention(theirs)
+    mine = mine[:queries]
+    theirs = jnp.concatenate([theirs[half:queries], theirs[:half]], axis=0)
     attended = [jnp.where(early, mine, theirs), jnp.where(early, theirs, mine)]
-    decay_mine, decay_theirs = mine_ref[2 * group : 2 * group + 1], theirs_ref[2 * group : 2 * group + 1]
     decay = [
         jnp.where(early, decay_mine, decay_theirs),
         jnp.where(early, decay_theirs, decay_mine),
     ]
     taps = dw_ref.shape[0]
-    hidden = []
+    refined = []
     for frame in range(2):
         depth = None
         for tap in range(taps):
@@ -352,29 +366,19 @@
             if 0 <= source < 2:
                 term = dw_ref[tap : tap + 1, :] * attended[source]
                 depth = term if depth is None else depth + term
-        hidden.append(jax.nn.gelu(depth).astype(BF16))
-    hidden = jnp.concatenate(hidden, axis=0)
-    mixed = jnp.dot(hidden, pw_ref[...], preferred_element_type=F32)
-    first = (1.0 - decay[0]) * (attended[0] + mixed[: 2 * group])
-    second = decay[1] * first + (1.0 - decay[1]) * (attended[1] + mixed[2 * group :])
+        hidden = jax.nn.gelu(depth).astype(BF16)
+        mixed = jnp.dot(hidden, pw_ref[...], preferred_element_type=F32)
+        refined.append(attended[frame] + mixed)
+    first = (1.0 - decay[0]) * refined[0]
+    second = decay[1] * first + (1.0 - decay[1]) * refined[1]
     memory = jnp.where(early, first, second)
     delta = lax.dot_general(
         ow_ref[...], memory, NT, preferred_element_type=F32, precision=lax.Precision.HIGHEST
     )
-    out_ref[...] = place_ref[...] + delta
-
-
-def lay_kernel(n_space, group, *refs):
-    out_ref = refs[n_space]
-    lines = by_partner([ref[...] for ref in refs[:n_space]], n_space)
-    early = lax.axis_index("tm") == 0
-    swapped = [pltpu.roll(line, group, 1) for line in lines]
-    halves = [jnp.where(early, a, b) for a, b in zip(lines, swapped)]
-    halves += [jnp.where(early, b, a) for a, b in zip(lines, swapped)]
-    lane = lax.broadcasted_iota(jnp.int32, lines[0].shape, 1)
-    for tile in range(n_space):
-        low, high = halves[2 * tile], pltpu.roll(halves[2 * tile + 1], group, 1)
-        out_ref[0, :, tile * LANES : (tile + 1) * LANES] = jnp.where(lane < group, low, high)
+    line = place_ref[...] + delta
+    low, high = line[:, :half], line[:, half:]
+    out_ref[0, :, :half] = jnp.where(early, low, high)
+    out_ref[0, :, half:] = jnp.where(early, high, low)
 
 
 def swap(value, axis, bit):
@@ -460,12 +464,18 @@
     return jnp.transpose(own, (1, 0, 2)).reshape(1, n_out, queries)
 
 
-def partner(value, flip, bits):
+def core_swap(value):
+    return lax.ppermute(value, "tm", [(0, 1), (1, 0)])
+
+
+def space_swap(value, step):
     n_space = lax.axis_size("space")
+    bits = n_space.bit_length() - 1
     pairs = []
     for tm in range(2):
         for space in range(n_space):
-            pairs.append((tm * n_space + space, (tm ^ flip) * n_space + (space ^ bits)))
+            to = space ^ (1 << (tm + step) % bits)
+            pairs.append((tm * n_space + space, tm * n_space + to))
     return lax.ppermute(value, ("tm", "space"), pairs)
 
 
@@ -476,7 +486,6 @@
     queries = query_frame.shape[0]
     n_space = lax.axis_size("space")
     half = queries // 2
-    group = half // n_space
     height = rows_here * n_space
     positions = rows_here * map_width
     maps = feature_maps.reshape(positions, channels)
@@ -495,7 +504,7 @@
             transcendentals=0,
         )(target, maps)
 
-    arrived = partner(pick(1), 1, 0)
+    arrived = core_swap(pick(1))
     coords = call(
         functools.partial(coord_kernel, map_width),
         jax.ShapeDtypeStruct((positions, LANES), BF16),
@@ -504,61 +513,68 @@
         bytes_accessed=2 * positions * LANES,
         transcendentals=0,
     )(target)
-    mine = all_sum(pick(0) + arrived, "space")
-    theirs = partner(mine, 1, 0)
+    mine = pick(0) + arrived
+    steps = n_space.bit_length() - 1
+    for step in range(steps):
+        mine = mine + space_swap(mine, step)
+    theirs = core_swap(mine)
+
+    block = jax.ShapeDtypeStruct((half + half // LANES * PIECE_ROWS, LANES), F32)
 
     def blocks_of(feats):
-        shape = jax.ShapeDtypeStruct((group + PIECE_ROWS, LANES), F32)
         return call(
-            functools.partial(half_kernel, n_space, rows_here, height, map_width),
-            [shape] * n_space,
+            functools.partial(half_kernel, rows_here, height, map_width),
+            block,
             3,
             flops=3 * queries * positions * channels,
             bytes_accessed=4 * positions * channels,
             transcendentals=half * positions,
         )(feats, maps, coords)
 
-    near, far = blocks_of(mine), blocks_of(theirs)
-    blocks = [jnp.concatenate([a, b], axis=0) for a, b in zip(near, far)]
-    for k in reversed(range(1, n_space)):
-        blocks[k] = partner(blocks[k].astype(jnp.float16), 0, k).astype(F32)
+    def sent(value, step):
+        value = lax.optimization_barrier(value.astype(jnp.float16))
+        return value.astype(F32), space_swap(value, step).astype(F32)
+
+    def merge(pair, step):
+        return call(
+            functools.partial(merge_kernel, n_space, step),
+            block,
+            2,
+            flops=4 * half * channels,
+            bytes_accessed=12 * half * channels,
+            transcendentals=0,
+        )(*pair)
+
+    pairs = [sent(blocks_of(mine), 0), sent(blocks_of(theirs), 0)]
+    for step in range(1, steps):
+        pairs = [sent(merge(pair, step - 1), step) for pair in pairs]
 
     n_out = out_weight.shape[0]
     attended, place = call(
-        functools.partial(merge_kernel, group),
+        functools.partial(last_merge_kernel, n_space, steps - 1),
         [
-            jax.ShapeDtypeStruct((2 * group + 8, LANES), F32),
-            jax.ShapeDtypeStruct((n_out, LANES), F32),
+            jax.ShapeDtypeStruct((queries + PIECE_ROWS, LANES), BF16),
+            jax.ShapeDtypeStruct((n_out, queries), F32),
         ],
-        1 + n_space,
-        flops=4 * n_space * group * channels,
-        bytes_accessed=8 * n_space * group * channels,
+        5,
+        flops=4 * queries * channels,
+        bytes_accessed=12 * queries * channels,
         transcendentals=0,
-    )(ema_decay, *blocks)
-    line = call(
-        functools.partial(track_kernel, group),
-        jax.ShapeDtypeStruct((n_out, LANES), F32),
+    )(ema_decay, *pairs[0], *pairs[1])
+    return call(
+        track_kernel,
+        jax.ShapeDtypeStruct((1, n_out, queries), F32),
         6,
-        flops=16 * group * channels * channels,
-        bytes_accessed=16 * group * channels,
-        transcendentals=4 * group * channels,
-    )(dw_kernel, pw_weight, out_weight, place, attended, partner(attended, 1, 0))
-    lines = [line] + [partner(line, 0, k) for k in range(1, n_space)]
-    return call(
-        functools.partial(lay_kernel, n_space, group),
-        jax.ShapeDtypeStruct((1, n_out, queries), F32),
-        n_space,
-        flops=n_out * queries,
-        bytes_accessed=8 * n_out * queries,
-        transcendentals=0,
-    )(*lines)
+        flops=8 * queries * channels * channels,
+        bytes_accessed=8 * queries * channels,
+        transcendentals=2 * queries * channels,
+    )(dw_kernel, pw_weight, out_weight, place, attended, core_swap(attended))
 
 
 def local(feature_maps, query_frame, *rest):
     n_tm, n_space = lax.axis_size("tm"), lax.axis_size("space")
-    group = query_frame.shape[0] // (n_tm * n_space)
-    paired = n_tm == 2 and n_space & (n_space - 1) == 0 and n_space <= 8
-    if paired and 2 * group == LANES:
+    paired = n_tm == 2 and n_space > 1 and n_space & (n_space - 1) == 0
+    if paired and query_frame.shape[0] % (2 * LANES) == 0:
         return local_pair(feature_maps, query_frame, *rest)
     return local_general(feature_maps, query_frame, *rest)
 

time: 41.5 us -> 40.6 us (0.978)
  starting transfers between devices: 15.1 us -> 12.5 us
  waiting for transfers between devices: 12.9 us -> 13.8 us
  Pallas kernels: 10.6 us -> 11.3 us
    ppermute x11 -> x9, starting transfers between devices: 15.1 us -> 12.5 us  [the longest x6 11.9 us: space_swap(): return lax.ppermute(value, ('tm', 'space'), pairs)]
    ppermute x11 -> x9, waiting for transfers between devices: 12.9 us -> 13.8 us  [the longest x6 12.5 us: space_swap(): return lax.ppermute(value, ('tm', 'space'), pairs)]
    pallas_call x5 -> x6, Pallas kernels: 6.92 us -> 7.64 us  [the longest x2 5.39 us: blocks_of(): call(functools.partial(half_kernel, rows_here, height, map_width), block,...]
  transfers between devices with their start and end apart: 11 -> 9, of which waited for: 8 -> 7; matrix products, arithmetic and copies ran while one was open for 0% -> 0% of each run, Pallas kernels for 13% -> 21%
where the time goes in v4:
time: 40.6 us; the launch traced here: 40.4 us
  waiting for transfers between devices  13.8 us (34%)
  starting transfers between devices  12.5 us (31%)
  Pallas kernels  11.3 us (28%)
  local copies, waits for them, and re-layouts  1.58 us (4%)
  other arithmetic  0.93 us (2%)
    ppermute x6, waiting for transfers between devices, space_swap(): return lax.ppermute(value, ('tm', 'space'), pairs)  12.5 us
    ppermute x6, starting transfers between devices, space_swap(): return lax.ppermute(value, ('tm', 'space'), pairs)  11.9 us
    pallas_call x2, Pallas kernels, blocks_of(): call(functools.partial(half_kernel, rows_here, height, map_width), block,...  5.39 us
    pallas_call x2, Pallas kernels, pick(): call(functools.partial(pick_kernel, core_flip), jax.ShapeDtypeStruct((hal...  2.49 us
    unnamed x12, local copies, waits for them, and re-layouts  1.58 us
    ppermute x3, waiting for transfers between devices, core_swap(): return lax.ppermute(value, 'tm', [(0, 1), (1, 0)])  1.35 us
    pallas_call x1, Pallas kernels, local_pair(): call(track_kernel, jax.ShapeDtypeStruct((1, n_out, queries), F32), 6, flo...  1.29 us
    pallas_call x1, Pallas kernels, local_pair(): call(functools.partial(coord_kernel, map_width), jax.ShapeDtypeStruct((po...  1.19 us
  transfers between devices with their start and end apart: 9, of which 7 were waited for; matrix products, arithmetic and copies ran while one was open for 0% of the time, Pallas kernels for 21%

profile of v4, /device:TPU:0, one launch (start us, length us, event | category | flops | bytes accessed | tf_op | source)
XLA Modules:
  0.0 40.4 jit_solution(10259654695357272666)
XLA Ops:
  0.0 0.7 %add_select_fusion = s32[512]{0:T(512)S(1)} fusion(s32[512]{0:T(512)} %param.11, s32[512]{0:T(512)} %param.10, s32[512]{0:T(512)} %param.9, s32[]{:T(128)S(6)} %mul.9, s32[]{:T(128)S(6)} %axis_index.23), kind=kLoop, calls=%fused_computation | loop fusion | flops 4608 | bytes 8200 | tf_op jit(solution)/shard_map/jit(_where)/select_n | solution.py:495
  0.7 0.0 copy-start
  0.7 1.5 %copy-done = bf16[1,32,240,128]{3,2,1,0:T(8,128)(2,1)S(1)} copy-done((bf16[1,32,240,128]{3,2,1,0:T(8,128)(2,1)S(1)}, bf16[1,32,240,128]{3,2,1,0:T(8,128)(2,1)}, u32[]{:S(2)}) %copy-start) | copy-done | bytes 1966104
  2.3 1.2 %shard_map.83 = bf16[256,128]{1,0:T(8,128)(2,1)S(1)} custom-call(s32[1,512]{1,0:T(1,128)S(1)} %bitcast.6, bf16[7680,128]{1,0:T(8,128)(2,1)S(1)} %bitcast.2), custom_call_target="tpu_custom_call" | custom-call | flops 503316480 | bytes 1966080 | tf_op jit(solution)/shard_map/pallas_call | solution.py:498
  3.5 0.0 copy-start.1
  3.5 0.5 %collective-permute-start = (bf16[256,128]{1,0:T(8,128)(2,1)S(1)}, bf16[256,128]{1,0:T(8,128)(2,1)S(1)}, u32[]{:S(2)}, u32[]{:S(2)}) collective-permute-start(bf16[256,128]{1,0:T(8,128)(2,1)S(1)} %shard_map.83), channel_id=1, source_target_pairs={{0,4},{4,0},{1,5},{5,1},{2,6},{6,2},{3,7},{7,3},{8,12},{12,8},{9,1... | collective-permute-start | bytes 196616 | tf_op jit(solution)/shard_map/ppermute | solution.py:468
  4.0 1.2 %shard_map.82 = bf16[256,128]{1,0:T(8,128)(2,1)S(1)} custom-call(s32[1,512]{1,0:T(1,128)S(1)} %bitcast.7, bf16[7680,128]{1,0:T(8,128)(2,1)S(1)} %bitcast.3), custom_call_target="tpu_custom_call" | custom-call | flops 503316480 | bytes 1966080 | tf_op jit(solution)/shard_map/pallas_call | solution.py:498
  5.3 0.0 collective-permute-done
  5.3 2.6 %collective-permute-start.1 = (bf16[256,128]{1,0:T(8,128)(2,1)S(1)}, bf16[256,128]{1,0:T(8,128)(2,1)S(1)}, u32[]{:S(2)}, u32[]{:S(2)}) collective-permute-start(bf16[256,128]{1,0:T(8,128)(2,1)S(1)} %add.13), channel_id=1, source_target_pairs={{0,1},{1,0},{2,3},{3,2},{4,6},{5,7},{6,4},{7,5},{8,9},{9,8},{10,11... | collective-permute-start | bytes 196616 | tf_op jit(solution)/shard_map/ppermute | solution.py:479
  8.0 2.2 %collective-permute-done.1 = bf16[256,128]{1,0:T(8,128)(2,1)S(1)} collective-permute-done((bf16[256,128]{1,0:T(8,128)(2,1)S(1)}, bf16[256,128]{1,0:T(8,128)(2,1)S(1)}, u32[]{:S(2)}, u32[]{:S(2)}) %collective-permute-start.1) | collective-permute-done | bytes 65568 | tf_op jit(solution)/shard_map/ppermute | solution.py:479
  10.3 3.2 %collective-permute-start.2 = (bf16[256,128]{1,0:T(8,128)(2,1)S(1)}, bf16[256,128]{1,0:T(8,128)(2,1)S(1)}, u32[]{:S(2)}, u32[]{:S(2)}) collective-permute-start(bf16[256,128]{1,0:T(8,128)(2,1)S(1)} %add.14), channel_id=1, source_target_pairs={{0,2},{1,3},{2,0},{3,1},{4,5},{5,4},{6,7},{7,6},{8,10},{9,11},{10,... | collective-permute-start | bytes 196616 | tf_op jit(solution)/shard_map/ppermute | solution.py:479
  13.5 1.2 %shard_map.84.coord_ref = bf16[7680,128]{1,0:T(8,128)(2,1)S(1)} custom-call(s32[1,512]{1,0:T(1,128)S(1)} %bitcast.8), custom_call_target="tpu_custom_call" | custom-call | flops 7864320 | bytes 1966080 | tf_op jit(solution)/shard_map/pallas_call | solution.py:508
  14.7 1.1 %collective-permute-done.2 = bf16[256,128]{1,0:T(8,128)(2,1)S(1)} collective-permute-done((bf16[256,128]{1,0:T(8,128)(2,1)S(1)}, bf16[256,128]{1,0:T(8,128)(2,1)S(1)}, u32[]{:S(2)}, u32[]{:S(2)}) %collective-permute-start.2) | collective-permute-done | bytes 65568 | tf_op jit(solution)/shard_map/ppermute | solution.py:479
  15.7 0.1 collective-permute-start.5
  15.8 0.0 copy-done.1
  15.8 2.7 %shard_map.85 = f32[288,128]{1,0:T(8,128)S(1)} custom-call(bf16[256,128]{1,0:T(8,128)(2,1)S(1)} %add.15.query_ref, bf16[7680,128]{1,0:T(8,128)(2,1)S(1)} %bitcast.4, bf16[7680,128]{1,0:T(8,128)(2,1)S(1)} %shard_map.84.coord_ref), custom_call_target="tpu_custom_call" | custom-call | flops 1509949440 | bytes 3932160 | tf_op jit(solution)/shard_map/pallas_call | solution.py:525
  18.6 2.4 %collective-permute-start.3 = (f16[288,128]{1,0:T(8,128)(2,1)S(1)}, f16[288,128]{1,0:T(8,128)(2,1)S(1)}, u32[]{:S(2)}, u32[]{:S(2)}) collective-permute-start(f16[288,128]{1,0:T(8,128)(2,1)S(1)} %convert_element_type.36), channel_id=1, source_target_pairs={{0,1},{1,0},{2,3},{3,2},{4,6},{5,7},{6,4},{7,5},{8,9},{9,8},{10,11... | collective-permute-start | bytes 221192 | tf_op jit(solution)/shard_map/ppermute | solution.py:479
  21.0 0.0 collective-permute-done.5.query_ref
  21.0 2.7 %shard_map.87 = f32[288,128]{1,0:T(8,128)S(1)} custom-call(bf16[256,128]{1,0:T(8,128)(2,1)S(1)} %collective-permute-done.5.query_ref, bf16[7680,128]{1,0:T(8,128)(2,1)S(1)} %bitcast.5, bf16[7680,128]{1,0:T(8,128)(2,1)S(1)} %shard_map.84.coord_ref), custom_call_target="tpu_custom_call" | custom-call | flops 1509949440 | bytes 3932160 | tf_op jit(solution)/shard_map/pallas_call | solution.py:525
  23.7 0.0 copy-start.5
  23.7 0.0 copy-start.2
  23.7 0.0 copy-start.3
  23.7 0.0 copy-start.4
  23.7 0.1 collective-permute-start.6
  23.8 0.2 collective-permute-done.3
  24.1 0.3 shard_map.86
  24.4 3.8 %collective-permute-done.6 = f16[288,128]{1,0:T(8,128)(2,1)S(1)} collective-permute-done((f16[288,128]{1,0:T(8,128)(2,1)S(1)}, f16[288,128]{1,0:T(8,128)(2,1)S(1)}, u32[]{:S(2)}, u32[]{:S(2)}) %collective-permute-start.6) | collective-permute-done | bytes 73760 | tf_op jit(solution)/shard_map/ppermute | solution.py:479
  28.2 3.5 %collective-permute-start.4 = (f16[288,128]{1,0:T(8,128)(2,1)S(1)}, f16[288,128]{1,0:T(8,128)(2,1)S(1)}, u32[]{:S(2)}, u32[]{:S(2)}) collective-permute-start(f16[288,128]{1,0:T(8,128)(2,1)S(1)} %convert_element_type.39), channel_id=1, source_target_pairs={{0,2},{1,3},{2,0},{3,1},{4,5},{5,4},{6,7},{7,6},{8,10},{9,11},{10,... | collective-permute-start | bytes 221192 | tf_op jit(solution)/shard_map/ppermute | solution.py:479
  31.6 0.2 shard_map.88
  31.9 0.1 collective-permute-start.7
  32.0 2.4 %collective-permute-done.4 = f16[288,128]{1,0:T(8,128)(2,1)S(1)} collective-permute-done((f16[288,128]{1,0:T(8,128)(2,1)S(1)}, f16[288,128]{1,0:T(8,128)(2,1)S(1)}, u32[]{:S(2)}, u32[]{:S(2)}) %collective-permute-start.4) | collective-permute-done | bytes 73760 | tf_op jit(solution)/shard_map/ppermute | solution.py:479
  34.4 2.8 %collective-permute-done.7 = f16[288,128]{1,0:T(8,128)(2,1)S(1)} collective-permute-done((f16[288,128]{1,0:T(8,128)(2,1)S(1)}, f16[288,128]{1,0:T(8,128)(2,1)S(1)}, u32[]{:S(2)}, u32[]{:S(2)}) %collective-permute-start.7) | collective-permute-done | bytes 73760 | tf_op jit(solution)/shard_map/ppermute | solution.py:479
  37.2 0.0 copy-done.5
  37.2 0.5 %shard_map.89 = (bf16[528,128]{1,0:T(8,128)(2,1)S(1)}, f32[2,512]{1,0:T(2,128)S(1)}) custom-call(f32[1,128]{1,0:T(1,128)S(1)} %copy-done.5, f32[288,128]{1,0:T(8,128)S(1)} %convert_element_type.40.near_own, f32[288,128]{1,0:T(8,128)S(1)} %convert_element_type.41.near_came, f32[288,128]{1,0:T(8,128)S(1)} %convert_element_type.46.far_own, ...), custom_call_target="tpu_custom_call" | custom-call | flops 262144 | bytes 786432 | tf_op jit(solution)/shard_map/pallas_call | solution.py:553
  37.7 0.1 collective-permute-start.8
  37.8 1.3 %collective-permute-done.8.theirs_ref = bf16[528,128]{1,0:T(8,128)(2,1)S(1)} collective-permute-done((bf16[528,128]{1,0:T(8,128)(2,1)S(1)}, bf16[528,128]{1,0:T(8,128)(2,1)S(1)}, u32[]{:S(2)}, u32[]{:S(2)}) %collective-permute-start.8) | collective-permute-done | bytes 135200 | tf_op jit(solution)/shard_map/ppermute | solution.py:468
  39.1 0.0 copy-done.2
  39.1 0.0 copy-done.3
  39.1 0.0 copy-done.4
  39.1 1.3 %shard_map.90 = f32[1,2,512]{2,1,0:T(2,128)} custom-call(f32[3,128]{1,0:T(4,128)S(1)} %copy-done.3, bf16[128,128]{1,0:T(8,128)(2,1)S(1)} %copy-done.2, f32[2,128]{1,0:T(2,128)S(1)} %copy-done.4, f32[2,512]{1,0:T(2,128)S(1)} %get-tuple-element.7.place_ref, bf16[528,128]{1,0:T(8,128)(2,1)S(1)} %get-tuple-element.8.mine_ref, ...), custom_call_target="tpu_custom_call" | custom-call | flops 67108864 | bytes 524288 | tf_op jit(solution)/shard_map/pallas_call | solution.py:564
  (15 shorter events, 0.2 us)
Async XLA Ops:
  0.7 1.5 %copy-start = (bf16[1,32,240,128]{3,2,1,0:T(8,128)(2,1)S(1)}, bf16[1,32,240,128]{3,2,1,0:T(8,128)(2,1)}, u32[]{:S(2)}) copy-start(bf16[1,32,240,128]{3,2,1,0:T(8,128)(2,1)} %param.8) | copy-start | bytes 5898244
  3.5 12.3 %copy-start.1 = (bf16[1,32,240,128]{3,2,1,0:T(8,128)(2,1)S(1)}, bf16[1,32,240,128]{3,2,1,0:T(8,128)(2,1)}, u32[]{:S(2)}) copy-start(bf16[1,32,240,128]{3,2,1,0:T(8,128)(2,1)} %param.8) | copy-start | bytes 5898244
  3.5 1.8 %collective-permute-start = (bf16[256,128]{1,0:T(8,128)(2,1)S(1)}, bf16[256,128]{1,0:T(8,128)(2,1)S(1)}, u32[]{:S(2)}, u32[]{:S(2)}) collective-permute-start(bf16[256,128]{1,0:T(8,128)(2,1)S(1)} %shard_map.83), channel_id=1, source_target_pairs={{0,4},{4,0},{1,5},{5,1},{2,6},{6,2},{3,7},{7,3},{8,12},{12,8},{9,1... | collective-permute-start | bytes 196616 | tf_op jit(solution)/shard_map/ppermute | solution.py:468
  5.3 4.9 %collective-permute-start.1 = (bf16[256,128]{1,0:T(8,128)(2,1)S(1)}, bf16[256,128]{1,0:T(8,128)(2,1)S(1)}, u32[]{:S(2)}, u32[]{:S(2)}) collective-permute-start(bf16[256,128]{1,0:T(8,128)(2,1)S(1)} %add.13), channel_id=1, source_target_pairs={{0,1},{1,0},{2,3},{3,2},{4,6},{5,7},{6,4},{7,5},{8,9},{9,8},{10,11... | collective-permute-start | bytes 196616 | tf_op jit(solution)/shard_map/ppermute | solution.py:479
  10.3 5.5 %collective-permute-start.2 = (bf16[256,128]{1,0:T(8,128)(2,1)S(1)}, bf16[256,128]{1,0:T(8,128)(2,1)S(1)}, u32[]{:S(2)}, u32[]{:S(2)}) collective-permute-start(bf16[256,128]{1,0:T(8,128)(2,1)S(1)} %add.14), channel_id=1, source_target_pairs={{0,2},{1,3},{2,0},{3,1},{4,5},{5,4},{6,7},{7,6},{8,10},{9,11},{10,... | collective-permute-start | bytes 196616 | tf_op jit(solution)/shard_map/ppermute | solution.py:479
  15.7 5.2 %collective-permute-start.5 = (bf16[256,128]{1,0:T(8,128)(2,1)S(1)}, bf16[256,128]{1,0:T(8,128)(2,1)S(1)}, u32[]{:S(2)}, u32[]{:S(2)}) collective-permute-start(bf16[256,128]{1,0:T(8,128)(2,1)S(1)} %add.15.query_ref), channel_id=1, source_target_pairs={{0,4},{4,0},{1,5},{5,1},{2,6},{6,2},{3,7},{7,3},{8,12},{12,8},{9,1... | collective-permute-start | bytes 196616 | tf_op jit(solution)/shard_map/ppermute | solution.py:468
  18.6 5.5 %collective-permute-start.3 = (f16[288,128]{1,0:T(8,128)(2,1)S(1)}, f16[288,128]{1,0:T(8,128)(2,1)S(1)}, u32[]{:S(2)}, u32[]{:S(2)}) collective-permute-start(f16[288,128]{1,0:T(8,128)(2,1)S(1)} %convert_element_type.36), channel_id=1, source_target_pairs={{0,1},{1,0},{2,3},{3,2},{4,6},{5,7},{6,4},{7,5},{8,9},{9,8},{10,11... | collective-permute-start | bytes 221192 | tf_op jit(solution)/shard_map/ppermute | solution.py:479
  23.7 13.6 %copy-start.5 = (f32[1,128]{1,0:T(1,128)S(1)}, f32[1,128]{1,0:T(1,128)}, u32[]{:S(2)}) copy-start(f32[1,128]{1,0:T(1,128)} %decay_ref.1) | copy-start | bytes 1540
  23.7 15.5 %copy-start.2 = (bf16[128,128]{1,0:T(8,128)(2,1)S(1)}, bf16[128,128]{1,0:T(8,128)(2,1)}, u32[]{:S(2)}) copy-start(bf16[128,128]{1,0:T(8,128)(2,1)} %pw_ref.1) | copy-start | bytes 98308
  23.7 15.4 %copy-start.3 = (f32[3,128]{1,0:T(4,128)S(1)}, f32[3,128]{1,0:T(4,128)}, u32[]{:S(2)}) copy-start(f32[3,128]{1,0:T(4,128)} %dw_ref.1) | copy-start | bytes 4612
  23.7 15.4 %copy-start.4 = (f32[2,128]{1,0:T(2,128)S(1)}, f32[2,128]{1,0:T(2,128)}, u32[]{:S(2)}) copy-start(f32[2,128]{1,0:T(2,128)} %ow_ref.1) | copy-start | bytes 3076
  23.7 4.4 %collective-permute-start.6 = (f16[288,128]{1,0:T(8,128)(2,1)S(1)}, f16[288,128]{1,0:T(8,128)(2,1)S(1)}, u32[]{:S(2)}, u32[]{:S(2)}) collective-permute-start(f16[288,128]{1,0:T(8,128)(2,1)S(1)} %convert_element_type.42), channel_id=1, source_target_pairs={{0,1},{1,0},{2,3},{3,2},{4,6},{5,7},{6,4},{7,5},{8,9},{9,8},{10,11... | collective-permute-start | bytes 221192 | tf_op jit(solution)/shard_map/ppermute | solution.py:479
  28.2 6.2 %collective-permute-start.4 = (f16[288,128]{1,0:T(8,128)(2,1)S(1)}, f16[288,128]{1,0:T(8,128)(2,1)S(1)}, u32[]{:S(2)}, u32[]{:S(2)}) collective-permute-start(f16[288,128]{1,0:T(8,128)(2,1)S(1)} %convert_element_type.39), channel_id=1, source_target_pairs={{0,2},{1,3},{2,0},{3,1},{4,5},{5,4},{6,7},{7,6},{8,10},{9,11},{10,... | collective-permute-start | bytes 221192 | tf_op jit(solution)/shard_map/ppermute | solution.py:479
  31.9 5.3 %collective-permute-start.7 = (f16[288,128]{1,0:T(8,128)(2,1)S(1)}, f16[288,128]{1,0:T(8,128)(2,1)S(1)}, u32[]{:S(2)}, u32[]{:S(2)}) collective-permute-start(f16[288,128]{1,0:T(8,128)(2,1)S(1)} %convert_element_type.45), channel_id=1, source_target_pairs={{0,2},{1,3},{2,0},{3,1},{4,5},{5,4},{6,7},{7,6},{8,10},{9,11},{10,... | collective-permute-start | bytes 221192 | tf_op jit(solution)/shard_map/ppermute | solution.py:479
  37.7 1.4 %collective-permute-start.8 = (bf16[528,128]{1,0:T(8,128)(2,1)S(1)}, bf16[528,128]{1,0:T(8,128)(2,1)S(1)}, u32[]{:S(2)}, u32[]{:S(2)}) collective-permute-start(bf16[528,128]{1,0:T(8,128)(2,1)S(1)} %get-tuple-element.8.mine_ref), channel_id=1, source_target_pairs={{0,4},{4,0},{1,5},{5,1},{2,6},{6,2},{3,7},{7,3},{8,12},{12,8},{9,1... | collective-permute-start | bytes 405512 | tf_op jit(solution)/shard_map/ppermute | solution.py:468

commit v5 on v4

--- a/solution.py
+++ b/solution.py
@@ -14,6 +14,7 @@
 AUX_ROWS = 8
 PIECE_ROWS = 16
 VMEM_LIMIT = 40 * 1024 * 1024
+FIRST_LIMIT = 60 * 1024 * 1024
 NT = (((1,), (1,)), ((), ()))
 
 
@@ -198,18 +199,59 @@
     return jnp.dot(hot, map_ref[base : base + chunk, :], preferred_element_type=F32)
 
 
-def pick_kernel(core_flip, target_ref, map_ref, out_ref):
-    half = target_ref.shape[1] // 2
-    positions = map_ref.shape[0]
-    chunk = pick_chunk(positions, 1536)
-    second = lax.axis_index("tm") != core_flip
-    target = jnp.where(second, target_ref[:, half:], target_ref[:, :half])
-    target = jnp.transpose(jnp.broadcast_to(target, (LANES, half)))
+def pick_both_kernel(
+    rows_here,
+    map_width,
+    frame_hbm,
+    row_hbm,
+    col_hbm,
+    map_hbm,
+    send_ref,
+    keep_ref,
+    index_ref,
+    map_ref,
+    index_sem,
+    map_sem,
+):
+    index_copies = [
+        pltpu.make_async_copy(ref, index_ref.at[i], index_sem.at[i])
+        for i, ref in enumerate((frame_hbm, row_hbm, col_hbm))
+    ]
+    chunk = map_ref.shape[0] // map_sem.shape[0]
+    map_copies = [
+        pltpu.make_async_copy(
+            map_hbm.at[pl.ds(i * chunk, chunk)], map_ref.at[pl.ds(i * chunk, chunk)], map_sem.at[i]
+        )
+        for i in range(map_sem.shape[0])
+    ]
+    for copy in index_copies + map_copies:
+        copy.start()
+    for copy in index_copies:
+        copy.wait()
+    tm = lax.axis_index("tm")
+    row = index_ref[1] - lax.axis_index("space") * rows_here
+    here = (index_ref[0] == tm) & (row >= 0) & (row < rows_here)
+    target = jnp.where(here, row * map_width + index_ref[2], -1)
+    queries = target.shape[1]
+    target = jnp.transpose(jnp.broadcast_to(target, (LANES, queries)))
+    tile = jnp.right_shift(target, 7).astype(F32).astype(BF16)
+    lane = lax.broadcasted_iota(jnp.int32, (queries, LANES), 1)
+    hot_lane = jnp.where(lane == jnp.bitwise_and(target, LANES - 1), 1.0, 0.0).astype(BF16)
     picked = None
-    for base in range(0, positions, chunk):
-        term = hot_rows(target, map_ref, base, chunk)
+    for index, copy in enumerate(map_copies):
+        tiles = range(index * chunk // LANES, (index + 1) * chunk // LANES)
+        hot = jnp.concatenate(
+            [jnp.where(tile == jnp.asarray(j, BF16), hot_lane, jnp.zeros_like(hot_lane)) for j in tiles],
+            axis=1,
+        )
+        copy.wait()
+        window = slice(index * chunk, (index + 1) * chunk)
+        term = jnp.dot(hot, map_ref[window, :], preferred_element_type=F32)
         picked = term if picked is None else picked + term
-    out_ref[...] = picked.astype(BF16)
+    half = queries // 2
+    first, second = picked[:half], picked[half:]
+    send_ref[...] = jnp.where(tm == 0, second, first).astype(BF16)
+    keep_ref[...] = jnp.where(tm == 0, first, second).astype(BF16)
 
 
 def coord_kernel(map_width, after_ref, out_ref):
@@ -490,21 +532,28 @@
     positions = rows_here * map_width
     maps = feature_maps.reshape(positions, channels)
 
-    row = query_row - lax.axis_index("space") * rows_here
-    here = (query_frame == lax.axis_index("tm")) & (row >= 0) & (row < rows_here)
-    target = jnp.where(here, row * map_width + query_col, -1)[None]
-
-    def pick(core_flip):
-        return call(
-            functools.partial(pick_kernel, core_flip),
-            jax.ShapeDtypeStruct((half, channels), BF16),
-            2,
-            flops=queries * positions * channels,
+    half_shape = jax.ShapeDtypeStruct((half, channels), BF16)
+    vmem, hbm = pl.BlockSpec(memory_space=pltpu.VMEM), pl.BlockSpec(memory_space=pl.ANY)
+    n_chunks = positions // pick_chunk(positions, 1536)
+    send, keep = pl.pallas_call(
+        functools.partial(pick_both_kernel, rows_here, map_width),
+        out_shape=[half_shape] * 2,
+        in_specs=[hbm] * 4,
+        out_specs=[vmem] * 2,
+        scratch_shapes=[
+            pltpu.VMEM((3, 1, queries), jnp.int32),
+            pltpu.VMEM((positions, channels), BF16),
+            pltpu.SemaphoreType.DMA((3,)),
+            pltpu.SemaphoreType.DMA((n_chunks,)),
+        ],
+        compiler_params=pltpu.CompilerParams(vmem_limit_bytes=FIRST_LIMIT),
+        cost_estimate=pl.CostEstimate(
+            flops=2 * queries * positions * channels,
             bytes_accessed=2 * positions * channels,
             transcendentals=0,
-        )(target, maps)
-
-    arrived = core_swap(pick(1))
+        ),
+    )(query_frame[None], query_row[None], query_col[None], maps)
+    arrived = core_swap(send)
     coords = call(
         functools.partial(coord_kernel, map_width),
         jax.ShapeDtypeStruct((positions, LANES), BF16),
@@ -512,8 +561,8 @@
         flops=8 * positions * LANES,
         bytes_accessed=2 * positions * LANES,
         transcendentals=0,
-    )(target)
-    mine = pick(0) + arrived
+    )(keep)
+    mine = keep + arrived
     steps = n_space.bit_length() - 1
     for step in range(steps):
         mine = mine + space_swap(mine, step)
@@ -540,8 +589,8 @@
             functools.partial(merge_kernel, n_space, step),
             block,
             2,
-            flops=4 * half * channels,
-            bytes_accessed=12 * half * channels,
+            flops=0,
+            bytes_accessed=0,
             transcendentals=0,
         )(*pair)
 

time: 40.6 us -> 43 us (1.059)
  Pallas kernels: 11.3 us -> 15.6 us
  waiting for transfers between devices: 13.8 us -> 12.8 us
  local copies, waits for them, and re-layouts: 1.58 us -> 0.87 us
    pallas_call x4 -> x3, Pallas kernels: 2.98 us -> 7.25 us  [the longest x1 6.75 us: local_pair(): pl.pallas_call(functools.partial(pick_both_kernel, rows_here, map_width),...]
    ppermute x6, waiting for transfers between devices: 12.5 us -> 10.3 us  [space_swap(): return lax.ppermute(value, ('tm', 'space'), pairs)]
    ppermute x3, waiting for transfers between devices: 1.35 us -> 2.46 us  [core_swap(): return lax.ppermute(value, 'tm', [(0, 1), (1, 0)])]
    add x1, other arithmetic: 0.02 us -> 0.86 us  [local_pair(): mine = keep + arrived]
    select_n x1 -> x0, other arithmetic: 0.72 us -> none  [local_pair(): target = jnp.where(here, row * map_width + query_col, -1)[None]]
    unnamed x12, local copies, waits for them, and re-layouts: 1.58 us -> 0.87 us
  transfers between devices with their start and end apart: 9 -> 9, of which waited for: 7 -> 7; matrix products, arithmetic and copies ran while one was open for 0% -> 0% of each run, Pallas kernels for 21% -> 17%
where the time goes in v5:
time: 43 us; the launch traced here: 42.8 us
  Pallas kernels  15.6 us (36%)
  waiting for transfers between devices  12.8 us (30%)
  starting transfers between devices  12.3 us (29%)
  other arithmetic  1.05 us (2%)
  local copies, waits for them, and re-layouts  0.87 us (2%)
    ppermute x6, starting transfers between devices, space_swap(): return lax.ppermute(value, ('tm', 'space'), pairs)  11.7 us
    ppermute x6, waiting for transfers between devices, space_swap(): return lax.ppermute(value, ('tm', 'space'), pairs)  10.3 us
    pallas_call x1, Pallas kernels, local_pair(): pl.pallas_call(functools.partial(pick_both_kernel, rows_here, map_width),...  6.75 us
    pallas_call x2, Pallas kernels, blocks_of(): call(functools.partial(half_kernel, rows_here, height, map_width), block,...  5.39 us
    ppermute x3, waiting for transfers between devices, core_swap(): return lax.ppermute(value, 'tm', [(0, 1), (1, 0)])  2.46 us
    pallas_call x1, Pallas kernels, local_pair(): call(track_kernel, jax.ShapeDtypeStruct((1, n_out, queries), F32), 6, flo...  1.29 us
    pallas_call x1, Pallas kernels, local_pair(): call(functools.partial(coord_kernel, map_width), jax.ShapeDtypeStruct((po...  1.19 us
    unnamed x12, local copies, waits for them, and re-layouts  0.87 us
  transfers between devices with their start and end apart: 9, of which 7 were waited for; matrix products, arithmetic and copies ran while one was open for 0% of the time, Pallas kernels for 17%

profile of v5, /device:TPU:0, one launch (start us, length us, event | category | flops | bytes accessed | tf_op | source)
XLA Modules:
  0.0 42.8 jit_solution(7352057604303822789)
XLA Ops:
  0.0 0.0 copy-start.5
  0.0 6.8 %shard_map.82 = (bf16[256,128]{1,0:T(8,128)(2,1)}, bf16[256,128]{1,0:T(8,128)(2,1)}) custom-call(s32[1,512]{1,0:T(1,128)} %bitcast.7, s32[1,512]{1,0:T(1,128)} %bitcast.8, s32[1,512]{1,0:T(1,128)} %bitcast.9, bf16[7680,128]{1,0:T(8,128)(2,1)} %bitcast.4), custom_call_target="tpu_custom_call" | custom-call | flops 1006632960 | bytes 1966080 | tf_op jit(solution)/shard_map/pallas_call | solution.py:538
  6.8 0.5 %collective-permute-start = (bf16[256,128]{1,0:T(8,128)(2,1)}, bf16[256,128]{1,0:T(8,128)(2,1)S(1)}, u32[]{:S(2)}, u32[]{:S(2)}) collective-permute-start(bf16[256,128]{1,0:T(8,128)(2,1)} %get-tuple-element.10), channel_id=1, source_target_pairs={{0,4},{4,0},{1,5},{5,1},{2,6},{6,2},{3,7},{7,3},{8,12},{12,8},{9,1... | collective-permute-start | bytes 196616 | tf_op jit(solution)/shard_map/ppermute | solution.py:510
  7.3 1.1 %collective-permute-done = bf16[256,128]{1,0:T(8,128)(2,1)S(1)} collective-permute-done((bf16[256,128]{1,0:T(8,128)(2,1)}, bf16[256,128]{1,0:T(8,128)(2,1)S(1)}, u32[]{:S(2)}, u32[]{:S(2)}) %collective-permute-start) | collective-permute-done | bytes 65568 | tf_op jit(solution)/shard_map/ppermute | solution.py:510
  8.4 0.9 %add.9 = bf16[256,128]{1,0:T(8,128)(2,1)S(1)} add(bf16[256,128]{1,0:T(8,128)(2,1)} %get-tuple-element.9.after_ref, bf16[256,128]{1,0:T(8,128)(2,1)S(1)} %collective-permute-done) | non-fusion elementwise | flops 32768 | bytes 196608 | tf_op jit(solution)/shard_map/add | solution.py:565
  9.3 3.0 %collective-permute-start.1 = (bf16[256,128]{1,0:T(8,128)(2,1)S(1)}, bf16[256,128]{1,0:T(8,128)(2,1)S(1)}, u32[]{:S(2)}, u32[]{:S(2)}) collective-permute-start(bf16[256,128]{1,0:T(8,128)(2,1)S(1)} %add.9), channel_id=1, source_target_pairs={{0,1},{1,0},{2,3},{3,2},{4,6},{5,7},{6,4},{7,5},{8,9},{9,8},{10,11... | collective-permute-start | bytes 196616 | tf_op jit(solution)/shard_map/ppermute | solution.py:521
  12.2 2.9 %collective-permute-done.1 = bf16[256,128]{1,0:T(8,128)(2,1)S(1)} collective-permute-done((bf16[256,128]{1,0:T(8,128)(2,1)S(1)}, bf16[256,128]{1,0:T(8,128)(2,1)S(1)}, u32[]{:S(2)}, u32[]{:S(2)}) %collective-permute-start.1) | collective-permute-done | bytes 65568 | tf_op jit(solution)/shard_map/ppermute | solution.py:521
  15.2 2.4 %collective-permute-start.2 = (bf16[256,128]{1,0:T(8,128)(2,1)S(1)}, bf16[256,128]{1,0:T(8,128)(2,1)S(1)}, u32[]{:S(2)}, u32[]{:S(2)}) collective-permute-start(bf16[256,128]{1,0:T(8,128)(2,1)S(1)} %add.10), channel_id=1, source_target_pairs={{0,2},{1,3},{2,0},{3,1},{4,5},{5,4},{6,7},{7,6},{8,10},{9,11},{10,... | collective-permute-start | bytes 196616 | tf_op jit(solution)/shard_map/ppermute | solution.py:521
  17.6 0.0 copy-start
  17.6 0.8 %copy-done = bf16[256,128]{1,0:T(8,128)(2,1)S(1)} copy-done((bf16[256,128]{1,0:T(8,128)(2,1)S(1)}, bf16[256,128]{1,0:T(8,128)(2,1)}, u32[]{:S(2)}) %copy-start) | copy-done | bytes 65560
  18.4 1.2 %shard_map.83.coord_ref = bf16[7680,128]{1,0:T(8,128)(2,1)S(1)} custom-call(bf16[256,128]{1,0:T(8,128)(2,1)S(1)} %copy-done), custom_call_target="tpu_custom_call" | custom-call | flops 7864320 | bytes 1966080 | tf_op jit(solution)/shard_map/pallas_call | solution.py:557
  19.6 0.8 %collective-permute-done.2 = bf16[256,128]{1,0:T(8,128)(2,1)S(1)} collective-permute-done((bf16[256,128]{1,0:T(8,128)(2,1)S(1)}, bf16[256,128]{1,0:T(8,128)(2,1)S(1)}, u32[]{:S(2)}, u32[]{:S(2)}) %collective-permute-start.2) | collective-permute-done | bytes 65568 | tf_op jit(solution)/shard_map/ppermute | solution.py:521
  20.5 0.1 collective-permute-start.5
  20.5 0.0 copy-done.5
  20.6 2.7 %shard_map.84 = f32[288,128]{1,0:T(8,128)S(1)} custom-call(bf16[256,128]{1,0:T(8,128)(2,1)S(1)} %add.11.query_ref, bf16[7680,128]{1,0:T(8,128)(2,1)S(1)} %bitcast.5, bf16[7680,128]{1,0:T(8,128)(2,1)S(1)} %shard_map.83.coord_ref), custom_call_target="tpu_custom_call" | custom-call | flops 1509949440 | bytes 3932160 | tf_op jit(solution)/shard_map/pallas_call | solution.py:574
  23.3 1.9 %collective-permute-start.3 = (f16[288,128]{1,0:T(8,128)(2,1)S(1)}, f16[288,128]{1,0:T(8,128)(2,1)S(1)}, u32[]{:S(2)}, u32[]{:S(2)}) collective-permute-start(f16[288,128]{1,0:T(8,128)(2,1)S(1)} %convert_element_type.36), channel_id=1, source_target_pairs={{0,1},{1,0},{2,3},{3,2},{4,6},{5,7},{6,4},{7,5},{8,9},{9,8},{10,11... | collective-permute-start | bytes 221192 | tf_op jit(solution)/shard_map/ppermute | solution.py:521
  25.2 0.0 collective-permute-done.5.query_ref
  25.2 2.7 %shard_map.86 = f32[288,128]{1,0:T(8,128)S(1)} custom-call(bf16[256,128]{1,0:T(8,128)(2,1)S(1)} %collective-permute-done.5.query_ref, bf16[7680,128]{1,0:T(8,128)(2,1)S(1)} %bitcast.6, bf16[7680,128]{1,0:T(8,128)(2,1)S(1)} %shard_map.83.coord_ref), custom_call_target="tpu_custom_call" | custom-call | flops 1509949440 | bytes 3932160 | tf_op jit(solution)/shard_map/pallas_call | solution.py:574
  27.9 0.0 copy-start.4
  27.9 0.0 copy-start.1
  27.9 0.0 copy-start.2
  27.9 0.0 copy-start.3
  27.9 0.3 collective-permute-start.6
  28.2 0.2 collective-permute-done.3
  28.5 0.3 shard_map.85
  28.8 2.3 %collective-permute-start.4 = (f16[288,128]{1,0:T(8,128)(2,1)S(1)}, f16[288,128]{1,0:T(8,128)(2,1)S(1)}, u32[]{:S(2)}, u32[]{:S(2)}) collective-permute-start(f16[288,128]{1,0:T(8,128)(2,1)S(1)} %convert_element_type.39), channel_id=1, source_target_pairs={{0,2},{1,3},{2,0},{3,1},{4,5},{5,4},{6,7},{7,6},{8,10},{9,11},{10,... | collective-permute-start | bytes 221192 | tf_op jit(solution)/shard_map/ppermute | solution.py:521
  31.1 2.8 %collective-permute-done.6 = f16[288,128]{1,0:T(8,128)(2,1)S(1)} collective-permute-done((f16[288,128]{1,0:T(8,128)(2,1)S(1)}, f16[288,128]{1,0:T(8,128)(2,1)S(1)}, u32[]{:S(2)}, u32[]{:S(2)}) %collective-permute-start.6) | collective-permute-done | bytes 73760 | tf_op jit(solution)/shard_map/ppermute | solution.py:521
  34.0 0.3 shard_map.87
  34.3 1.8 %collective-permute-start.7 = (f16[288,128]{1,0:T(8,128)(2,1)S(1)}, f16[288,128]{1,0:T(8,128)(2,1)S(1)}, u32[]{:S(2)}, u32[]{:S(2)}) collective-permute-start(f16[288,128]{1,0:T(8,128)(2,1)S(1)} %convert_element_type.45), channel_id=1, source_target_pairs={{0,2},{1,3},{2,0},{3,1},{4,5},{5,4},{6,7},{7,6},{8,10},{9,11},{10,... | collective-permute-start | bytes 221192 | tf_op jit(solution)/shard_map/ppermute | solution.py:521
  36.1 0.0 collective-permute-done.4
  36.1 3.5 %collective-permute-done.7 = f16[288,128]{1,0:T(8,128)(2,1)S(1)} collective-permute-done((f16[288,128]{1,0:T(8,128)(2,1)S(1)}, f16[288,128]{1,0:T(8,128)(2,1)S(1)}, u32[]{:S(2)}, u32[]{:S(2)}) %collective-permute-start.7) | collective-permute-done | bytes 73760 | tf_op jit(solution)/shard_map/ppermute | solution.py:521
  39.6 0.0 copy-done.4
  39.6 0.5 %shard_map.88 = (bf16[528,128]{1,0:T(8,128)(2,1)S(1)}, f32[2,512]{1,0:T(2,128)S(1)}) custom-call(f32[1,128]{1,0:T(1,128)S(1)} %copy-done.4, f32[288,128]{1,0:T(8,128)S(1)} %convert_element_type.40.near_own, f32[288,128]{1,0:T(8,128)S(1)} %convert_element_type.41.near_came, f32[288,128]{1,0:T(8,128)S(1)} %convert_element_type.46.far_own, ...), custom_call_target="tpu_custom_call" | custom-call | flops 262144 | bytes 786432 | tf_op jit(solution)/shard_map/pallas_call | solution.py:602
  40.1 0.1 collective-permute-start.8
  40.2 1.3 %collective-permute-done.8.theirs_ref = bf16[528,128]{1,0:T(8,128)(2,1)S(1)} collective-permute-done((bf16[528,128]{1,0:T(8,128)(2,1)S(1)}, bf16[528,128]{1,0:T(8,128)(2,1)S(1)}, u32[]{:S(2)}, u32[]{:S(2)}) %collective-permute-start.8) | collective-permute-done | bytes 135200 | tf_op jit(solution)/shard_map/ppermute | solution.py:510
  41.5 0.0 copy-done.1
  41.5 0.0 copy-done.2
  41.5 0.0 copy-done.3
  41.5 1.3 %shard_map.89 = f32[1,2,512]{2,1,0:T(2,128)} custom-call(f32[3,128]{1,0:T(4,128)S(1)} %copy-done.2, bf16[128,128]{1,0:T(8,128)(2,1)S(1)} %copy-done.1, f32[2,128]{1,0:T(2,128)S(1)} %copy-done.3, f32[2,512]{1,0:T(2,128)S(1)} %get-tuple-element.11.place_ref, bf16[528,128]{1,0:T(8,128)(2,1)S(1)} %get-tuple-element.12.mine_ref, ...), custom_call_target="tpu_custom_call" | custom-call | flops 67108864 | bytes 524288 | tf_op jit(solution)/shard_map/pallas_call | solution.py:613
  (14 shorter events, 0.2 us)
Async XLA Ops:
  0.0 20.5 %copy-start.5 = (bf16[1,32,240,128]{3,2,1,0:T(8,128)(2,1)S(1)}, bf16[1,32,240,128]{3,2,1,0:T(8,128)(2,1)}, u32[]{:S(2)}) copy-start(bf16[1,32,240,128]{3,2,1,0:T(8,128)(2,1)} %param.8) | copy-start | bytes 5898244
  6.8 1.6 %collective-permute-start = (bf16[256,128]{1,0:T(8,128)(2,1)}, bf16[256,128]{1,0:T(8,128)(2,1)S(1)}, u32[]{:S(2)}, u32[]{:S(2)}) collective-permute-start(bf16[256,128]{1,0:T(8,128)(2,1)} %get-tuple-element.10), channel_id=1, source_target_pairs={{0,4},{4,0},{1,5},{5,1},{2,6},{6,2},{3,7},{7,3},{8,12},{12,8},{9,1... | collective-permute-start | bytes 196616 | tf_op jit(solution)/shard_map/ppermute | solution.py:510
  9.3 5.9 %collective-permute-start.1 = (bf16[256,128]{1,0:T(8,128)(2,1)S(1)}, bf16[256,128]{1,0:T(8,128)(2,1)S(1)}, u32[]{:S(2)}, u32[]{:S(2)}) collective-permute-start(bf16[256,128]{1,0:T(8,128)(2,1)S(1)} %add.9), channel_id=1, source_target_pairs={{0,1},{1,0},{2,3},{3,2},{4,6},{5,7},{6,4},{7,5},{8,9},{9,8},{10,11... | collective-permute-start | bytes 196616 | tf_op jit(solution)/shard_map/ppermute | solution.py:521
  15.2 5.2 %collective-permute-start.2 = (bf16[256,128]{1,0:T(8,128)(2,1)S(1)}, bf16[256,128]{1,0:T(8,128)(2,1)S(1)}, u32[]{:S(2)}, u32[]{:S(2)}) collective-permute-start(bf16[256,128]{1,0:T(8,128)(2,1)S(1)} %add.10), channel_id=1, source_target_pairs={{0,2},{1,3},{2,0},{3,1},{4,5},{5,4},{6,7},{7,6},{8,10},{9,11},{10,... | collective-permute-start | bytes 196616 | tf_op jit(solution)/shard_map/ppermute | solution.py:521
  17.6 0.8 %copy-start = (bf16[256,128]{1,0:T(8,128)(2,1)S(1)}, bf16[256,128]{1,0:T(8,128)(2,1)}, u32[]{:S(2)}) copy-start(bf16[256,128]{1,0:T(8,128)(2,1)} %get-tuple-element.9.after_ref) | copy-start | bytes 196612
  20.5 4.7 %collective-permute-start.5 = (bf16[256,128]{1,0:T(8,128)(2,1)S(1)}, bf16[256,128]{1,0:T(8,128)(2,1)S(1)}, u32[]{:S(2)}, u32[]{:S(2)}) collective-permute-start(bf16[256,128]{1,0:T(8,128)(2,1)S(1)} %add.11.query_ref), channel_id=1, source_target_pairs={{0,4},{4,0},{1,5},{5,1},{2,6},{6,2},{3,7},{7,3},{8,12},{12,8},{9,1... | collective-permute-start | bytes 196616 | tf_op jit(solution)/shard_map/ppermute | solution.py:510
  23.3 5.2 %collective-permute-start.3 = (f16[288,128]{1,0:T(8,128)(2,1)S(1)}, f16[288,128]{1,0:T(8,128)(2,1)S(1)}, u32[]{:S(2)}, u32[]{:S(2)}) collective-permute-start(f16[288,128]{1,0:T(8,128)(2,1)S(1)} %convert_element_type.36), channel_id=1, source_target_pairs={{0,1},{1,0},{2,3},{3,2},{4,6},{5,7},{6,4},{7,5},{8,9},{9,8},{10,11... | collective-permute-start | bytes 221192 | tf_op jit(solution)/shard_map/ppermute | solution.py:521
  27.9 11.7 %copy-start.4 = (f32[1,128]{1,0:T(1,128)S(1)}, f32[1,128]{1,0:T(1,128)}, u32[]{:S(2)}) copy-start(f32[1,128]{1,0:T(1,128)} %decay_ref.1) | copy-start | bytes 1540
  27.9 13.6 %copy-start.1 = (bf16[128,128]{1,0:T(8,128)(2,1)S(1)}, bf16[128,128]{1,0:T(8,128)(2,1)}, u32[]{:S(2)}) copy-start(bf16[128,128]{1,0:T(8,128)(2,1)} %pw_ref.1) | copy-start | bytes 98308
  27.9 13.6 %copy-start.2 = (f32[3,128]{1,0:T(4,128)S(1)}, f32[3,128]{1,0:T(4,128)}, u32[]{:S(2)}) copy-start(f32[3,128]{1,0:T(4,128)} %dw_ref.1) | copy-start | bytes 4612
  27.9 13.6 %copy-start.3 = (f32[2,128]{1,0:T(2,128)S(1)}, f32[2,128]{1,0:T(2,128)}, u32[]{:S(2)}) copy-start(f32[2,128]{1,0:T(2,128)} %ow_ref.1) | copy-start | bytes 3076
  27.9 6.0 %collective-permute-start.6 = (f16[288,128]{1,0:T(8,128)(2,1)S(1)}, f16[288,128]{1,0:T(8,128)(2,1)S(1)}, u32[]{:S(2)}, u32[]{:S(2)}) collective-permute-start(f16[288,128]{1,0:T(8,128)(2,1)S(1)} %convert_element_type.42), channel_id=1, source_target_pairs={{0,1},{1,0},{2,3},{3,2},{4,6},{5,7},{6,4},{7,5},{8,9},{9,8},{10,11... | collective-permute-start | bytes 221192 | tf_op jit(solution)/shard_map/ppermute | solution.py:521
  28.8 7.3 %collective-permute-start.4 = (f16[288,128]{1,0:T(8,128)(2,1)S(1)}, f16[288,128]{1,0:T(8,128)(2,1)S(1)}, u32[]{:S(2)}, u32[]{:S(2)}) collective-permute-start(f16[288,128]{1,0:T(8,128)(2,1)S(1)} %convert_element_type.39), channel_id=1, source_target_pairs={{0,2},{1,3},{2,0},{3,1},{4,5},{5,4},{6,7},{7,6},{8,10},{9,11},{10,... | collective-permute-start | bytes 221192 | tf_op jit(solution)/shard_map/ppermute | solution.py:521
  34.3 5.3 %collective-permute-start.7 = (f16[288,128]{1,0:T(8,128)(2,1)S(1)}, f16[288,128]{1,0:T(8,128)(2,1)S(1)}, u32[]{:S(2)}, u32[]{:S(2)}) collective-permute-start(f16[288,128]{1,0:T(8,128)(2,1)S(1)} %convert_element_type.45), channel_id=1, source_target_pairs={{0,2},{1,3},{2,0},{3,1},{4,5},{5,4},{6,7},{7,6},{8,10},{9,11},{10,... | collective-permute-start | bytes 221192 | tf_op jit(solution)/shard_map/ppermute | solution.py:521
  40.1 1.4 %collective-permute-start.8 = (bf16[528,128]{1,0:T(8,128)(2,1)S(1)}, bf16[528,128]{1,0:T(8,128)(2,1)S(1)}, u32[]{:S(2)}, u32[]{:S(2)}) collective-permute-start(bf16[528,128]{1,0:T(8,128)(2,1)S(1)} %get-tuple-element.12.mine_ref), channel_id=1, source_target_pairs={{0,4},{4,0},{1,5},{5,1},{2,6},{6,2},{3,7},{7,3},{8,12},{12,8},{9,1... | collective-permute-start | bytes 405512 | tf_op jit(solution)/shard_map/ppermute | solution.py:510

commit v6 on v4

--- a/solution.py
+++ b/solution.py
@@ -227,6 +227,14 @@
         out_ref[pl.ds(pl.multiple_of(step * chunk, chunk), chunk), :] = value.astype(BF16)
 
 
+def turn_kernel(map_ref, after_ref, out_ref):
+    positions = map_ref.shape[0]
+    chunk = pick_chunk(positions, 768)
+    for base in range(0, positions, chunk):
+        rows = map_ref[base : base + chunk, :].astype(F32)
+        out_ref[:, base : base + chunk] = jnp.transpose(rows).astype(BF16)
+
+
 def split(value):
     pieces = []
     for _ in range(3):
@@ -236,7 +244,7 @@
     return pieces
 
 
-def half_kernel(rows_here, height, width, query_ref, map_ref, coord_ref, out_ref):
+def half_kernel(rows_here, height, width, query_ref, map_ref, turned_ref, coord_ref, out_ref):
     positions, channels = map_ref.shape
     factor = math.log2(math.e) / math.sqrt(channels)
     query = query_ref[...]
@@ -244,8 +252,8 @@
     chunk = pick_chunk(positions, 1280)
 
     def score(base):
-        keys = map_ref[base : base + chunk, :]
-        return lax.dot_general(query, keys, NT, preferred_element_type=F32)
+        keys = turned_ref[:, base : base + chunk]
+        return jnp.dot(query, keys, preferred_element_type=F32)
 
     top = sums = None
     ahead = score(0)
@@ -513,10 +521,20 @@
         bytes_accessed=2 * positions * LANES,
         transcendentals=0,
     )(target)
-    mine = pick(0) + arrived
+    keep = pick(0)
+    turned = call(
+        turn_kernel,
+        jax.ShapeDtypeStruct((channels, positions), BF16),
+        2,
+        flops=8 * positions * LANES,
+        bytes_accessed=4 * positions * LANES,
+        transcendentals=0,
+    )(maps, keep)
+    mine = keep + arrived
     steps = n_space.bit_length() - 1
     for step in range(steps):
         mine = mine + space_swap(mine, step)
+        mine, turned = lax.optimization_barrier((mine, turned))
     theirs = core_swap(mine)
 
     block = jax.ShapeDtypeStruct((half + half // LANES * PIECE_ROWS, LANES), F32)
@@ -525,11 +543,11 @@
         return call(
             functools.partial(half_kernel, rows_here, height, map_width),
             block,
-            3,
+            4,
             flops=3 * queries * positions * channels,
             bytes_accessed=4 * positions * channels,
             transcendentals=half * positions,
-        )(feats, maps, coords)
+        )(feats, maps, turned, coords)
 
     def sent(value, step):
         value = lax.optimization_barrier(value.astype(jnp.float16))
@@ -540,8 +558,8 @@
             functools.partial(merge_kernel, n_space, step),
             block,
             2,
-            flops=4 * half * channels,
-            bytes_accessed=12 * half * channels,
+            flops=0,
+            bytes_accessed=0,
             transcendentals=0,
         )(*pair)
 

time: 40.6 us -> 39.2 us (0.966)
  waiting for transfers between devices: 13.8 us -> 10.5 us
  Pallas kernels: 11.3 us -> 12.3 us
  starting transfers between devices: 12.5 us -> 13.5 us
    ppermute x6, waiting for transfers between devices: 12.5 us -> 9.16 us  [space_swap(): return lax.ppermute(value, ('tm', 'space'), pairs)]
    ppermute x6, starting transfers between devices: 11.9 us -> 12.9 us  [space_swap(): return lax.ppermute(value, ('tm', 'space'), pairs)]
    pallas_call x2 -> x3, Pallas kernels: 0.49 us -> 1.08 us  [the longest x1 0.57 us: local_pair(): call(turn_kernel, jax.ShapeDtypeStruct((channels, positions), BF16), 2, f...]
  transfers between devices with their start and end apart: 9 -> 9, of which waited for: 7 -> 5; matrix products, arithmetic and copies ran while one was open for 0% -> 0% of each run, Pallas kernels for 21% -> 24%
where the time goes in v6:
time: 39.2 us; the launch traced here: 39 us
  starting transfers between devices  13.5 us (34%)
  Pallas kernels  12.3 us (31%)
  waiting for transfers between devices  10.5 us (27%)
  local copies, waits for them, and re-layouts  1.57 us (4%)
  other arithmetic  0.93 us (2%)
    ppermute x6, starting transfers between devices, space_swap(): return lax.ppermute(value, ('tm', 'space'), pairs)  12.9 us
    ppermute x6, waiting for transfers between devices, space_swap(): return lax.ppermute(value, ('tm', 'space'), pairs)  9.16 us
    pallas_call x2, Pallas kernels, blocks_of(): call(functools.partial(half_kernel, rows_here, height, map_width), block,...  5.73 us
    pallas_call x2, Pallas kernels, pick(): call(functools.partial(pick_kernel, core_flip), jax.ShapeDtypeStruct((hal...  2.49 us
    unnamed x12, local copies, waits for them, and re-layouts  1.57 us
    ppermute x3, waiting for transfers between devices, core_swap(): return lax.ppermute(value, 'tm', [(0, 1), (1, 0)])  1.35 us
    pallas_call x1, Pallas kernels, local_pair(): call(track_kernel, jax.ShapeDtypeStruct((1, n_out, queries), F32), 6, flo...  1.29 us
    pallas_call x1, Pallas kernels, local_pair(): call(functools.partial(coord_kernel, map_width), jax.ShapeDtypeStruct((po...  1.19 us
  transfers between devices with their start and end apart: 9, of which 5 were waited for; matrix products, arithmetic and copies ran while one was open for 0% of the time, Pallas kernels for 24%

profile of v6, /device:TPU:0, one launch (start us, length us, event | category | flops | bytes accessed | tf_op | source)
XLA Modules:
  0.0 39.0 jit_solution(2947296158300322995)
XLA Ops:
  0.0 0.7 %add_select_fusion = s32[512]{0:T(512)S(1)} fusion(s32[512]{0:T(512)} %param.11, s32[512]{0:T(512)} %param.10, s32[512]{0:T(512)} %param.9, s32[]{:T(128)S(6)} %mul.9, s32[]{:T(128)S(6)} %axis_index.23), kind=kLoop, calls=%fused_computation | loop fusion | flops 4608 | bytes 8200 | tf_op jit(solution)/shard_map/jit(_where)/select_n | solution.py:503
  0.7 0.0 copy-start
  0.7 1.5 %copy-done = bf16[1,32,240,128]{3,2,1,0:T(8,128)(2,1)S(1)} copy-done((bf16[1,32,240,128]{3,2,1,0:T(8,128)(2,1)S(1)}, bf16[1,32,240,128]{3,2,1,0:T(8,128)(2,1)}, u32[]{:S(2)}) %copy-start) | copy-done | bytes 1966104
  2.3 0.0 copy-start.1
  2.3 1.2 %shard_map.83 = bf16[256,128]{1,0:T(8,128)(2,1)S(1)} custom-call(s32[1,512]{1,0:T(1,128)S(1)} %bitcast.7, bf16[7680,128]{1,0:T(8,128)(2,1)S(1)} %bitcast.2), custom_call_target="tpu_custom_call" | custom-call | flops 503316480 | bytes 1966080 | tf_op jit(solution)/shard_map/pallas_call | solution.py:506
  3.5 0.5 %collective-permute-start = (bf16[256,128]{1,0:T(8,128)(2,1)S(1)}, bf16[256,128]{1,0:T(8,128)(2,1)S(1)}, u32[]{:S(2)}, u32[]{:S(2)}) collective-permute-start(bf16[256,128]{1,0:T(8,128)(2,1)S(1)} %shard_map.83), channel_id=1, source_target_pairs={{0,4},{4,0},{1,5},{5,1},{2,6},{6,2},{3,7},{7,3},{8,12},{12,8},{9,1... | collective-permute-start | bytes 196616 | tf_op jit(solution)/shard_map/ppermute | solution.py:476
  4.0 1.2 %shard_map.82.after_ref = bf16[256,128]{1,0:T(8,128)(2,1)S(1)} custom-call(s32[1,512]{1,0:T(1,128)S(1)} %bitcast.8, bf16[7680,128]{1,0:T(8,128)(2,1)S(1)} %bitcast.3), custom_call_target="tpu_custom_call" | custom-call | flops 503316480 | bytes 1966080 | tf_op jit(solution)/shard_map/pallas_call | solution.py:506
  5.3 0.0 collective-permute-done
  5.3 2.7 %collective-permute-start.1 = (bf16[256,128]{1,0:T(8,128)(2,1)S(1)}, bf16[256,128]{1,0:T(8,128)(2,1)S(1)}, u32[]{:S(2)}, u32[]{:S(2)}) collective-permute-start(bf16[256,128]{1,0:T(8,128)(2,1)S(1)} %add.13), channel_id=1, source_target_pairs={{0,1},{1,0},{2,3},{3,2},{4,6},{5,7},{6,4},{7,5},{8,9},{9,8},{10,11... | collective-permute-start | bytes 196616 | tf_op jit(solution)/shard_map/ppermute | solution.py:487
  8.0 0.0 copy-done.1
  8.0 0.6 %shard_map.84.turned_ref = bf16[128,7680]{1,0:T(8,128)(2,1)S(1)} custom-call(bf16[7680,128]{1,0:T(8,128)(2,1)S(1)} %bitcast.4, bf16[256,128]{1,0:T(8,128)(2,1)S(1)} %shard_map.82.after_ref), custom_call_target="tpu_custom_call" | custom-call | flops 7864320 | bytes 3932160 | tf_op jit(solution)/shard_map/pallas_call | solution.py:525
  8.6 1.7 %collective-permute-done.1 = bf16[256,128]{1,0:T(8,128)(2,1)S(1)} collective-permute-done((bf16[256,128]{1,0:T(8,128)(2,1)S(1)}, bf16[256,128]{1,0:T(8,128)(2,1)S(1)}, u32[]{:S(2)}, u32[]{:S(2)}) %collective-permute-start.1) | collective-permute-done | bytes 65568 | tf_op jit(solution)/shard_map/ppermute | solution.py:487
  10.3 3.2 %collective-permute-start.2 = (bf16[256,128]{1,0:T(8,128)(2,1)S(1)}, bf16[256,128]{1,0:T(8,128)(2,1)S(1)}, u32[]{:S(2)}, u32[]{:S(2)}) collective-permute-start(bf16[256,128]{1,0:T(8,128)(2,1)S(1)} %add.14), channel_id=1, source_target_pairs={{0,2},{1,3},{2,0},{3,1},{4,5},{5,4},{6,7},{7,6},{8,10},{9,11},{10,... | collective-permute-start | bytes 196616 | tf_op jit(solution)/shard_map/ppermute | solution.py:487
  13.5 1.2 %shard_map.85.coord_ref = bf16[7680,128]{1,0:T(8,128)(2,1)S(1)} custom-call(s32[1,512]{1,0:T(1,128)S(1)} %bitcast.9), custom_call_target="tpu_custom_call" | custom-call | flops 7864320 | bytes 1966080 | tf_op jit(solution)/shard_map/pallas_call | solution.py:516
  14.7 1.1 %collective-permute-done.2 = bf16[256,128]{1,0:T(8,128)(2,1)S(1)} collective-permute-done((bf16[256,128]{1,0:T(8,128)(2,1)S(1)}, bf16[256,128]{1,0:T(8,128)(2,1)S(1)}, u32[]{:S(2)}, u32[]{:S(2)}) %collective-permute-start.2) | collective-permute-done | bytes 65568 | tf_op jit(solution)/shard_map/ppermute | solution.py:487
  15.7 0.1 collective-permute-start.5
  15.8 2.9 %shard_map.86 = f32[288,128]{1,0:T(8,128)S(1)} custom-call(bf16[256,128]{1,0:T(8,128)(2,1)S(1)} %add.15.query_ref, bf16[7680,128]{1,0:T(8,128)(2,1)S(1)} %bitcast.5, bf16[128,7680]{1,0:T(8,128)(2,1)S(1)} %shard_map.84.turned_ref, bf16[7680,128]{1,0:T(8,128)(2,1)S(1)} %shard_map.85.coord_ref), custom_call_target="tpu_custom_call" | custom-call | flops 1509949440 | bytes 3932160 | tf_op jit(solution)/shard_map/pallas_call | solution.py:543
  18.7 2.4 %collective-permute-start.3 = (f16[288,128]{1,0:T(8,128)(2,1)S(1)}, f16[288,128]{1,0:T(8,128)(2,1)S(1)}, u32[]{:S(2)}, u32[]{:S(2)}) collective-permute-start(f16[288,128]{1,0:T(8,128)(2,1)S(1)} %convert_element_type.36), channel_id=1, source_target_pairs={{0,1},{1,0},{2,3},{3,2},{4,6},{5,7},{6,4},{7,5},{8,9},{9,8},{10,11... | collective-permute-start | bytes 221192 | tf_op jit(solution)/shard_map/ppermute | solution.py:487
  21.1 0.0 collective-permute-done.5.query_ref
  21.1 2.9 %shard_map.88 = f32[288,128]{1,0:T(8,128)S(1)} custom-call(bf16[256,128]{1,0:T(8,128)(2,1)S(1)} %collective-permute-done.5.query_ref, bf16[7680,128]{1,0:T(8,128)(2,1)S(1)} %bitcast.6, bf16[128,7680]{1,0:T(8,128)(2,1)S(1)} %shard_map.84.turned_ref, bf16[7680,128]{1,0:T(8,128)(2,1)S(1)} %shard_map.85.coord_ref), custom_call_target="tpu_custom_call" | custom-call | flops 1509949440 | bytes 3932160 | tf_op jit(solution)/shard_map/pallas_call | solution.py:543
  24.0 0.0 copy-start.5
  24.0 0.0 copy-start.2
  24.0 0.0 copy-start.3
  24.0 0.0 copy-start.4
  24.1 0.1 collective-permute-start.6
  24.2 0.0 collective-permute-done.3
  24.2 0.3 shard_map.87
  24.5 2.8 %collective-permute-start.4 = (f16[288,128]{1,0:T(8,128)(2,1)S(1)}, f16[288,128]{1,0:T(8,128)(2,1)S(1)}, u32[]{:S(2)}, u32[]{:S(2)}) collective-permute-start(f16[288,128]{1,0:T(8,128)(2,1)S(1)} %convert_element_type.39), channel_id=1, source_target_pairs={{0,2},{1,3},{2,0},{3,1},{4,5},{5,4},{6,7},{7,6},{8,10},{9,11},{10,... | collective-permute-start | bytes 221192 | tf_op jit(solution)/shard_map/ppermute | solution.py:487
  27.3 2.9 %collective-permute-done.6 = f16[288,128]{1,0:T(8,128)(2,1)S(1)} collective-permute-done((f16[288,128]{1,0:T(8,128)(2,1)S(1)}, f16[288,128]{1,0:T(8,128)(2,1)S(1)}, u32[]{:S(2)}, u32[]{:S(2)}) %collective-permute-start.6) | collective-permute-done | bytes 73760 | tf_op jit(solution)/shard_map/ppermute | solution.py:487
  30.2 0.3 shard_map.89
  30.5 1.7 %collective-permute-start.7 = (f16[288,128]{1,0:T(8,128)(2,1)S(1)}, f16[288,128]{1,0:T(8,128)(2,1)S(1)}, u32[]{:S(2)}, u32[]{:S(2)}) collective-permute-start(f16[288,128]{1,0:T(8,128)(2,1)S(1)} %convert_element_type.45), channel_id=1, source_target_pairs={{0,2},{1,3},{2,0},{3,1},{4,5},{5,4},{6,7},{7,6},{8,10},{9,11},{10,... | collective-permute-start | bytes 221192 | tf_op jit(solution)/shard_map/ppermute | solution.py:487
  32.3 0.0 collective-permute-done.4
  32.3 3.5 %collective-permute-done.7 = f16[288,128]{1,0:T(8,128)(2,1)S(1)} collective-permute-done((f16[288,128]{1,0:T(8,128)(2,1)S(1)}, f16[288,128]{1,0:T(8,128)(2,1)S(1)}, u32[]{:S(2)}, u32[]{:S(2)}) %collective-permute-start.7) | collective-permute-done | bytes 73760 | tf_op jit(solution)/shard_map/ppermute | solution.py:487
  35.8 0.0 copy-done.5
  35.8 0.5 %shard_map.90 = (bf16[528,128]{1,0:T(8,128)(2,1)S(1)}, f32[2,512]{1,0:T(2,128)S(1)}) custom-call(f32[1,128]{1,0:T(1,128)S(1)} %copy-done.5, f32[288,128]{1,0:T(8,128)S(1)} %convert_element_type.40.near_own, f32[288,128]{1,0:T(8,128)S(1)} %convert_element_type.41.near_came, f32[288,128]{1,0:T(8,128)S(1)} %convert_element_type.46.far_own, ...), custom_call_target="tpu_custom_call" | custom-call | flops 262144 | bytes 786432 | tf_op jit(solution)/shard_map/pallas_call | solution.py:571
  36.3 0.1 collective-permute-start.8
  36.4 1.3 %collective-permute-done.8.theirs_ref = bf16[528,128]{1,0:T(8,128)(2,1)S(1)} collective-permute-done((bf16[528,128]{1,0:T(8,128)(2,1)S(1)}, bf16[528,128]{1,0:T(8,128)(2,1)S(1)}, u32[]{:S(2)}, u32[]{:S(2)}) %collective-permute-start.8) | collective-permute-done | bytes 135200 | tf_op jit(solution)/shard_map/ppermute | solution.py:476
  37.7 0.0 copy-done.2
  37.7 0.0 copy-done.3
  37.7 0.0 copy-done.4
  37.7 1.3 %shard_map.91 = f32[1,2,512]{2,1,0:T(2,128)} custom-call(f32[3,128]{1,0:T(4,128)S(1)} %copy-done.3, bf16[128,128]{1,0:T(8,128)(2,1)S(1)} %copy-done.2, f32[2,128]{1,0:T(2,128)S(1)} %copy-done.4, f32[2,512]{1,0:T(2,128)S(1)} %get-tuple-element.15.place_ref, bf16[528,128]{1,0:T(8,128)(2,1)S(1)} %get-tuple-element.16.mine_ref, ...), custom_call_target="tpu_custom_call" | custom-call | flops 67108864 | bytes 524288 | tf_op jit(solution)/shard_map/pallas_call | solution.py:582
  (15 shorter events, 0.2 us)
Async XLA Ops:
  0.7 1.5 %copy-start = (bf16[1,32,240,128]{3,2,1,0:T(8,128)(2,1)S(1)}, bf16[1,32,240,128]{3,2,1,0:T(8,128)(2,1)}, u32[]{:S(2)}) copy-start(bf16[1,32,240,128]{3,2,1,0:T(8,128)(2,1)} %param.8) | copy-start | bytes 5898244
  2.3 5.7 %copy-start.1 = (bf16[1,32,240,128]{3,2,1,0:T(8,128)(2,1)S(1)}, bf16[1,32,240,128]{3,2,1,0:T(8,128)(2,1)}, u32[]{:S(2)}) copy-start(bf16[1,32,240,128]{3,2,1,0:T(8,128)(2,1)} %param.8) | copy-start | bytes 5898244
  3.5 1.8 %collective-permute-start = (bf16[256,128]{1,0:T(8,128)(2,1)S(1)}, bf16[256,128]{1,0:T(8,128)(2,1)S(1)}, u32[]{:S(2)}, u32[]{:S(2)}) collective-permute-start(bf16[256,128]{1,0:T(8,128)(2,1)S(1)} %shard_map.83), channel_id=1, source_target_pairs={{0,4},{4,0},{1,5},{5,1},{2,6},{6,2},{3,7},{7,3},{8,12},{12,8},{9,1... | collective-permute-start | bytes 196616 | tf_op jit(solution)/shard_map/ppermute | solution.py:476
  5.3 4.9 %collective-permute-start.1 = (bf16[256,128]{1,0:T(8,128)(2,1)S(1)}, bf16[256,128]{1,0:T(8,128)(2,1)S(1)}, u32[]{:S(2)}, u32[]{:S(2)}) collective-permute-start(bf16[256,128]{1,0:T(8,128)(2,1)S(1)} %add.13), channel_id=1, source_target_pairs={{0,1},{1,0},{2,3},{3,2},{4,6},{5,7},{6,4},{7,5},{8,9},{9,8},{10,11... | collective-permute-start | bytes 196616 | tf_op jit(solution)/shard_map/ppermute | solution.py:487
  10.3 5.5 %collective-permute-start.2 = (bf16[256,128]{1,0:T(8,128)(2,1)S(1)}, bf16[256,128]{1,0:T(8,128)(2,1)S(1)}, u32[]{:S(2)}, u32[]{:S(2)}) collective-permute-start(bf16[256,128]{1,0:T(8,128)(2,1)S(1)} %add.14), channel_id=1, source_target_pairs={{0,2},{1,3},{2,0},{3,1},{4,5},{5,4},{6,7},{7,6},{8,10},{9,11},{10,... | collective-permute-start | bytes 196616 | tf_op jit(solution)/shard_map/ppermute | solution.py:487
  15.7 5.4 %collective-permute-start.5 = (bf16[256,128]{1,0:T(8,128)(2,1)S(1)}, bf16[256,128]{1,0:T(8,128)(2,1)S(1)}, u32[]{:S(2)}, u32[]{:S(2)}) collective-permute-start(bf16[256,128]{1,0:T(8,128)(2,1)S(1)} %add.15.query_ref), channel_id=1, source_target_pairs={{0,4},{4,0},{1,5},{5,1},{2,6},{6,2},{3,7},{7,3},{8,12},{12,8},{9,1... | collective-permute-start | bytes 196616 | tf_op jit(solution)/shard_map/ppermute | solution.py:476
  18.7 5.5 %collective-permute-start.3 = (f16[288,128]{1,0:T(8,128)(2,1)S(1)}, f16[288,128]{1,0:T(8,128)(2,1)S(1)}, u32[]{:S(2)}, u32[]{:S(2)}) collective-permute-start(f16[288,128]{1,0:T(8,128)(2,1)S(1)} %convert_element_type.36), channel_id=1, source_target_pairs={{0,1},{1,0},{2,3},{3,2},{4,6},{5,7},{6,4},{7,5},{8,9},{9,8},{10,11... | collective-permute-start | bytes 221192 | tf_op jit(solution)/shard_map/ppermute | solution.py:487
  24.0 11.8 %copy-start.5 = (f32[1,128]{1,0:T(1,128)S(1)}, f32[1,128]{1,0:T(1,128)}, u32[]{:S(2)}) copy-start(f32[1,128]{1,0:T(1,128)} %decay_ref.1) | copy-start | bytes 1540
  24.0 13.7 %copy-start.2 = (bf16[128,128]{1,0:T(8,128)(2,1)S(1)}, bf16[128,128]{1,0:T(8,128)(2,1)}, u32[]{:S(2)}) copy-start(bf16[128,128]{1,0:T(8,128)(2,1)} %pw_ref.1) | copy-start | bytes 98308
  24.0 13.7 %copy-start.3 = (f32[3,128]{1,0:T(4,128)S(1)}, f32[3,128]{1,0:T(4,128)}, u32[]{:S(2)}) copy-start(f32[3,128]{1,0:T(4,128)} %dw_ref.1) | copy-start | bytes 4612
  24.0 13.7 %copy-start.4 = (f32[2,128]{1,0:T(2,128)S(1)}, f32[2,128]{1,0:T(2,128)}, u32[]{:S(2)}) copy-start(f32[2,128]{1,0:T(2,128)} %ow_ref.1) | copy-start | bytes 3076
  24.1 6.1 %collective-permute-start.6 = (f16[288,128]{1,0:T(8,128)(2,1)S(1)}, f16[288,128]{1,0:T(8,128)(2,1)S(1)}, u32[]{:S(2)}, u32[]{:S(2)}) collective-permute-start(f16[288,128]{1,0:T(8,128)(2,1)S(1)} %convert_element_type.42), channel_id=1, source_target_pairs={{0,1},{1,0},{2,3},{3,2},{4,6},{5,7},{6,4},{7,5},{8,9},{9,8},{10,11... | collective-permute-start | bytes 221192 | tf_op jit(solution)/shard_map/ppermute | solution.py:487
  24.5 7.7 %collective-permute-start.4 = (f16[288,128]{1,0:T(8,128)(2,1)S(1)}, f16[288,128]{1,0:T(8,128)(2,1)S(1)}, u32[]{:S(2)}, u32[]{:S(2)}) collective-permute-start(f16[288,128]{1,0:T(8,128)(2,1)S(1)} %convert_element_type.39), channel_id=1, source_target_pairs={{0,2},{1,3},{2,0},{3,1},{4,5},{5,4},{6,7},{7,6},{8,10},{9,11},{10,... | collective-permute-start | bytes 221192 | tf_op jit(solution)/shard_map/ppermute | solution.py:487
  30.5 5.3 %collective-permute-start.7 = (f16[288,128]{1,0:T(8,128)(2,1)S(1)}, f16[288,128]{1,0:T(8,128)(2,1)S(1)}, u32[]{:S(2)}, u32[]{:S(2)}) collective-permute-start(f16[288,128]{1,0:T(8,128)(2,1)S(1)} %convert_element_type.45), channel_id=1, source_target_pairs={{0,2},{1,3},{2,0},{3,1},{4,5},{5,4},{6,7},{7,6},{8,10},{9,11},{10,... | collective-permute-start | bytes 221192 | tf_op jit(solution)/shard_map/ppermute | solution.py:487
  36.3 1.4 %collective-permute-start.8 = (bf16[528,128]{1,0:T(8,128)(2,1)S(1)}, bf16[528,128]{1,0:T(8,128)(2,1)S(1)}, u32[]{:S(2)}, u32[]{:S(2)}) collective-permute-start(bf16[528,128]{1,0:T(8,128)(2,1)S(1)} %get-tuple-element.16.mine_ref), channel_id=1, source_target_pairs={{0,4},{4,0},{1,5},{5,1},{2,6},{6,2},{3,7},{7,3},{8,12},{12,8},{9,1... | collective-permute-start | bytes 405512 | tf_op jit(solution)/shard_map/ppermute | solution.py:476

commit v7 on v4

--- a/solution.py
+++ b/solution.py
@@ -212,7 +212,7 @@
     out_ref[...] = picked.astype(BF16)
 
 
-def coord_kernel(map_width, after_ref, out_ref):
+def coord_kernel(map_width, out_ref):
     positions = out_ref.shape[0]
     chunk = pick_chunk(positions, 512)
     lane = lax.broadcasted_iota(jnp.int32, (chunk, LANES), 1)
@@ -241,7 +241,7 @@
     factor = math.log2(math.e) / math.sqrt(channels)
     query = query_ref[...]
     first_row = (lax.axis_index("space") * rows_here).astype(F32)
-    chunk = pick_chunk(positions, 1280)
+    chunk = pick_chunk(positions, 2560)
 
     def score(base):
         keys = map_ref[base : base + chunk, :]
@@ -372,10 +372,12 @@
     first = (1.0 - decay[0]) * refined[0]
     second = decay[1] * first + (1.0 - decay[1]) * refined[1]
     memory = jnp.where(early, first, second)
-    delta = lax.dot_general(
-        ow_ref[...], memory, NT, preferred_element_type=F32, precision=lax.Precision.HIGHEST
-    )
-    line = place_ref[...] + delta
+    n_out = ow_ref.shape[0]
+    weights = jnp.concatenate(split(ow_ref[...]), axis=0).astype(BF16)
+    line = place_ref[...]
+    for piece in split(memory)[:2]:
+        terms = lax.dot_general(weights, piece.astype(BF16), NT, preferred_element_type=F32)
+        line = line + terms[:n_out] + terms[n_out : 2 * n_out] + terms[2 * n_out :]
     low, high = line[:, :half], line[:, half:]
     out_ref[0, :, :half] = jnp.where(early, low, high)
     out_ref[0, :, half:] = jnp.where(early, high, low)
@@ -494,6 +496,16 @@
     here = (query_frame == lax.axis_index("tm")) & (row >= 0) & (row < rows_here)
     target = jnp.where(here, row * map_width + query_col, -1)[None]
 
+    coords = call(
+        functools.partial(coord_kernel, map_width),
+        jax.ShapeDtypeStruct((positions, LANES), BF16),
+        0,
+        flops=2048 * positions * LANES,
+        bytes_accessed=2 * positions * LANES,
+        transcendentals=0,
+    )()
+    target, coords = lax.optimization_barrier((target, coords))
+
     def pick(core_flip):
         return call(
             functools.partial(pick_kernel, core_flip),
@@ -505,14 +517,6 @@
         )(target, maps)
 
     arrived = core_swap(pick(1))
-    coords = call(
-        functools.partial(coord_kernel, map_width),
-        jax.ShapeDtypeStruct((positions, LANES), BF16),
-        1,
-        flops=8 * positions * LANES,
-        bytes_accessed=2 * positions * LANES,
-        transcendentals=0,
-    )(target)
     mine = pick(0) + arrived
     steps = n_space.bit_length() - 1
     for step in range(steps):
@@ -540,8 +544,8 @@
             functools.partial(merge_kernel, n_space, step),
             block,
             2,
-            flops=4 * half * channels,
-            bytes_accessed=12 * half * channels,
+            flops=0,
+            bytes_accessed=0,
             transcendentals=0,
         )(*pair)
 

time: 40.6 us -> 38.9 us (0.958)
  waiting for transfers between devices: 13.8 us -> 12.5 us
  starting transfers between devices: 12.5 us -> 13.3 us
  other arithmetic: 0.93 us -> 0.22 us
    ppermute x6, waiting for transfers between devices: 12.5 us -> 11.2 us  [space_swap(): return lax.ppermute(value, ('tm', 'space'), pairs)]
    ppermute x6, starting transfers between devices: 11.9 us -> 12.7 us  [space_swap(): return lax.ppermute(value, ('tm', 'space'), pairs)]
    select_n x1, other arithmetic: 0.72 us -> 0.01 us  [local_pair(): target = jnp.where(here, row * map_width + query_col, -1)[None]]
    unnamed x12 -> x20, local copies, waits for them, and re-layouts: 1.58 us -> 1.33 us
  transfers between devices with their start and end apart: 9 -> 9, of which waited for: 7 -> 6; matrix products, arithmetic and copies ran while one was open for 0% -> 0% of each run, Pallas kernels for 21% -> 18%
where the time goes in v7:
time: 38.9 us; the launch traced here: 38.7 us
  starting transfers between devices  13.3 us (34%)
  waiting for transfers between devices  12.5 us (32%)
  Pallas kernels  11.1 us (29%)
  local copies, waits for them, and re-layouts  1.33 us (3%)
    ppermute x6, starting transfers between devices, space_swap(): return lax.ppermute(value, ('tm', 'space'), pairs)  12.7 us
    ppermute x6, waiting for transfers between devices, space_swap(): return lax.ppermute(value, ('tm', 'space'), pairs)  11.2 us
    pallas_call x2, Pallas kernels, blocks_of(): call(functools.partial(half_kernel, rows_here, height, map_width), block,...  5.26 us
    pallas_call x2, Pallas kernels, pick(): call(functools.partial(pick_kernel, core_flip), jax.ShapeDtypeStruct((hal...  2.49 us
    ppermute x3, waiting for transfers between devices, core_swap(): return lax.ppermute(value, 'tm', [(0, 1), (1, 0)])  1.35 us
    unnamed x20, local copies, waits for them, and re-layouts  1.33 us
    pallas_call x1, Pallas kernels, local_pair(): call(functools.partial(coord_kernel, map_width), jax.ShapeDtypeStruct((po...  1.19 us
    pallas_call x1, Pallas kernels, local_pair(): call(track_kernel, jax.ShapeDtypeStruct((1, n_out, queries), F32), 6, flo...  1.16 us
  transfers between devices with their start and end apart: 9, of which 6 were waited for; matrix products, arithmetic and copies ran while one was open for 0% of the time, Pallas kernels for 18%

profile of v7, /device:TPU:0, one launch (start us, length us, event | category | flops | bytes accessed | tf_op | source)
XLA Modules:
  0.0 38.7 jit_solution(5016454011449495615)
XLA Ops:
  0.0 0.0 copy-start.7
  0.0 0.0 copy-start.8
  0.0 0.0 copy-start.9
  0.0 0.0 copy-start
  0.0 1.2 %shard_map.82.coord_ref = bf16[7680,128]{1,0:T(8,128)(2,1)S(1)} custom-call(), custom_call_target="tpu_custom_call" | custom-call | flops 2013265920 | bytes 1966080 | tf_op jit(solution)/shard_map/pallas_call | solution.py:499
  1.2 0.0 copy-start.5
  1.2 1.3 %copy-done.5 = bf16[7680,128]{1,0:T(8,128)(2,1)} copy-done((bf16[7680,128]{1,0:T(8,128)(2,1)}, bf16[7680,128]{1,0:T(8,128)(2,1)S(1)}, u32[]{:S(2)}) %copy-start.5) | copy-done | bytes 1966104
  2.5 0.0 copy-done.7
  2.5 0.0 copy-done.8
  2.5 0.0 copy-done.9
  2.5 0.0 copy-done
  2.5 0.0 copy-start.6
  2.5 1.2 %shard_map.84 = bf16[256,128]{1,0:T(8,128)(2,1)S(1)} custom-call(s32[1,512]{1,0:T(1,128)S(1)} %bitcast.6, bf16[7680,128]{1,0:T(8,128)(2,1)S(1)} %bitcast.2), custom_call_target="tpu_custom_call" | custom-call | flops 503316480 | bytes 1966080 | tf_op jit(solution)/shard_map/pallas_call | solution.py:510
  3.8 0.5 %collective-permute-start = (bf16[256,128]{1,0:T(8,128)(2,1)S(1)}, bf16[256,128]{1,0:T(8,128)(2,1)S(1)}, u32[]{:S(2)}, u32[]{:S(2)}) collective-permute-start(bf16[256,128]{1,0:T(8,128)(2,1)S(1)} %shard_map.84), channel_id=1, source_target_pairs={{0,4},{4,0},{1,5},{5,1},{2,6},{6,2},{3,7},{7,3},{8,12},{12,8},{9,1... | collective-permute-start | bytes 196616 | tf_op jit(solution)/shard_map/ppermute | solution.py:470
  4.3 1.2 %shard_map.83 = bf16[256,128]{1,0:T(8,128)(2,1)S(1)} custom-call(s32[1,512]{1,0:T(1,128)S(1)} %bitcast.7, bf16[7680,128]{1,0:T(8,128)(2,1)S(1)} %bitcast.3), custom_call_target="tpu_custom_call" | custom-call | flops 503316480 | bytes 1966080 | tf_op jit(solution)/shard_map/pallas_call | solution.py:510
  5.6 0.0 collective-permute-done
  5.6 2.6 %collective-permute-start.1 = (bf16[256,128]{1,0:T(8,128)(2,1)S(1)}, bf16[256,128]{1,0:T(8,128)(2,1)S(1)}, u32[]{:S(2)}, u32[]{:S(2)}) collective-permute-start(bf16[256,128]{1,0:T(8,128)(2,1)S(1)} %add.13), channel_id=1, source_target_pairs={{0,1},{1,0},{2,3},{3,2},{4,6},{5,7},{6,4},{7,5},{8,9},{9,8},{10,11... | collective-permute-start | bytes 196616 | tf_op jit(solution)/shard_map/ppermute | solution.py:481
  8.3 2.2 %collective-permute-done.1 = bf16[256,128]{1,0:T(8,128)(2,1)S(1)} collective-permute-done((bf16[256,128]{1,0:T(8,128)(2,1)S(1)}, bf16[256,128]{1,0:T(8,128)(2,1)S(1)}, u32[]{:S(2)}, u32[]{:S(2)}) %collective-permute-start.1) | collective-permute-done | bytes 65568 | tf_op jit(solution)/shard_map/ppermute | solution.py:481
  10.5 3.2 %collective-permute-start.2 = (bf16[256,128]{1,0:T(8,128)(2,1)S(1)}, bf16[256,128]{1,0:T(8,128)(2,1)S(1)}, u32[]{:S(2)}, u32[]{:S(2)}) collective-permute-start(bf16[256,128]{1,0:T(8,128)(2,1)S(1)} %add.14), channel_id=1, source_target_pairs={{0,2},{1,3},{2,0},{3,1},{4,5},{5,4},{6,7},{7,6},{8,10},{9,11},{10,... | collective-permute-start | bytes 196616 | tf_op jit(solution)/shard_map/ppermute | solution.py:481
  13.7 2.2 %collective-permute-done.2 = bf16[256,128]{1,0:T(8,128)(2,1)S(1)} collective-permute-done((bf16[256,128]{1,0:T(8,128)(2,1)S(1)}, bf16[256,128]{1,0:T(8,128)(2,1)S(1)}, u32[]{:S(2)}, u32[]{:S(2)}) %collective-permute-start.2) | collective-permute-done | bytes 65568 | tf_op jit(solution)/shard_map/ppermute | solution.py:481
  16.0 0.1 collective-permute-start.5
  16.1 0.0 copy-done.6
  16.1 2.6 %shard_map.85 = f32[288,128]{1,0:T(8,128)S(1)} custom-call(bf16[256,128]{1,0:T(8,128)(2,1)S(1)} %add.15.query_ref, bf16[7680,128]{1,0:T(8,128)(2,1)S(1)} %bitcast.4, bf16[7680,128]{1,0:T(8,128)(2,1)S(1)} %copy-done.6), custom_call_target="tpu_custom_call" | custom-call | flops 1509949440 | bytes 3932160 | tf_op jit(solution)/shard_map/pallas_call | solution.py:529
  18.8 2.4 %collective-permute-start.3 = (f16[288,128]{1,0:T(8,128)(2,1)S(1)}, f16[288,128]{1,0:T(8,128)(2,1)S(1)}, u32[]{:S(2)}, u32[]{:S(2)}) collective-permute-start(f16[288,128]{1,0:T(8,128)(2,1)S(1)} %convert_element_type.36), channel_id=1, source_target_pairs={{0,1},{1,0},{2,3},{3,2},{4,6},{5,7},{6,4},{7,5},{8,9},{9,8},{10,11... | collective-permute-start | bytes 221192 | tf_op jit(solution)/shard_map/ppermute | solution.py:481
  21.2 0.0 collective-permute-done.5.query_ref
  21.2 2.6 %shard_map.87 = f32[288,128]{1,0:T(8,128)S(1)} custom-call(bf16[256,128]{1,0:T(8,128)(2,1)S(1)} %collective-permute-done.5.query_ref, bf16[7680,128]{1,0:T(8,128)(2,1)S(1)} %bitcast.5, bf16[7680,128]{1,0:T(8,128)(2,1)S(1)} %copy-done.6), custom_call_target="tpu_custom_call" | custom-call | flops 1509949440 | bytes 3932160 | tf_op jit(solution)/shard_map/pallas_call | solution.py:529
  23.8 0.0 copy-start.4
  23.8 0.0 copy-start.1
  23.8 0.0 copy-start.2
  23.8 0.0 copy-start.3
  23.9 0.1 collective-permute-start.6
  24.0 0.3 collective-permute-done.3
  24.3 0.3 shard_map.86
  24.6 2.6 %collective-permute-start.4 = (f16[288,128]{1,0:T(8,128)(2,1)S(1)}, f16[288,128]{1,0:T(8,128)(2,1)S(1)}, u32[]{:S(2)}, u32[]{:S(2)}) collective-permute-start(f16[288,128]{1,0:T(8,128)(2,1)S(1)} %convert_element_type.39), channel_id=1, source_target_pairs={{0,2},{1,3},{2,0},{3,1},{4,5},{5,4},{6,7},{7,6},{8,10},{9,11},{10,... | collective-permute-start | bytes 221192 | tf_op jit(solution)/shard_map/ppermute | solution.py:481
  27.2 2.8 %collective-permute-done.6 = f16[288,128]{1,0:T(8,128)(2,1)S(1)} collective-permute-done((f16[288,128]{1,0:T(8,128)(2,1)S(1)}, f16[288,128]{1,0:T(8,128)(2,1)S(1)}, u32[]{:S(2)}, u32[]{:S(2)}) %collective-permute-start.6) | collective-permute-done | bytes 73760 | tf_op jit(solution)/shard_map/ppermute | solution.py:481
  30.0 0.3 shard_map.88
  30.3 1.7 %collective-permute-start.7 = (f16[288,128]{1,0:T(8,128)(2,1)S(1)}, f16[288,128]{1,0:T(8,128)(2,1)S(1)}, u32[]{:S(2)}, u32[]{:S(2)}) collective-permute-start(f16[288,128]{1,0:T(8,128)(2,1)S(1)} %convert_element_type.45), channel_id=1, source_target_pairs={{0,2},{1,3},{2,0},{3,1},{4,5},{5,4},{6,7},{7,6},{8,10},{9,11},{10,... | collective-permute-start | bytes 221192 | tf_op jit(solution)/shard_map/ppermute | solution.py:481
  32.0 0.0 collective-permute-done.4
  32.1 3.6 %collective-permute-done.7 = f16[288,128]{1,0:T(8,128)(2,1)S(1)} collective-permute-done((f16[288,128]{1,0:T(8,128)(2,1)S(1)}, f16[288,128]{1,0:T(8,128)(2,1)S(1)}, u32[]{:S(2)}, u32[]{:S(2)}) %collective-permute-start.7) | collective-permute-done | bytes 73760 | tf_op jit(solution)/shard_map/ppermute | solution.py:481
  35.6 0.0 copy-done.4
  35.7 0.5 %shard_map.89 = (bf16[528,128]{1,0:T(8,128)(2,1)S(1)}, f32[2,512]{1,0:T(2,128)S(1)}) custom-call(f32[1,128]{1,0:T(1,128)S(1)} %copy-done.4, f32[288,128]{1,0:T(8,128)S(1)} %convert_element_type.40.near_own, f32[288,128]{1,0:T(8,128)S(1)} %convert_element_type.41.near_came, f32[288,128]{1,0:T(8,128)S(1)} %convert_element_type.46.far_own, ...), custom_call_target="tpu_custom_call" | custom-call | flops 262144 | bytes 786432 | tf_op jit(solution)/shard_map/pallas_call | solution.py:557
  36.1 0.1 collective-permute-start.8
  36.2 1.3 %collective-permute-done.8.theirs_ref = bf16[528,128]{1,0:T(8,128)(2,1)S(1)} collective-permute-done((bf16[528,128]{1,0:T(8,128)(2,1)S(1)}, bf16[528,128]{1,0:T(8,128)(2,1)S(1)}, u32[]{:S(2)}, u32[]{:S(2)}) %collective-permute-start.8) | collective-permute-done | bytes 135200 | tf_op jit(solution)/shard_map/ppermute | solution.py:470
  37.5 0.0 copy-done.1
  37.5 0.0 copy-done.2
  37.6 0.0 copy-done.3
  37.6 1.2 %shard_map.90 = f32[1,2,512]{2,1,0:T(2,128)} custom-call(f32[3,128]{1,0:T(4,128)S(1)} %copy-done.2, bf16[128,128]{1,0:T(8,128)(2,1)S(1)} %copy-done.1, f32[2,128]{1,0:T(2,128)S(1)} %copy-done.3, f32[2,512]{1,0:T(2,128)S(1)} %get-tuple-element.11.place_ref, bf16[528,128]{1,0:T(8,128)(2,1)S(1)} %get-tuple-element.12.mine_ref, ...), custom_call_target="tpu_custom_call" | custom-call | flops 67108864 | bytes 524288 | tf_op jit(solution)/shard_map/pallas_call | solution.py:568
  (16 shorter events, 0.2 us)
Async XLA Ops:
  0.0 2.5 %copy-start.7 = (s32[512]{0:T(512)S(1)}, s32[512]{0:T(512)}, u32[]{:S(2)}) copy-start(s32[512]{0:T(512)} %param.11) | copy-start | bytes 6148
  0.0 2.5 %copy-start.8 = (s32[512]{0:T(512)S(1)}, s32[512]{0:T(512)}, u32[]{:S(2)}) copy-start(s32[512]{0:T(512)} %param.10) | copy-start | bytes 6148
  0.0 2.5 %copy-start.9 = (s32[512]{0:T(512)S(1)}, s32[512]{0:T(512)}, u32[]{:S(2)}) copy-start(s32[512]{0:T(512)} %param.9) | copy-start | bytes 6148
  0.0 2.5 %copy-start = (bf16[1,32,240,128]{3,2,1,0:T(8,128)(2,1)S(1)}, bf16[1,32,240,128]{3,2,1,0:T(8,128)(2,1)}, u32[]{:S(2)}) copy-start(bf16[1,32,240,128]{3,2,1,0:T(8,128)(2,1)} %param.8) | copy-start | bytes 5898244
  1.2 1.3 %copy-start.5 = (bf16[7680,128]{1,0:T(8,128)(2,1)}, bf16[7680,128]{1,0:T(8,128)(2,1)S(1)}, u32[]{:S(2)}) copy-start(bf16[7680,128]{1,0:T(8,128)(2,1)S(1)} %shard_map.82.coord_ref) | copy-start | bytes 5898244
  2.5 13.6 %copy-start.6 = (bf16[7680,128]{1,0:T(8,128)(2,1)S(1)}, bf16[7680,128]{1,0:T(8,128)(2,1)}, u32[]{:S(2)}) copy-start(bf16[7680,128]{1,0:T(8,128)(2,1)} %copy-done.5) | copy-start | bytes 5898244
  3.8 1.8 %collective-permute-start = (bf16[256,128]{1,0:T(8,128)(2,1)S(1)}, bf16[256,128]{1,0:T(8,128)(2,1)S(1)}, u32[]{:S(2)}, u32[]{:S(2)}) collective-permute-start(bf16[256,128]{1,0:T(8,128)(2,1)S(1)} %shard_map.84), channel_id=1, source_target_pairs={{0,4},{4,0},{1,5},{5,1},{2,6},{6,2},{3,7},{7,3},{8,12},{12,8},{9,1... | collective-permute-start | bytes 196616 | tf_op jit(solution)/shard_map/ppermute | solution.py:470
  5.6 4.9 %collective-permute-start.1 = (bf16[256,128]{1,0:T(8,128)(2,1)S(1)}, bf16[256,128]{1,0:T(8,128)(2,1)S(1)}, u32[]{:S(2)}, u32[]{:S(2)}) collective-permute-start(bf16[256,128]{1,0:T(8,128)(2,1)S(1)} %add.13), channel_id=1, source_target_pairs={{0,1},{1,0},{2,3},{3,2},{4,6},{5,7},{6,4},{7,5},{8,9},{9,8},{10,11... | collective-permute-start | bytes 196616 | tf_op jit(solution)/shard_map/ppermute | solution.py:481
  10.5 5.5 %collective-permute-start.2 = (bf16[256,128]{1,0:T(8,128)(2,1)S(1)}, bf16[256,128]{1,0:T(8,128)(2,1)S(1)}, u32[]{:S(2)}, u32[]{:S(2)}) collective-permute-start(bf16[256,128]{1,0:T(8,128)(2,1)S(1)} %add.14), channel_id=1, source_target_pairs={{0,2},{1,3},{2,0},{3,1},{4,5},{5,4},{6,7},{7,6},{8,10},{9,11},{10,... | collective-permute-start | bytes 196616 | tf_op jit(solution)/shard_map/ppermute | solution.py:481
  16.0 5.1 %collective-permute-start.5 = (bf16[256,128]{1,0:T(8,128)(2,1)S(1)}, bf16[256,128]{1,0:T(8,128)(2,1)S(1)}, u32[]{:S(2)}, u32[]{:S(2)}) collective-permute-start(bf16[256,128]{1,0:T(8,128)(2,1)S(1)} %add.15.query_ref), channel_id=1, source_target_pairs={{0,4},{4,0},{1,5},{5,1},{2,6},{6,2},{3,7},{7,3},{8,12},{12,8},{9,1... | collective-permute-start | bytes 196616 | tf_op jit(solution)/shard_map/ppermute | solution.py:470
  18.8 5.5 %collective-permute-start.3 = (f16[288,128]{1,0:T(8,128)(2,1)S(1)}, f16[288,128]{1,0:T(8,128)(2,1)S(1)}, u32[]{:S(2)}, u32[]{:S(2)}) collective-permute-start(f16[288,128]{1,0:T(8,128)(2,1)S(1)} %convert_element_type.36), channel_id=1, source_target_pairs={{0,1},{1,0},{2,3},{3,2},{4,6},{5,7},{6,4},{7,5},{8,9},{9,8},{10,11... | collective-permute-start | bytes 221192 | tf_op jit(solution)/shard_map/ppermute | solution.py:481
  23.8 11.9 %copy-start.4 = (f32[1,128]{1,0:T(1,128)S(1)}, f32[1,128]{1,0:T(1,128)}, u32[]{:S(2)}) copy-start(f32[1,128]{1,0:T(1,128)} %decay_ref.1) | copy-start | bytes 1540
  23.8 13.7 %copy-start.1 = (bf16[128,128]{1,0:T(8,128)(2,1)S(1)}, bf16[128,128]{1,0:T(8,128)(2,1)}, u32[]{:S(2)}) copy-start(bf16[128,128]{1,0:T(8,128)(2,1)} %pw_ref.1) | copy-start | bytes 98308
  23.8 13.7 %copy-start.2 = (f32[3,128]{1,0:T(4,128)S(1)}, f32[3,128]{1,0:T(4,128)}, u32[]{:S(2)}) copy-start(f32[3,128]{1,0:T(4,128)} %dw_ref.1) | copy-start | bytes 4612
  23.8 13.7 %copy-start.3 = (f32[2,128]{1,0:T(2,128)S(1)}, f32[2,128]{1,0:T(2,128)}, u32[]{:S(2)}) copy-start(f32[2,128]{1,0:T(2,128)} %ow_ref.1) | copy-start | bytes 3076
  23.9 6.2 %collective-permute-start.6 = (f16[288,128]{1,0:T(8,128)(2,1)S(1)}, f16[288,128]{1,0:T(8,128)(2,1)S(1)}, u32[]{:S(2)}, u32[]{:S(2)}) collective-permute-start(f16[288,128]{1,0:T(8,128)(2,1)S(1)} %convert_element_type.42), channel_id=1, source_target_pairs={{0,1},{1,0},{2,3},{3,2},{4,6},{5,7},{6,4},{7,5},{8,9},{9,8},{10,11... | collective-permute-start | bytes 221192 | tf_op jit(solution)/shard_map/ppermute | solution.py:481
  24.6 7.5 %collective-permute-start.4 = (f16[288,128]{1,0:T(8,128)(2,1)S(1)}, f16[288,128]{1,0:T(8,128)(2,1)S(1)}, u32[]{:S(2)}, u32[]{:S(2)}) collective-permute-start(f16[288,128]{1,0:T(8,128)(2,1)S(1)} %convert_element_type.39), channel_id=1, source_target_pairs={{0,2},{1,3},{2,0},{3,1},{4,5},{5,4},{6,7},{7,6},{8,10},{9,11},{10,... | collective-permute-start | bytes 221192 | tf_op jit(solution)/shard_map/ppermute | solution.py:481
  30.3 5.3 %collective-permute-start.7 = (f16[288,128]{1,0:T(8,128)(2,1)S(1)}, f16[288,128]{1,0:T(8,128)(2,1)S(1)}, u32[]{:S(2)}, u32[]{:S(2)}) collective-permute-start(f16[288,128]{1,0:T(8,128)(2,1)S(1)} %convert_element_type.45), channel_id=1, source_target_pairs={{0,2},{1,3},{2,0},{3,1},{4,5},{5,4},{6,7},{7,6},{8,10},{9,11},{10,... | collective-permute-start | bytes 221192 | tf_op jit(solution)/shard_map/ppermute | solution.py:481
  36.1 1.4 %collective-permute-start.8 = (bf16[528,128]{1,0:T(8,128)(2,1)S(1)}, bf16[528,128]{1,0:T(8,128)(2,1)S(1)}, u32[]{:S(2)}, u32[]{:S(2)}) collective-permute-start(bf16[528,128]{1,0:T(8,128)(2,1)S(1)} %get-tuple-element.12.mine_ref), channel_id=1, source_target_pairs={{0,4},{4,0},{1,5},{5,1},{2,6},{6,2},{3,7},{7,3},{8,12},{12,8},{9,1... | collective-permute-start | bytes 405512 | tf_op jit(solution)/shard_map/ppermute | solution.py:470

commit v8 on v4

--- a/solution.py
+++ b/solution.py
@@ -241,7 +241,7 @@
     factor = math.log2(math.e) / math.sqrt(channels)
     query = query_ref[...]
     first_row = (lax.axis_index("space") * rows_here).astype(F32)
-    chunk = pick_chunk(positions, 1280)
+    chunk = pick_chunk(positions, 2560)
 
     def score(base):
         keys = map_ref[base : base + chunk, :]
@@ -322,36 +322,31 @@
     store_block(out_ref, *merged(my_bit(step, n_space), own_ref, came_ref))
 
 
-def last_merge_kernel(n_space, step, decay_ref, near_own, near_came, far_own, far_came, *outs):
-    out_ref, place_ref = outs
-    bit = my_bit(step, n_space)
-    base = 0
-    for own_ref, came_ref in ((near_own, near_came), (far_own, far_came)):
-        feats, lines = merged(bit, own_ref, came_ref)
-        window = slice(base, base + feats.shape[0])
-        out_ref[window, :] = feats.astype(BF16)
-        place_ref[0:1, window] = lines[2]
-        place_ref[1:2, window] = lines[3]
-        base += feats.shape[0]
+def last_merge_kernel(n_space, step, decay_ref, own_ref, came_ref, out_ref, place_ref):
+    feats, lines = merged(my_bit(step, n_space), own_ref, came_ref)
+    out_ref[: feats.shape[0], :] = feats.astype(BF16)
+    place_ref[0:1, :] = lines[2]
+    place_ref[1:2, :] = lines[3]
     sub = lax.broadcasted_iota(jnp.int32, (PIECE_ROWS, LANES), 0)
     rows = jnp.zeros((PIECE_ROWS, LANES), F32)
     for index, piece in enumerate(split(decay_ref[...])):
         rows = jnp.where(sub == index, piece, rows)
-    out_ref[base:, :] = rows.astype(BF16)
-
-
-def track_kernel(dw_ref, pw_ref, ow_ref, place_ref, mine_ref, theirs_ref, out_ref):
+    out_ref[feats.shape[0] :, :] = rows.astype(BF16)
+
+
+def track_kernel(
+    dw_ref, pw_ref, ow_ref, near_place, far_place, near_mine, far_mine, near_came, far_came, out_ref
+):
     early = lax.axis_index("tm") == 0
-    queries = place_ref.shape[1]
-    half = queries // 2
-    mine, theirs = mine_ref[...].astype(F32), theirs_ref[...].astype(F32)
-
-    def retention(rows):
-        return rows[queries : queries + 1] + rows[queries + 1 : queries + 2] + rows[queries + 2 : queries + 3]
-
-    decay_mine, decay_theirs = retention(mine), retention(theirs)
-    mine = mine[:queries]
-    theirs = jnp.concatenate([theirs[half:queries], theirs[:half]], axis=0)
+    half = near_place.shape[1]
+
+    def retention(ref):
+        rows = ref[half:, :].astype(F32)
+        return rows[0:1] + rows[1:2] + rows[2:3]
+
+    decay_mine, decay_theirs = retention(near_mine), retention(near_came)
+    mine = jnp.concatenate([near_mine[:half, :], far_mine[:half, :]], axis=0).astype(F32)
+    theirs = jnp.concatenate([far_came[:half, :], near_came[:half, :]], axis=0).astype(F32)
     attended = [jnp.where(early, mine, theirs), jnp.where(early, theirs, mine)]
     decay = [
         jnp.where(early, decay_mine, decay_theirs),
@@ -372,10 +367,12 @@
     first = (1.0 - decay[0]) * refined[0]
     second = decay[1] * first + (1.0 - decay[1]) * refined[1]
     memory = jnp.where(early, first, second)
-    delta = lax.dot_general(
-        ow_ref[...], memory, NT, preferred_element_type=F32, precision=lax.Precision.HIGHEST
-    )
-    line = place_ref[...] + delta
+    n_out = ow_ref.shape[0]
+    weights = jnp.concatenate(split(ow_ref[...]), axis=0).astype(BF16)
+    line = jnp.concatenate([near_place[...], far_place[...]], axis=1)
+    for piece in split(memory)[:2]:
+        terms = lax.dot_general(weights, piece.astype(BF16), NT, preferred_element_type=F32)
+        line = line + terms[:n_out] + terms[n_out : 2 * n_out] + terms[2 * n_out :]
     low, high = line[:, :half], line[:, half:]
     out_ref[0, :, :half] = jnp.where(early, low, high)
     out_ref[0, :, half:] = jnp.where(early, high, low)
@@ -540,8 +537,8 @@
             functools.partial(merge_kernel, n_space, step),
             block,
             2,
-            flops=4 * half * channels,
-            bytes_accessed=12 * half * channels,
+            flops=0,
+            bytes_accessed=0,
             transcendentals=0,
         )(*pair)
 
@@ -550,25 +547,29 @@
         pairs = [sent(merge(pair, step - 1), step) for pair in pairs]
 
     n_out = out_weight.shape[0]
-    attended, place = call(
-        functools.partial(last_merge_kernel, n_space, steps - 1),
-        [
-            jax.ShapeDtypeStruct((queries + PIECE_ROWS, LANES), BF16),
-            jax.ShapeDtypeStruct((n_out, queries), F32),
-        ],
-        5,
-        flops=4 * queries * channels,
-        bytes_accessed=12 * queries * channels,
-        transcendentals=0,
-    )(ema_decay, *pairs[0], *pairs[1])
+    attended, places = [], []
+    for pair in pairs:
+        value, place = call(
+            functools.partial(last_merge_kernel, n_space, steps - 1),
+            [
+                jax.ShapeDtypeStruct((half + PIECE_ROWS, LANES), BF16),
+                jax.ShapeDtypeStruct((n_out, half), F32),
+            ],
+            3,
+            flops=0,
+            bytes_accessed=0,
+            transcendentals=0,
+        )(ema_decay, *pair)
+        attended.append(value)
+        places.append(place)
     return call(
         track_kernel,
         jax.ShapeDtypeStruct((1, n_out, queries), F32),
-        6,
+        9,
         flops=8 * queries * channels * channels,
         bytes_accessed=8 * queries * channels,
         transcendentals=2 * queries * channels,
-    )(dw_kernel, pw_weight, out_weight, place, attended, core_swap(attended))
+    )(dw_kernel, pw_weight, out_weight, *places, *attended, *[core_swap(v) for v in attended])
 
 
 def local(feature_maps, query_frame, *rest):

time: 40.6 us -> 38.3 us (0.943)
  waiting for transfers between devices: 13.8 us -> 10.7 us
  starting transfers between devices: 12.5 us -> 13.6 us
    ppermute x6, waiting for transfers between devices: 12.5 us -> 9.46 us  [space_swap(): return lax.ppermute(value, ('tm', 'space'), pairs)]
    ppermute x6, starting transfers between devices: 11.9 us -> 12.7 us  [space_swap(): return lax.ppermute(value, ('tm', 'space'), pairs)]
    ppermute x3 -> x4, starting transfers between devices: 0.66 us -> 0.89 us  [core_swap(): return lax.ppermute(value, 'tm', [(0, 1), (1, 0)])]
    ppermute x3 -> x4, waiting for transfers between devices: 1.35 us -> 1.24 us  [core_swap(): return lax.ppermute(value, 'tm', [(0, 1), (1, 0)])]
  transfers between devices with their start and end apart: 9 -> 10, of which waited for: 7 -> 6; matrix products, arithmetic and copies ran while one was open for 0% -> 0% of each run, Pallas kernels for 21% -> 23%
where the time goes in v8:
time: 38.3 us; the launch traced here: 38.1 us
  starting transfers between devices  13.6 us (36%)
  Pallas kernels  11.1 us (29%)
  waiting for transfers between devices  10.7 us (28%)
  local copies, waits for them, and re-layouts  1.58 us (4%)
  other arithmetic  0.93 us (2%)
    ppermute x6, starting transfers between devices, space_swap(): return lax.ppermute(value, ('tm', 'space'), pairs)  12.7 us
    ppermute x6, waiting for transfers between devices, space_swap(): return lax.ppermute(value, ('tm', 'space'), pairs)  9.46 us
    pallas_call x2, Pallas kernels, blocks_of(): call(functools.partial(half_kernel, rows_here, height, map_width), block,...  5.26 us
    pallas_call x2, Pallas kernels, pick(): call(functools.partial(pick_kernel, core_flip), jax.ShapeDtypeStruct((hal...  2.49 us
    unnamed x12, local copies, waits for them, and re-layouts  1.58 us
    ppermute x4, waiting for transfers between devices, core_swap(): return lax.ppermute(value, 'tm', [(0, 1), (1, 0)])  1.24 us
    pallas_call x1, Pallas kernels, local_pair(): call(functools.partial(coord_kernel, map_width), jax.ShapeDtypeStruct((po...  1.19 us
    pallas_call x1, Pallas kernels, local_pair(): call(track_kernel, jax.ShapeDtypeStruct((1, n_out, queries), F32), 9, flo...  1.16 us
  transfers between devices with their start and end apart: 10, of which 6 were waited for; matrix products, arithmetic and copies ran while one was open for 0% of the time, Pallas kernels for 23%

profile of v8, /device:TPU:0, one launch (start us, length us, event | category | flops | bytes accessed | tf_op | source)
XLA Modules:
  0.0 38.1 jit_solution(9798063746541377993)
XLA Ops:
  0.0 0.7 %add_select_fusion = s32[512]{0:T(512)S(1)} fusion(s32[512]{0:T(512)} %param.11, s32[512]{0:T(512)} %param.10, s32[512]{0:T(512)} %param.9, s32[]{:T(128)S(6)} %mul.9, s32[]{:T(128)S(6)} %axis_index.23), kind=kLoop, calls=%fused_computation | loop fusion | flops 4608 | bytes 8200 | tf_op jit(solution)/shard_map/jit(_where)/select_n | solution.py:492
  0.7 0.0 copy-start
  0.7 1.5 %copy-done = bf16[1,32,240,128]{3,2,1,0:T(8,128)(2,1)S(1)} copy-done((bf16[1,32,240,128]{3,2,1,0:T(8,128)(2,1)S(1)}, bf16[1,32,240,128]{3,2,1,0:T(8,128)(2,1)}, u32[]{:S(2)}) %copy-start) | copy-done | bytes 1966104
  2.3 1.2 %shard_map.83 = bf16[256,128]{1,0:T(8,128)(2,1)S(1)} custom-call(s32[1,512]{1,0:T(1,128)S(1)} %bitcast.6, bf16[7680,128]{1,0:T(8,128)(2,1)S(1)} %bitcast.2), custom_call_target="tpu_custom_call" | custom-call | flops 503316480 | bytes 1966080 | tf_op jit(solution)/shard_map/pallas_call | solution.py:495
  3.5 0.0 copy-start.1
  3.5 0.5 %collective-permute-start = (bf16[256,128]{1,0:T(8,128)(2,1)S(1)}, bf16[256,128]{1,0:T(8,128)(2,1)S(1)}, u32[]{:S(2)}, u32[]{:S(2)}) collective-permute-start(bf16[256,128]{1,0:T(8,128)(2,1)S(1)} %shard_map.83), channel_id=1, source_target_pairs={{0,4},{4,0},{1,5},{5,1},{2,6},{6,2},{3,7},{7,3},{8,12},{12,8},{9,1... | collective-permute-start | bytes 196616 | tf_op jit(solution)/shard_map/ppermute | solution.py:465
  4.0 1.2 %shard_map.82 = bf16[256,128]{1,0:T(8,128)(2,1)S(1)} custom-call(s32[1,512]{1,0:T(1,128)S(1)} %bitcast.7, bf16[7680,128]{1,0:T(8,128)(2,1)S(1)} %bitcast.3), custom_call_target="tpu_custom_call" | custom-call | flops 503316480 | bytes 1966080 | tf_op jit(solution)/shard_map/pallas_call | solution.py:495
  5.3 0.0 collective-permute-done
  5.3 2.6 %collective-permute-start.1 = (bf16[256,128]{1,0:T(8,128)(2,1)S(1)}, bf16[256,128]{1,0:T(8,128)(2,1)S(1)}, u32[]{:S(2)}, u32[]{:S(2)}) collective-permute-start(bf16[256,128]{1,0:T(8,128)(2,1)S(1)} %add.13), channel_id=1, source_target_pairs={{0,1},{1,0},{2,3},{3,2},{4,6},{5,7},{6,4},{7,5},{8,9},{9,8},{10,11... | collective-permute-start | bytes 196616 | tf_op jit(solution)/shard_map/ppermute | solution.py:476
  8.0 2.2 %collective-permute-done.1 = bf16[256,128]{1,0:T(8,128)(2,1)S(1)} collective-permute-done((bf16[256,128]{1,0:T(8,128)(2,1)S(1)}, bf16[256,128]{1,0:T(8,128)(2,1)S(1)}, u32[]{:S(2)}, u32[]{:S(2)}) %collective-permute-start.1) | collective-permute-done | bytes 65568 | tf_op jit(solution)/shard_map/ppermute | solution.py:476
  10.3 3.2 %collective-permute-start.2 = (bf16[256,128]{1,0:T(8,128)(2,1)S(1)}, bf16[256,128]{1,0:T(8,128)(2,1)S(1)}, u32[]{:S(2)}, u32[]{:S(2)}) collective-permute-start(bf16[256,128]{1,0:T(8,128)(2,1)S(1)} %add.14), channel_id=1, source_target_pairs={{0,2},{1,3},{2,0},{3,1},{4,5},{5,4},{6,7},{7,6},{8,10},{9,11},{10,... | collective-permute-start | bytes 196616 | tf_op jit(solution)/shard_map/ppermute | solution.py:476
  13.5 1.2 %shard_map.84.coord_ref = bf16[7680,128]{1,0:T(8,128)(2,1)S(1)} custom-call(s32[1,512]{1,0:T(1,128)S(1)} %bitcast.8), custom_call_target="tpu_custom_call" | custom-call | flops 7864320 | bytes 1966080 | tf_op jit(solution)/shard_map/pallas_call | solution.py:505
  14.7 1.1 %collective-permute-done.2 = bf16[256,128]{1,0:T(8,128)(2,1)S(1)} collective-permute-done((bf16[256,128]{1,0:T(8,128)(2,1)S(1)}, bf16[256,128]{1,0:T(8,128)(2,1)S(1)}, u32[]{:S(2)}, u32[]{:S(2)}) %collective-permute-start.2) | collective-permute-done | bytes 65568 | tf_op jit(solution)/shard_map/ppermute | solution.py:476
  15.7 0.1 collective-permute-start.5
  15.8 0.0 copy-done.1
  15.8 2.6 %shard_map.85 = f32[288,128]{1,0:T(8,128)S(1)} custom-call(bf16[256,128]{1,0:T(8,128)(2,1)S(1)} %add.15.query_ref, bf16[7680,128]{1,0:T(8,128)(2,1)S(1)} %bitcast.4, bf16[7680,128]{1,0:T(8,128)(2,1)S(1)} %shard_map.84.coord_ref), custom_call_target="tpu_custom_call" | custom-call | flops 1509949440 | bytes 3932160 | tf_op jit(solution)/shard_map/pallas_call | solution.py:522
  18.5 2.4 %collective-permute-start.3 = (f16[288,128]{1,0:T(8,128)(2,1)S(1)}, f16[288,128]{1,0:T(8,128)(2,1)S(1)}, u32[]{:S(2)}, u32[]{:S(2)}) collective-permute-start(f16[288,128]{1,0:T(8,128)(2,1)S(1)} %convert_element_type.36), channel_id=1, source_target_pairs={{0,1},{1,0},{2,3},{3,2},{4,6},{5,7},{6,4},{7,5},{8,9},{9,8},{10,11... | collective-permute-start | bytes 221192 | tf_op jit(solution)/shard_map/ppermute | solution.py:476
  20.9 0.0 collective-permute-done.5.query_ref
  20.9 2.6 %shard_map.88 = f32[288,128]{1,0:T(8,128)S(1)} custom-call(bf16[256,128]{1,0:T(8,128)(2,1)S(1)} %collective-permute-done.5.query_ref, bf16[7680,128]{1,0:T(8,128)(2,1)S(1)} %bitcast.5, bf16[7680,128]{1,0:T(8,128)(2,1)S(1)} %shard_map.84.coord_ref), custom_call_target="tpu_custom_call" | custom-call | flops 1509949440 | bytes 3932160 | tf_op jit(solution)/shard_map/pallas_call | solution.py:522
  23.5 0.0 copy-start.4
  23.5 0.0 copy-start.2
  23.6 0.0 copy-start.3
  23.6 0.0 copy-start.5
  23.6 0.1 collective-permute-start.6
  23.7 0.3 collective-permute-done.3
  24.0 0.3 shard_map.86
  24.3 2.6 %collective-permute-start.4 = (f16[288,128]{1,0:T(8,128)(2,1)S(1)}, f16[288,128]{1,0:T(8,128)(2,1)S(1)}, u32[]{:S(2)}, u32[]{:S(2)}) collective-permute-start(f16[288,128]{1,0:T(8,128)(2,1)S(1)} %convert_element_type.39), channel_id=1, source_target_pairs={{0,2},{1,3},{2,0},{3,1},{4,5},{5,4},{6,7},{7,6},{8,10},{9,11},{10,... | collective-permute-start | bytes 221192 | tf_op jit(solution)/shard_map/ppermute | solution.py:476
  26.9 2.8 %collective-permute-done.6 = f16[288,128]{1,0:T(8,128)(2,1)S(1)} collective-permute-done((f16[288,128]{1,0:T(8,128)(2,1)S(1)}, f16[288,128]{1,0:T(8,128)(2,1)S(1)}, u32[]{:S(2)}, u32[]{:S(2)}) %collective-permute-start.6) | collective-permute-done | bytes 73760 | tf_op jit(solution)/shard_map/ppermute | solution.py:476
  29.8 0.3 shard_map.89
  30.0 1.7 %collective-permute-start.7 = (f16[288,128]{1,0:T(8,128)(2,1)S(1)}, f16[288,128]{1,0:T(8,128)(2,1)S(1)}, u32[]{:S(2)}, u32[]{:S(2)}) collective-permute-start(f16[288,128]{1,0:T(8,128)(2,1)S(1)} %convert_element_type.45), channel_id=1, source_target_pairs={{0,2},{1,3},{2,0},{3,1},{4,5},{5,4},{6,7},{7,6},{8,10},{9,11},{10,... | collective-permute-start | bytes 221192 | tf_op jit(solution)/shard_map/ppermute | solution.py:476
  31.8 0.0 collective-permute-done.4
  31.8 0.0 copy-done.4
  31.8 0.3 shard_map.87
  32.1 0.2 collective-permute-start.8
  32.3 3.0 %collective-permute-done.7 = f16[288,128]{1,0:T(8,128)(2,1)S(1)} collective-permute-done((f16[288,128]{1,0:T(8,128)(2,1)S(1)}, f16[288,128]{1,0:T(8,128)(2,1)S(1)}, u32[]{:S(2)}, u32[]{:S(2)}) %collective-permute-start.7) | collective-permute-done | bytes 73760 | tf_op jit(solution)/shard_map/ppermute | solution.py:476
  35.4 0.3 shard_map.90
  35.6 0.1 collective-permute-start.9
  35.7 0.0 collective-permute-done.8.near_came
  35.7 1.2 %collective-permute-done.9.far_came = bf16[272,128]{1,0:T(8,128)(2,1)S(1)} collective-permute-done((bf16[272,128]{1,0:T(8,128)(2,1)S(1)}, bf16[272,128]{1,0:T(8,128)(2,1)S(1)}, u32[]{:S(2)}, u32[]{:S(2)}) %collective-permute-start.9) | collective-permute-done | bytes 69664 | tf_op jit(solution)/shard_map/ppermute | solution.py:465
  37.0 0.0 copy-done.2
  37.0 0.0 copy-done.3
  37.0 0.0 copy-done.5
  37.0 1.2 %shard_map.91 = f32[1,2,512]{2,1,0:T(2,128)} custom-call(f32[3,128]{1,0:T(4,128)S(1)} %copy-done.3, bf16[128,128]{1,0:T(8,128)(2,1)S(1)} %copy-done.2, f32[2,128]{1,0:T(2,128)S(1)} %copy-done.5, f32[2,256]{1,0:T(2,128)S(1)} %get-tuple-element.9.near_place, f32[2,256]{1,0:T(2,128)S(1)} %get-tuple-element.10.far_place, ...), custom_call_target="tpu_custom_call" | custom-call | flops 67108864 | bytes 524288 | tf_op jit(solution)/shard_map/pallas_call | solution.py:565
  (15 shorter events, 0.2 us)
Async XLA Ops:
  0.7 1.5 %copy-start = (bf16[1,32,240,128]{3,2,1,0:T(8,128)(2,1)S(1)}, bf16[1,32,240,128]{3,2,1,0:T(8,128)(2,1)}, u32[]{:S(2)}) copy-start(bf16[1,32,240,128]{3,2,1,0:T(8,128)(2,1)} %param.8) | copy-start | bytes 5898244
  3.5 12.3 %copy-start.1 = (bf16[1,32,240,128]{3,2,1,0:T(8,128)(2,1)S(1)}, bf16[1,32,240,128]{3,2,1,0:T(8,128)(2,1)}, u32[]{:S(2)}) copy-start(bf16[1,32,240,128]{3,2,1,0:T(8,128)(2,1)} %param.8) | copy-start | bytes 5898244
  3.5 1.8 %collective-permute-start = (bf16[256,128]{1,0:T(8,128)(2,1)S(1)}, bf16[256,128]{1,0:T(8,128)(2,1)S(1)}, u32[]{:S(2)}, u32[]{:S(2)}) collective-permute-start(bf16[256,128]{1,0:T(8,128)(2,1)S(1)} %shard_map.83), channel_id=1, source_target_pairs={{0,4},{4,0},{1,5},{5,1},{2,6},{6,2},{3,7},{7,3},{8,12},{12,8},{9,1... | collective-permute-start | bytes 196616 | tf_op jit(solution)/shard_map/ppermute | solution.py:465
  5.3 4.9 %collective-permute-start.1 = (bf16[256,128]{1,0:T(8,128)(2,1)S(1)}, bf16[256,128]{1,0:T(8,128)(2,1)S(1)}, u32[]{:S(2)}, u32[]{:S(2)}) collective-permute-start(bf16[256,128]{1,0:T(8,128)(2,1)S(1)} %add.13), channel_id=1, source_target_pairs={{0,1},{1,0},{2,3},{3,2},{4,6},{5,7},{6,4},{7,5},{8,9},{9,8},{10,11... | collective-permute-start | bytes 196616 | tf_op jit(solution)/shard_map/ppermute | solution.py:476
  10.3 5.5 %collective-permute-start.2 = (bf16[256,128]{1,0:T(8,128)(2,1)S(1)}, bf16[256,128]{1,0:T(8,128)(2,1)S(1)}, u32[]{:S(2)}, u32[]{:S(2)}) collective-permute-start(bf16[256,128]{1,0:T(8,128)(2,1)S(1)} %add.14), channel_id=1, source_target_pairs={{0,2},{1,3},{2,0},{3,1},{4,5},{5,4},{6,7},{7,6},{8,10},{9,11},{10,... | collective-permute-start | bytes 196616 | tf_op jit(solution)/shard_map/ppermute | solution.py:476
  15.7 5.1 %collective-permute-start.5 = (bf16[256,128]{1,0:T(8,128)(2,1)S(1)}, bf16[256,128]{1,0:T(8,128)(2,1)S(1)}, u32[]{:S(2)}, u32[]{:S(2)}) collective-permute-start(bf16[256,128]{1,0:T(8,128)(2,1)S(1)} %add.15.query_ref), channel_id=1, source_target_pairs={{0,4},{4,0},{1,5},{5,1},{2,6},{6,2},{3,7},{7,3},{8,12},{12,8},{9,1... | collective-permute-start | bytes 196616 | tf_op jit(solution)/shard_map/ppermute | solution.py:465
  18.5 5.5 %collective-permute-start.3 = (f16[288,128]{1,0:T(8,128)(2,1)S(1)}, f16[288,128]{1,0:T(8,128)(2,1)S(1)}, u32[]{:S(2)}, u32[]{:S(2)}) collective-permute-start(f16[288,128]{1,0:T(8,128)(2,1)S(1)} %convert_element_type.36), channel_id=1, source_target_pairs={{0,1},{1,0},{2,3},{3,2},{4,6},{5,7},{6,4},{7,5},{8,9},{9,8},{10,11... | collective-permute-start | bytes 221192 | tf_op jit(solution)/shard_map/ppermute | solution.py:476
  23.5 8.3 %copy-start.4 = (f32[1,128]{1,0:T(1,128)S(1)}, f32[1,128]{1,0:T(1,128)}, u32[]{:S(2)}) copy-start(f32[1,128]{1,0:T(1,128)} %decay_ref.3) | copy-start | bytes 1540
  23.5 13.4 %copy-start.2 = (bf16[128,128]{1,0:T(8,128)(2,1)S(1)}, bf16[128,128]{1,0:T(8,128)(2,1)}, u32[]{:S(2)}) copy-start(bf16[128,128]{1,0:T(8,128)(2,1)} %pw_ref.1) | copy-start | bytes 98308
  23.6 13.4 %copy-start.3 = (f32[3,128]{1,0:T(4,128)S(1)}, f32[3,128]{1,0:T(4,128)}, u32[]{:S(2)}) copy-start(f32[3,128]{1,0:T(4,128)} %dw_ref.1) | copy-start | bytes 4612
  23.6 13.4 %copy-start.5 = (f32[2,128]{1,0:T(2,128)S(1)}, f32[2,128]{1,0:T(2,128)}, u32[]{:S(2)}) copy-start(f32[2,128]{1,0:T(2,128)} %ow_ref.1) | copy-start | bytes 3076
  23.6 6.2 %collective-permute-start.6 = (f16[288,128]{1,0:T(8,128)(2,1)S(1)}, f16[288,128]{1,0:T(8,128)(2,1)S(1)}, u32[]{:S(2)}, u32[]{:S(2)}) collective-permute-start(f16[288,128]{1,0:T(8,128)(2,1)S(1)} %convert_element_type.42), channel_id=1, source_target_pairs={{0,1},{1,0},{2,3},{3,2},{4,6},{5,7},{6,4},{7,5},{8,9},{9,8},{10,11... | collective-permute-start | bytes 221192 | tf_op jit(solution)/shard_map/ppermute | solution.py:476
  24.3 7.5 %collective-permute-start.4 = (f16[288,128]{1,0:T(8,128)(2,1)S(1)}, f16[288,128]{1,0:T(8,128)(2,1)S(1)}, u32[]{:S(2)}, u32[]{:S(2)}) collective-permute-start(f16[288,128]{1,0:T(8,128)(2,1)S(1)} %convert_element_type.39), channel_id=1, source_target_pairs={{0,2},{1,3},{2,0},{3,1},{4,5},{5,4},{6,7},{7,6},{8,10},{9,11},{10,... | collective-permute-start | bytes 221192 | tf_op jit(solution)/shard_map/ppermute | solution.py:476
  30.0 5.3 %collective-permute-start.7 = (f16[288,128]{1,0:T(8,128)(2,1)S(1)}, f16[288,128]{1,0:T(8,128)(2,1)S(1)}, u32[]{:S(2)}, u32[]{:S(2)}) collective-permute-start(f16[288,128]{1,0:T(8,128)(2,1)S(1)} %convert_element_type.45), channel_id=1, source_target_pairs={{0,2},{1,3},{2,0},{3,1},{4,5},{5,4},{6,7},{7,6},{8,10},{9,11},{10,... | collective-permute-start | bytes 221192 | tf_op jit(solution)/shard_map/ppermute | solution.py:476
  32.1 3.6 %collective-permute-start.8 = (bf16[272,128]{1,0:T(8,128)(2,1)S(1)}, bf16[272,128]{1,0:T(8,128)(2,1)S(1)}, u32[]{:S(2)}, u32[]{:S(2)}) collective-permute-start(bf16[272,128]{1,0:T(8,128)(2,1)S(1)} %get-tuple-element.11.near_mine), channel_id=1, source_target_pairs={{0,4},{4,0},{1,5},{5,1},{2,6},{6,2},{3,7},{7,3},{8,12},{12,8},{9,1... | collective-permute-start | bytes 208904 | tf_op jit(solution)/shard_map/ppermute | solution.py:465
  35.6 1.3 %collective-permute-start.9 = (bf16[272,128]{1,0:T(8,128)(2,1)S(1)}, bf16[272,128]{1,0:T(8,128)(2,1)S(1)}, u32[]{:S(2)}, u32[]{:S(2)}) collective-permute-start(bf16[272,128]{1,0:T(8,128)(2,1)S(1)} %get-tuple-element.12.far_mine), channel_id=1, source_target_pairs={{0,4},{4,0},{1,5},{5,1},{2,6},{6,2},{3,7},{7,3},{8,12},{12,8},{9,1... | collective-permute-start | bytes 208904 | tf_op jit(solution)/shard_map/ppermute | solution.py:465

commit v9 on v8

--- a/solution.py
+++ b/solution.py
@@ -188,27 +188,26 @@
     )
 
 
-def hot_rows(target, map_ref, base, chunk):
-    rows = target.shape[0]
-    lane = lax.broadcasted_iota(jnp.int32, (rows, LANES), 1)
-    parts = []
-    for lane_base in range(base, base + chunk, LANES):
-        parts.append(jnp.where(lane + lane_base == target, 1.0, 0.0).astype(BF16))
-    hot = jnp.concatenate(parts, axis=1)
-    return jnp.dot(hot, map_ref[base : base + chunk, :], preferred_element_type=F32)
-
-
 def pick_kernel(core_flip, target_ref, map_ref, out_ref):
     half = target_ref.shape[1] // 2
-    positions = map_ref.shape[0]
-    chunk = pick_chunk(positions, 1536)
+    positions, channels = map_ref.shape
+    size = pick_chunk(positions, 256)
     second = lax.axis_index("tm") != core_flip
     target = jnp.where(second, target_ref[:, half:], target_ref[:, :half])
-    target = jnp.transpose(jnp.broadcast_to(target, (LANES, half)))
-    picked = None
-    for base in range(0, positions, chunk):
-        term = hot_rows(target, map_ref, base, chunk)
-        picked = term if picked is None else picked + term
+    tile = jnp.where(target < 0, -1, target // size)
+    place = target - tile * size
+    tile = jnp.transpose(jnp.broadcast_to(tile, (channels, half)))
+    place = jnp.transpose(jnp.broadcast_to(place, (LANES, half)))
+    lane = lax.broadcasted_iota(jnp.int32, (half, LANES), 1)
+    parts = [
+        jnp.where(lane + base == place, 1.0, 0.0).astype(BF16) for base in range(0, size, LANES)
+    ]
+    hot = jnp.concatenate(parts, axis=1)
+    picked = jnp.zeros((half, channels), F32)
+    for index in range(positions // size):
+        keys = map_ref[index * size : (index + 1) * size, :]
+        rows = jnp.dot(hot, keys, preferred_element_type=F32)
+        picked = jnp.where(tile == index, rows, picked)
     out_ref[...] = picked.astype(BF16)
 
 
@@ -262,7 +261,7 @@
         terms = jnp.dot(weights, values, preferred_element_type=F32)
         sums = terms if sums is None else terms + jnp.exp2(top - new_top) * sums
         top = new_top
-    feats = sums[:, :channels] / sums[:, channels + 2 : channels + 3]
+    feats = sums[:, :channels] * (1.0 / sums[:, channels + 2 : channels + 3])
     extra = sums[:, channels:]
     lane = lax.broadcasted_iota(jnp.int32, extra.shape, 1)
     extra = jnp.transpose(jnp.where(lane == 3, top, extra))

time: 38.3 us -> 38.4 us (level)
  no operation moved by 1% of the time
where the time goes in v9:
time: 38.4 us; the launch traced here: 38.2 us
  starting transfers between devices  13.6 us (35%)
  Pallas kernels  11.2 us (29%)
  waiting for transfers between devices  10.7 us (28%)
  local copies, waits for them, and re-layouts  1.58 us (4%)
  other arithmetic  0.93 us (2%)
    ppermute x6, starting transfers between devices, space_swap(): return lax.ppermute(value, ('tm', 'space'), pairs)  12.7 us
    ppermute x6, waiting for transfers between devices, space_swap(): return lax.ppermute(value, ('tm', 'space'), pairs)  9.45 us
    pallas_call x2, Pallas kernels, blocks_of(): call(functools.partial(half_kernel, rows_here, height, map_width), block,...  5.27 us
    pallas_call x2, Pallas kernels, pick(): call(functools.partial(pick_kernel, core_flip), jax.ShapeDtypeStruct((hal...  2.57 us
    unnamed x12, local copies, waits for them, and re-layouts  1.58 us
    ppermute x4, waiting for transfers between devices, core_swap(): return lax.ppermute(value, 'tm', [(0, 1), (1, 0)])  1.24 us
    pallas_call x1, Pallas kernels, local_pair(): call(functools.partial(coord_kernel, map_width), jax.ShapeDtypeStruct((po...  1.19 us
    pallas_call x1, Pallas kernels, local_pair(): call(track_kernel, jax.ShapeDtypeStruct((1, n_out, queries), F32), 9, flo...  1.16 us
  transfers between devices with their start and end apart: 10, of which 6 were waited for; matrix products, arithmetic and copies ran while one was open for 0% of the time, Pallas kernels for 23%

profile of v9, /device:TPU:0, one launch (start us, length us, event | category | flops | bytes accessed | tf_op | source)
XLA Modules:
  0.0 38.2 jit_solution(5058271298847553308)
XLA Ops:
  0.0 0.7 %add_select_fusion = s32[512]{0:T(512)S(1)} fusion(s32[512]{0:T(512)} %param.11, s32[512]{0:T(512)} %param.10, s32[512]{0:T(512)} %param.9, s32[]{:T(128)S(6)} %mul.9, s32[]{:T(128)S(6)} %axis_index.23), kind=kLoop, calls=%fused_computation | loop fusion | flops 4608 | bytes 8200 | tf_op jit(solution)/shard_map/jit(_where)/select_n | solution.py:491
  0.7 0.0 copy-start
  0.7 1.5 %copy-done = bf16[1,32,240,128]{3,2,1,0:T(8,128)(2,1)S(1)} copy-done((bf16[1,32,240,128]{3,2,1,0:T(8,128)(2,1)S(1)}, bf16[1,32,240,128]{3,2,1,0:T(8,128)(2,1)}, u32[]{:S(2)}) %copy-start) | copy-done | bytes 1966104
  2.3 1.3 %shard_map.83 = bf16[256,128]{1,0:T(8,128)(2,1)S(1)} custom-call(s32[1,512]{1,0:T(1,128)S(1)} %bitcast.6, bf16[7680,128]{1,0:T(8,128)(2,1)S(1)} %bitcast.2), custom_call_target="tpu_custom_call" | custom-call | flops 503316480 | bytes 1966080 | tf_op jit(solution)/shard_map/pallas_call | solution.py:494
  3.6 0.0 copy-start.1
  3.6 0.5 %collective-permute-start = (bf16[256,128]{1,0:T(8,128)(2,1)S(1)}, bf16[256,128]{1,0:T(8,128)(2,1)S(1)}, u32[]{:S(2)}, u32[]{:S(2)}) collective-permute-start(bf16[256,128]{1,0:T(8,128)(2,1)S(1)} %shard_map.83), channel_id=1, source_target_pairs={{0,4},{4,0},{1,5},{5,1},{2,6},{6,2},{3,7},{7,3},{8,12},{12,8},{9,1... | collective-permute-start | bytes 196616 | tf_op jit(solution)/shard_map/ppermute | solution.py:464
  4.1 1.3 %shard_map.82 = bf16[256,128]{1,0:T(8,128)(2,1)S(1)} custom-call(s32[1,512]{1,0:T(1,128)S(1)} %bitcast.7, bf16[7680,128]{1,0:T(8,128)(2,1)S(1)} %bitcast.3), custom_call_target="tpu_custom_call" | custom-call | flops 503316480 | bytes 1966080 | tf_op jit(solution)/shard_map/pallas_call | solution.py:494
  5.4 0.0 collective-permute-done
  5.4 2.7 %collective-permute-start.1 = (bf16[256,128]{1,0:T(8,128)(2,1)S(1)}, bf16[256,128]{1,0:T(8,128)(2,1)S(1)}, u32[]{:S(2)}, u32[]{:S(2)}) collective-permute-start(bf16[256,128]{1,0:T(8,128)(2,1)S(1)} %add.13), channel_id=1, source_target_pairs={{0,1},{1,0},{2,3},{3,2},{4,6},{5,7},{6,4},{7,5},{8,9},{9,8},{10,11... | collective-permute-start | bytes 196616 | tf_op jit(solution)/shard_map/ppermute | solution.py:475
  8.1 2.2 %collective-permute-done.1 = bf16[256,128]{1,0:T(8,128)(2,1)S(1)} collective-permute-done((bf16[256,128]{1,0:T(8,128)(2,1)S(1)}, bf16[256,128]{1,0:T(8,128)(2,1)S(1)}, u32[]{:S(2)}, u32[]{:S(2)}) %collective-permute-start.1) | collective-permute-done | bytes 65568 | tf_op jit(solution)/shard_map/ppermute | solution.py:475
  10.3 3.2 %collective-permute-start.2 = (bf16[256,128]{1,0:T(8,128)(2,1)S(1)}, bf16[256,128]{1,0:T(8,128)(2,1)S(1)}, u32[]{:S(2)}, u32[]{:S(2)}) collective-permute-start(bf16[256,128]{1,0:T(8,128)(2,1)S(1)} %add.14), channel_id=1, source_target_pairs={{0,2},{1,3},{2,0},{3,1},{4,5},{5,4},{6,7},{7,6},{8,10},{9,11},{10,... | collective-permute-start | bytes 196616 | tf_op jit(solution)/shard_map/ppermute | solution.py:475
  13.6 1.2 %shard_map.84.coord_ref = bf16[7680,128]{1,0:T(8,128)(2,1)S(1)} custom-call(s32[1,512]{1,0:T(1,128)S(1)} %bitcast.8), custom_call_target="tpu_custom_call" | custom-call | flops 7864320 | bytes 1966080 | tf_op jit(solution)/shard_map/pallas_call | solution.py:504
  14.7 1.1 %collective-permute-done.2 = bf16[256,128]{1,0:T(8,128)(2,1)S(1)} collective-permute-done((bf16[256,128]{1,0:T(8,128)(2,1)S(1)}, bf16[256,128]{1,0:T(8,128)(2,1)S(1)}, u32[]{:S(2)}, u32[]{:S(2)}) %collective-permute-start.2) | collective-permute-done | bytes 65568 | tf_op jit(solution)/shard_map/ppermute | solution.py:475
  15.8 0.1 collective-permute-start.5
  15.9 0.0 copy-done.1
  15.9 2.6 %shard_map.85 = f32[288,128]{1,0:T(8,128)S(1)} custom-call(bf16[256,128]{1,0:T(8,128)(2,1)S(1)} %add.15.query_ref, bf16[7680,128]{1,0:T(8,128)(2,1)S(1)} %bitcast.4, bf16[7680,128]{1,0:T(8,128)(2,1)S(1)} %shard_map.84.coord_ref), custom_call_target="tpu_custom_call" | custom-call | flops 1509949440 | bytes 3932160 | tf_op jit(solution)/shard_map/pallas_call | solution.py:521
  18.6 2.4 %collective-permute-start.3 = (f16[288,128]{1,0:T(8,128)(2,1)S(1)}, f16[288,128]{1,0:T(8,128)(2,1)S(1)}, u32[]{:S(2)}, u32[]{:S(2)}) collective-permute-start(f16[288,128]{1,0:T(8,128)(2,1)S(1)} %convert_element_type.36), channel_id=1, source_target_pairs={{0,1},{1,0},{2,3},{3,2},{4,6},{5,7},{6,4},{7,5},{8,9},{9,8},{10,11... | collective-permute-start | bytes 221192 | tf_op jit(solution)/shard_map/ppermute | solution.py:475
  21.0 0.0 collective-permute-done.5.query_ref
  21.0 2.6 %shard_map.88 = f32[288,128]{1,0:T(8,128)S(1)} custom-call(bf16[256,128]{1,0:T(8,128)(2,1)S(1)} %collective-permute-done.5.query_ref, bf16[7680,128]{1,0:T(8,128)(2,1)S(1)} %bitcast.5, bf16[7680,128]{1,0:T(8,128)(2,1)S(1)} %shard_map.84.coord_ref), custom_call_target="tpu_custom_call" | custom-call | flops 1509949440 | bytes 3932160 | tf_op jit(solution)/shard_map/pallas_call | solution.py:521
  23.6 0.0 copy-start.4
  23.6 0.0 copy-start.2
  23.6 0.0 copy-start.3
  23.7 0.0 copy-start.5
  23.7 0.1 collective-permute-start.6
  23.8 0.3 collective-permute-done.3
  24.1 0.3 shard_map.86
  24.4 2.6 %collective-permute-start.4 = (f16[288,128]{1,0:T(8,128)(2,1)S(1)}, f16[288,128]{1,0:T(8,128)(2,1)S(1)}, u32[]{:S(2)}, u32[]{:S(2)}) collective-permute-start(f16[288,128]{1,0:T(8,128)(2,1)S(1)} %convert_element_type.39), channel_id=1, source_target_pairs={{0,2},{1,3},{2,0},{3,1},{4,5},{5,4},{6,7},{7,6},{8,10},{9,11},{10,... | collective-permute-start | bytes 221192 | tf_op jit(solution)/shard_map/ppermute | solution.py:475
  27.0 2.8 %collective-permute-done.6 = f16[288,128]{1,0:T(8,128)(2,1)S(1)} collective-permute-done((f16[288,128]{1,0:T(8,128)(2,1)S(1)}, f16[288,128]{1,0:T(8,128)(2,1)S(1)}, u32[]{:S(2)}, u32[]{:S(2)}) %collective-permute-start.6) | collective-permute-done | bytes 73760 | tf_op jit(solution)/shard_map/ppermute | solution.py:475
  29.8 0.3 shard_map.89
  30.1 1.7 %collective-permute-start.7 = (f16[288,128]{1,0:T(8,128)(2,1)S(1)}, f16[288,128]{1,0:T(8,128)(2,1)S(1)}, u32[]{:S(2)}, u32[]{:S(2)}) collective-permute-start(f16[288,128]{1,0:T(8,128)(2,1)S(1)} %convert_element_type.45), channel_id=1, source_target_pairs={{0,2},{1,3},{2,0},{3,1},{4,5},{5,4},{6,7},{7,6},{8,10},{9,11},{10,... | collective-permute-start | bytes 221192 | tf_op jit(solution)/shard_map/ppermute | solution.py:475
  31.9 0.0 collective-permute-done.4
  31.9 0.0 copy-done.4
  31.9 0.3 shard_map.87
  32.2 0.2 collective-permute-start.8
  32.4 3.0 %collective-permute-done.7 = f16[288,128]{1,0:T(8,128)(2,1)S(1)} collective-permute-done((f16[288,128]{1,0:T(8,128)(2,1)S(1)}, f16[288,128]{1,0:T(8,128)(2,1)S(1)}, u32[]{:S(2)}, u32[]{:S(2)}) %collective-permute-start.7) | collective-permute-done | bytes 73760 | tf_op jit(solution)/shard_map/ppermute | solution.py:475
  35.5 0.3 shard_map.90
  35.7 0.1 collective-permute-start.9
  35.8 0.0 collective-permute-done.8.near_came
  35.8 1.2 %collective-permute-done.9.far_came = bf16[272,128]{1,0:T(8,128)(2,1)S(1)} collective-permute-done((bf16[272,128]{1,0:T(8,128)(2,1)S(1)}, bf16[272,128]{1,0:T(8,128)(2,1)S(1)}, u32[]{:S(2)}, u32[]{:S(2)}) %collective-permute-start.9) | collective-permute-done | bytes 69664 | tf_op jit(solution)/shard_map/ppermute | solution.py:464
  37.0 0.0 copy-done.2
  37.0 0.0 copy-done.3
  37.0 0.0 copy-done.5
  37.1 1.2 %shard_map.91 = f32[1,2,512]{2,1,0:T(2,128)} custom-call(f32[3,128]{1,0:T(4,128)S(1)} %copy-done.3, bf16[128,128]{1,0:T(8,128)(2,1)S(1)} %copy-done.2, f32[2,128]{1,0:T(2,128)S(1)} %copy-done.5, f32[2,256]{1,0:T(2,128)S(1)} %get-tuple-element.9.near_place, f32[2,256]{1,0:T(2,128)S(1)} %get-tuple-element.10.far_place, ...), custom_call_target="tpu_custom_call" | custom-call | flops 67108864 | bytes 524288 | tf_op jit(solution)/shard_map/pallas_call | solution.py:564
  (15 shorter events, 0.2 us)
Async XLA Ops:
  0.7 1.5 %copy-start = (bf16[1,32,240,128]{3,2,1,0:T(8,128)(2,1)S(1)}, bf16[1,32,240,128]{3,2,1,0:T(8,128)(2,1)}, u32[]{:S(2)}) copy-start(bf16[1,32,240,128]{3,2,1,0:T(8,128)(2,1)} %param.8) | copy-start | bytes 5898244
  3.6 12.3 %copy-start.1 = (bf16[1,32,240,128]{3,2,1,0:T(8,128)(2,1)S(1)}, bf16[1,32,240,128]{3,2,1,0:T(8,128)(2,1)}, u32[]{:S(2)}) copy-start(bf16[1,32,240,128]{3,2,1,0:T(8,128)(2,1)} %param.8) | copy-start | bytes 5898244
  3.6 1.8 %collective-permute-start = (bf16[256,128]{1,0:T(8,128)(2,1)S(1)}, bf16[256,128]{1,0:T(8,128)(2,1)S(1)}, u32[]{:S(2)}, u32[]{:S(2)}) collective-permute-start(bf16[256,128]{1,0:T(8,128)(2,1)S(1)} %shard_map.83), channel_id=1, source_target_pairs={{0,4},{4,0},{1,5},{5,1},{2,6},{6,2},{3,7},{7,3},{8,12},{12,8},{9,1... | collective-permute-start | bytes 196616 | tf_op jit(solution)/shard_map/ppermute | solution.py:464
  5.4 4.9 %collective-permute-start.1 = (bf16[256,128]{1,0:T(8,128)(2,1)S(1)}, bf16[256,128]{1,0:T(8,128)(2,1)S(1)}, u32[]{:S(2)}, u32[]{:S(2)}) collective-permute-start(bf16[256,128]{1,0:T(8,128)(2,1)S(1)} %add.13), channel_id=1, source_target_pairs={{0,1},{1,0},{2,3},{3,2},{4,6},{5,7},{6,4},{7,5},{8,9},{9,8},{10,11... | collective-permute-start | bytes 196616 | tf_op jit(solution)/shard_map/ppermute | solution.py:475
  10.3 5.5 %collective-permute-start.2 = (bf16[256,128]{1,0:T(8,128)(2,1)S(1)}, bf16[256,128]{1,0:T(8,128)(2,1)S(1)}, u32[]{:S(2)}, u32[]{:S(2)}) collective-permute-start(bf16[256,128]{1,0:T(8,128)(2,1)S(1)} %add.14), channel_id=1, source_target_pairs={{0,2},{1,3},{2,0},{3,1},{4,5},{5,4},{6,7},{7,6},{8,10},{9,11},{10,... | collective-permute-start | bytes 196616 | tf_op jit(solution)/shard_map/ppermute | solution.py:475
  15.8 5.2 %collective-permute-start.5 = (bf16[256,128]{1,0:T(8,128)(2,1)S(1)}, bf16[256,128]{1,0:T(8,128)(2,1)S(1)}, u32[]{:S(2)}, u32[]{:S(2)}) collective-permute-start(bf16[256,128]{1,0:T(8,128)(2,1)S(1)} %add.15.query_ref), channel_id=1, source_target_pairs={{0,4},{4,0},{1,5},{5,1},{2,6},{6,2},{3,7},{7,3},{8,12},{12,8},{9,1... | collective-permute-start | bytes 196616 | tf_op jit(solution)/shard_map/ppermute | solution.py:464
  18.6 5.5 %collective-permute-start.3 = (f16[288,128]{1,0:T(8,128)(2,1)S(1)}, f16[288,128]{1,0:T(8,128)(2,1)S(1)}, u32[]{:S(2)}, u32[]{:S(2)}) collective-permute-start(f16[288,128]{1,0:T(8,128)(2,1)S(1)} %convert_element_type.36), channel_id=1, source_target_pairs={{0,1},{1,0},{2,3},{3,2},{4,6},{5,7},{6,4},{7,5},{8,9},{9,8},{10,11... | collective-permute-start | bytes 221192 | tf_op jit(solution)/shard_map/ppermute | solution.py:475
  23.6 8.3 %copy-start.4 = (f32[1,128]{1,0:T(1,128)S(1)}, f32[1,128]{1,0:T(1,128)}, u32[]{:S(2)}) copy-start(f32[1,128]{1,0:T(1,128)} %decay_ref.3) | copy-start | bytes 1540
  23.6 13.4 %copy-start.2 = (bf16[128,128]{1,0:T(8,128)(2,1)S(1)}, bf16[128,128]{1,0:T(8,128)(2,1)}, u32[]{:S(2)}) copy-start(bf16[128,128]{1,0:T(8,128)(2,1)} %pw_ref.1) | copy-start | bytes 98308
  23.6 13.4 %copy-start.3 = (f32[3,128]{1,0:T(4,128)S(1)}, f32[3,128]{1,0:T(4,128)}, u32[]{:S(2)}) copy-start(f32[3,128]{1,0:T(4,128)} %dw_ref.1) | copy-start | bytes 4612
  23.7 13.4 %copy-start.5 = (f32[2,128]{1,0:T(2,128)S(1)}, f32[2,128]{1,0:T(2,128)}, u32[]{:S(2)}) copy-start(f32[2,128]{1,0:T(2,128)} %ow_ref.1) | copy-start | bytes 3076
  23.7 6.1 %collective-permute-start.6 = (f16[288,128]{1,0:T(8,128)(2,1)S(1)}, f16[288,128]{1,0:T(8,128)(2,1)S(1)}, u32[]{:S(2)}, u32[]{:S(2)}) collective-permute-start(f16[288,128]{1,0:T(8,128)(2,1)S(1)} %convert_element_type.42), channel_id=1, source_target_pairs={{0,1},{1,0},{2,3},{3,2},{4,6},{5,7},{6,4},{7,5},{8,9},{9,8},{10,11... | collective-permute-start | bytes 221192 | tf_op jit(solution)/shard_map/ppermute | solution.py:475
  24.4 7.5 %collective-permute-start.4 = (f16[288,128]{1,0:T(8,128)(2,1)S(1)}, f16[288,128]{1,0:T(8,128)(2,1)S(1)}, u32[]{:S(2)}, u32[]{:S(2)}) collective-permute-start(f16[288,128]{1,0:T(8,128)(2,1)S(1)} %convert_element_type.39), channel_id=1, source_target_pairs={{0,2},{1,3},{2,0},{3,1},{4,5},{5,4},{6,7},{7,6},{8,10},{9,11},{10,... | collective-permute-start | bytes 221192 | tf_op jit(solution)/shard_map/ppermute | solution.py:475
  30.1 5.3 %collective-permute-start.7 = (f16[288,128]{1,0:T(8,128)(2,1)S(1)}, f16[288,128]{1,0:T(8,128)(2,1)S(1)}, u32[]{:S(2)}, u32[]{:S(2)}) collective-permute-start(f16[288,128]{1,0:T(8,128)(2,1)S(1)} %convert_element_type.45), channel_id=1, source_target_pairs={{0,2},{1,3},{2,0},{3,1},{4,5},{5,4},{6,7},{7,6},{8,10},{9,11},{10,... | collective-permute-start | bytes 221192 | tf_op jit(solution)/shard_map/ppermute | solution.py:475
  32.2 3.6 %collective-permute-start.8 = (bf16[272,128]{1,0:T(8,128)(2,1)S(1)}, bf16[272,128]{1,0:T(8,128)(2,1)S(1)}, u32[]{:S(2)}, u32[]{:S(2)}) collective-permute-start(bf16[272,128]{1,0:T(8,128)(2,1)S(1)} %get-tuple-element.11.near_mine), channel_id=1, source_target_pairs={{0,4},{4,0},{1,5},{5,1},{2,6},{6,2},{3,7},{7,3},{8,12},{12,8},{9,1... | collective-permute-start | bytes 208904 | tf_op jit(solution)/shard_map/ppermute | solution.py:464
  35.7 1.3 %collective-permute-start.9 = (bf16[272,128]{1,0:T(8,128)(2,1)S(1)}, bf16[272,128]{1,0:T(8,128)(2,1)S(1)}, u32[]{:S(2)}, u32[]{:S(2)}) collective-permute-start(bf16[272,128]{1,0:T(8,128)(2,1)S(1)} %get-tuple-element.12.far_mine), channel_id=1, source_target_pairs={{0,4},{4,0},{1,5},{5,1},{2,6},{6,2},{3,7},{7,3},{8,12},{12,8},{9,1... | collective-permute-start | bytes 208904 | tf_op jit(solution)/shard_map/ppermute | solution.py:464

commit v10 on v9

--- a/solution.py
+++ b/solution.py
@@ -204,10 +204,15 @@
     ]
     hot = jnp.concatenate(parts, axis=1)
     picked = jnp.zeros((half, channels), F32)
-    for index in range(positions // size):
-        keys = map_ref[index * size : (index + 1) * size, :]
-        rows = jnp.dot(hot, keys, preferred_element_type=F32)
-        picked = jnp.where(tile == index, rows, picked)
+    tiles = positions // size
+    beside = 2 if tiles % 2 == 0 else 1
+    for index in range(tiles // beside):
+        chosen = [index + side * (tiles // beside) for side in range(beside)]
+        keys = [map_ref[i * size : (i + 1) * size, :] for i in chosen]
+        rows = jnp.dot(hot, jnp.concatenate(keys, axis=1), preferred_element_type=F32)
+        for side, i in enumerate(chosen):
+            part = rows[:, side * channels : (side + 1) * channels]
+            picked = jnp.where(tile == i, part, picked)
     out_ref[...] = picked.astype(BF16)
 
 

time: 38.4 us -> 37.3 us (0.971)
  Pallas kernels: 11.2 us -> 10.1 us
  starting transfers between devices: 13.6 us -> 13 us
  waiting for transfers between devices: 10.7 us -> 11.2 us
    pallas_call x2, Pallas kernels: 2.57 us -> 1.5 us  [pick(): call(functools.partial(pick_kernel, core_flip), jax.ShapeDtypeStruct((hal...]
    ppermute x6, starting transfers between devices: 12.7 us -> 12.1 us  [space_swap(): return lax.ppermute(value, ('tm', 'space'), pairs)]
    ppermute x6, waiting for transfers between devices: 9.45 us -> 9.85 us  [space_swap(): return lax.ppermute(value, ('tm', 'space'), pairs)]
  transfers between devices with their start and end apart: 10 -> 10, of which waited for: 6 -> 7; matrix products, arithmetic and copies ran while one was open for 0% -> 0% of each run, Pallas kernels for 23% -> 22%
where the time goes in v10:
time: 37.3 us; the launch traced here: 37.1 us
  starting transfers between devices  13 us (35%)
  waiting for transfers between devices  11.2 us (30%)
  Pallas kernels  10.1 us (27%)
  local copies, waits for them, and re-layouts  1.58 us (4%)
  other arithmetic  0.93 us (2%)
    ppermute x6, starting transfers between devices, space_swap(): return lax.ppermute(value, ('tm', 'space'), pairs)  12.1 us
    ppermute x6, waiting for transfers between devices, space_swap(): return lax.ppermute(value, ('tm', 'space'), pairs)  9.85 us
    pallas_call x2, Pallas kernels, blocks_of(): call(functools.partial(half_kernel, rows_here, height, map_width), block,...  5.27 us
    unnamed x12, local copies, waits for them, and re-layouts  1.58 us
    pallas_call x2, Pallas kernels, pick(): call(functools.partial(pick_kernel, core_flip), jax.ShapeDtypeStruct((hal...  1.5 us
    ppermute x4, waiting for transfers between devices, core_swap(): return lax.ppermute(value, 'tm', [(0, 1), (1, 0)])  1.39 us
    pallas_call x1, Pallas kernels, local_pair(): call(functools.partial(coord_kernel, map_width), jax.ShapeDtypeStruct((po...  1.19 us
    pallas_call x1, Pallas kernels, local_pair(): call(track_kernel, jax.ShapeDtypeStruct((1, n_out, queries), F32), 9, flo...  1.16 us
  transfers between devices with their start and end apart: 10, of which 7 were waited for; matrix products, arithmetic and copies ran while one was open for 0% of the time, Pallas kernels for 22%

profile of v10, /device:TPU:0, one launch (start us, length us, event | category | flops | bytes accessed | tf_op | source)
XLA Modules:
  0.0 37.1 jit_solution(8194299928900127330)
XLA Ops:
  0.0 0.7 %add_select_fusion = s32[512]{0:T(512)S(1)} fusion(s32[512]{0:T(512)} %param.11, s32[512]{0:T(512)} %param.10, s32[512]{0:T(512)} %param.9, s32[]{:T(128)S(6)} %mul.9, s32[]{:T(128)S(6)} %axis_index.23), kind=kLoop, calls=%fused_computation | loop fusion | flops 4608 | bytes 8200 | tf_op jit(solution)/shard_map/jit(_where)/select_n | solution.py:496
  0.7 0.0 copy-start
  0.7 1.5 %copy-done = bf16[1,32,240,128]{3,2,1,0:T(8,128)(2,1)S(1)} copy-done((bf16[1,32,240,128]{3,2,1,0:T(8,128)(2,1)S(1)}, bf16[1,32,240,128]{3,2,1,0:T(8,128)(2,1)}, u32[]{:S(2)}) %copy-start) | copy-done | bytes 1966104
  2.3 0.8 %shard_map.83 = bf16[256,128]{1,0:T(8,128)(2,1)S(1)} custom-call(s32[1,512]{1,0:T(1,128)S(1)} %bitcast.6, bf16[7680,128]{1,0:T(8,128)(2,1)S(1)} %bitcast.2), custom_call_target="tpu_custom_call" | custom-call | flops 503316480 | bytes 1966080 | tf_op jit(solution)/shard_map/pallas_call | solution.py:499
  3.0 0.0 copy-start.1
  3.0 0.5 %collective-permute-start = (bf16[256,128]{1,0:T(8,128)(2,1)S(1)}, bf16[256,128]{1,0:T(8,128)(2,1)S(1)}, u32[]{:S(2)}, u32[]{:S(2)}) collective-permute-start(bf16[256,128]{1,0:T(8,128)(2,1)S(1)} %shard_map.83), channel_id=1, source_target_pairs={{0,4},{4,0},{1,5},{5,1},{2,6},{6,2},{3,7},{7,3},{8,12},{12,8},{9,1... | collective-permute-start | bytes 196616 | tf_op jit(solution)/shard_map/ppermute | solution.py:469
  3.6 0.8 %shard_map.82 = bf16[256,128]{1,0:T(8,128)(2,1)S(1)} custom-call(s32[1,512]{1,0:T(1,128)S(1)} %bitcast.7, bf16[7680,128]{1,0:T(8,128)(2,1)S(1)} %bitcast.3), custom_call_target="tpu_custom_call" | custom-call | flops 503316480 | bytes 1966080 | tf_op jit(solution)/shard_map/pallas_call | solution.py:499
  4.3 0.1 collective-permute-done
  4.5 3.0 %collective-permute-start.1 = (bf16[256,128]{1,0:T(8,128)(2,1)S(1)}, bf16[256,128]{1,0:T(8,128)(2,1)S(1)}, u32[]{:S(2)}, u32[]{:S(2)}) collective-permute-start(bf16[256,128]{1,0:T(8,128)(2,1)S(1)} %add.13), channel_id=1, source_target_pairs={{0,1},{1,0},{2,3},{3,2},{4,6},{5,7},{6,4},{7,5},{8,9},{9,8},{10,11... | collective-permute-start | bytes 196616 | tf_op jit(solution)/shard_map/ppermute | solution.py:480
  7.5 2.9 %collective-permute-done.1 = bf16[256,128]{1,0:T(8,128)(2,1)S(1)} collective-permute-done((bf16[256,128]{1,0:T(8,128)(2,1)S(1)}, bf16[256,128]{1,0:T(8,128)(2,1)S(1)}, u32[]{:S(2)}, u32[]{:S(2)}) %collective-permute-start.1) | collective-permute-done | bytes 65568 | tf_op jit(solution)/shard_map/ppermute | solution.py:480
  10.4 2.4 %collective-permute-start.2 = (bf16[256,128]{1,0:T(8,128)(2,1)S(1)}, bf16[256,128]{1,0:T(8,128)(2,1)S(1)}, u32[]{:S(2)}, u32[]{:S(2)}) collective-permute-start(bf16[256,128]{1,0:T(8,128)(2,1)S(1)} %add.14), channel_id=1, source_target_pairs={{0,2},{1,3},{2,0},{3,1},{4,5},{5,4},{6,7},{7,6},{8,10},{9,11},{10,... | collective-permute-start | bytes 196616 | tf_op jit(solution)/shard_map/ppermute | solution.py:480
  12.8 1.2 %shard_map.84.coord_ref = bf16[7680,128]{1,0:T(8,128)(2,1)S(1)} custom-call(s32[1,512]{1,0:T(1,128)S(1)} %bitcast.8), custom_call_target="tpu_custom_call" | custom-call | flops 7864320 | bytes 1966080 | tf_op jit(solution)/shard_map/pallas_call | solution.py:509
  14.0 1.6 %collective-permute-done.2 = bf16[256,128]{1,0:T(8,128)(2,1)S(1)} collective-permute-done((bf16[256,128]{1,0:T(8,128)(2,1)S(1)}, bf16[256,128]{1,0:T(8,128)(2,1)S(1)}, u32[]{:S(2)}, u32[]{:S(2)}) %collective-permute-start.2) | collective-permute-done | bytes 65568 | tf_op jit(solution)/shard_map/ppermute | solution.py:480
  15.7 0.1 collective-permute-start.5
  15.8 0.0 copy-done.1
  15.8 2.6 %shard_map.85 = f32[288,128]{1,0:T(8,128)S(1)} custom-call(bf16[256,128]{1,0:T(8,128)(2,1)S(1)} %add.15.query_ref, bf16[7680,128]{1,0:T(8,128)(2,1)S(1)} %bitcast.4, bf16[7680,128]{1,0:T(8,128)(2,1)S(1)} %shard_map.84.coord_ref), custom_call_target="tpu_custom_call" | custom-call | flops 1509949440 | bytes 3932160 | tf_op jit(solution)/shard_map/pallas_call | solution.py:526
  18.5 1.9 %collective-permute-start.3 = (f16[288,128]{1,0:T(8,128)(2,1)S(1)}, f16[288,128]{1,0:T(8,128)(2,1)S(1)}, u32[]{:S(2)}, u32[]{:S(2)}) collective-permute-start(f16[288,128]{1,0:T(8,128)(2,1)S(1)} %convert_element_type.36), channel_id=1, source_target_pairs={{0,1},{1,0},{2,3},{3,2},{4,6},{5,7},{6,4},{7,5},{8,9},{9,8},{10,11... | collective-permute-start | bytes 221192 | tf_op jit(solution)/shard_map/ppermute | solution.py:480
  20.3 0.0 collective-permute-done.5.query_ref
  20.3 2.6 %shard_map.88 = f32[288,128]{1,0:T(8,128)S(1)} custom-call(bf16[256,128]{1,0:T(8,128)(2,1)S(1)} %collective-permute-done.5.query_ref, bf16[7680,128]{1,0:T(8,128)(2,1)S(1)} %bitcast.5, bf16[7680,128]{1,0:T(8,128)(2,1)S(1)} %shard_map.84.coord_ref), custom_call_target="tpu_custom_call" | custom-call | flops 1509949440 | bytes 3932160 | tf_op jit(solution)/shard_map/pallas_call | solution.py:526
  23.0 0.0 copy-start.4
  23.0 0.0 copy-start.2
  23.0 0.0 copy-start.3
  23.0 0.0 copy-start.5
  23.1 0.3 collective-permute-start.6
  23.4 0.3 collective-permute-done.3
  23.7 0.3 shard_map.86
  24.0 2.3 %collective-permute-start.4 = (f16[288,128]{1,0:T(8,128)(2,1)S(1)}, f16[288,128]{1,0:T(8,128)(2,1)S(1)}, u32[]{:S(2)}, u32[]{:S(2)}) collective-permute-start(f16[288,128]{1,0:T(8,128)(2,1)S(1)} %convert_element_type.39), channel_id=1, source_target_pairs={{0,2},{1,3},{2,0},{3,1},{4,5},{5,4},{6,7},{7,6},{8,10},{9,11},{10,... | collective-permute-start | bytes 221192 | tf_op jit(solution)/shard_map/ppermute | solution.py:480
  26.3 2.3 %collective-permute-done.6 = f16[288,128]{1,0:T(8,128)(2,1)S(1)} collective-permute-done((f16[288,128]{1,0:T(8,128)(2,1)S(1)}, f16[288,128]{1,0:T(8,128)(2,1)S(1)}, u32[]{:S(2)}, u32[]{:S(2)}) %collective-permute-start.6) | collective-permute-done | bytes 73760 | tf_op jit(solution)/shard_map/ppermute | solution.py:480
  28.6 0.3 shard_map.89
  28.9 2.3 %collective-permute-start.7 = (f16[288,128]{1,0:T(8,128)(2,1)S(1)}, f16[288,128]{1,0:T(8,128)(2,1)S(1)}, u32[]{:S(2)}, u32[]{:S(2)}) collective-permute-start(f16[288,128]{1,0:T(8,128)(2,1)S(1)} %convert_element_type.45), channel_id=1, source_target_pairs={{0,2},{1,3},{2,0},{3,1},{4,5},{5,4},{6,7},{7,6},{8,10},{9,11},{10,... | collective-permute-start | bytes 221192 | tf_op jit(solution)/shard_map/ppermute | solution.py:480
  31.2 0.0 collective-permute-done.4
  31.2 0.0 copy-done.4
  31.2 0.3 shard_map.87
  31.5 0.2 collective-permute-start.8
  31.7 2.7 %collective-permute-done.7 = f16[288,128]{1,0:T(8,128)(2,1)S(1)} collective-permute-done((f16[288,128]{1,0:T(8,128)(2,1)S(1)}, f16[288,128]{1,0:T(8,128)(2,1)S(1)}, u32[]{:S(2)}, u32[]{:S(2)}) %collective-permute-start.7) | collective-permute-done | bytes 73760 | tf_op jit(solution)/shard_map/ppermute | solution.py:480
  34.3 0.3 shard_map.90
  34.6 0.1 collective-permute-start.9
  34.7 0.0 collective-permute-done.8.near_came
  34.7 1.2 %collective-permute-done.9.far_came = bf16[272,128]{1,0:T(8,128)(2,1)S(1)} collective-permute-done((bf16[272,128]{1,0:T(8,128)(2,1)S(1)}, bf16[272,128]{1,0:T(8,128)(2,1)S(1)}, u32[]{:S(2)}, u32[]{:S(2)}) %collective-permute-start.9) | collective-permute-done | bytes 69664 | tf_op jit(solution)/shard_map/ppermute | solution.py:469
  35.9 0.0 copy-done.2
  35.9 0.0 copy-done.3
  35.9 0.0 copy-done.5
  35.9 1.2 %shard_map.91 = f32[1,2,512]{2,1,0:T(2,128)} custom-call(f32[3,128]{1,0:T(4,128)S(1)} %copy-done.3, bf16[128,128]{1,0:T(8,128)(2,1)S(1)} %copy-done.2, f32[2,128]{1,0:T(2,128)S(1)} %copy-done.5, f32[2,256]{1,0:T(2,128)S(1)} %get-tuple-element.9.near_place, f32[2,256]{1,0:T(2,128)S(1)} %get-tuple-element.10.far_place, ...), custom_call_target="tpu_custom_call" | custom-call | flops 67108864 | bytes 524288 | tf_op jit(solution)/shard_map/pallas_call | solution.py:569
  (15 shorter events, 0.2 us)
Async XLA Ops:
  0.7 1.5 %copy-start = (bf16[1,32,240,128]{3,2,1,0:T(8,128)(2,1)S(1)}, bf16[1,32,240,128]{3,2,1,0:T(8,128)(2,1)}, u32[]{:S(2)}) copy-start(bf16[1,32,240,128]{3,2,1,0:T(8,128)(2,1)} %param.8) | copy-start | bytes 5898244
  3.0 12.8 %copy-start.1 = (bf16[1,32,240,128]{3,2,1,0:T(8,128)(2,1)S(1)}, bf16[1,32,240,128]{3,2,1,0:T(8,128)(2,1)}, u32[]{:S(2)}) copy-start(bf16[1,32,240,128]{3,2,1,0:T(8,128)(2,1)} %param.8) | copy-start | bytes 5898244
  3.0 1.4 %collective-permute-start = (bf16[256,128]{1,0:T(8,128)(2,1)S(1)}, bf16[256,128]{1,0:T(8,128)(2,1)S(1)}, u32[]{:S(2)}, u32[]{:S(2)}) collective-permute-start(bf16[256,128]{1,0:T(8,128)(2,1)S(1)} %shard_map.83), channel_id=1, source_target_pairs={{0,4},{4,0},{1,5},{5,1},{2,6},{6,2},{3,7},{7,3},{8,12},{12,8},{9,1... | collective-permute-start | bytes 196616 | tf_op jit(solution)/shard_map/ppermute | solution.py:469
  4.5 5.9 %collective-permute-start.1 = (bf16[256,128]{1,0:T(8,128)(2,1)S(1)}, bf16[256,128]{1,0:T(8,128)(2,1)S(1)}, u32[]{:S(2)}, u32[]{:S(2)}) collective-permute-start(bf16[256,128]{1,0:T(8,128)(2,1)S(1)} %add.13), channel_id=1, source_target_pairs={{0,1},{1,0},{2,3},{3,2},{4,6},{5,7},{6,4},{7,5},{8,9},{9,8},{10,11... | collective-permute-start | bytes 196616 | tf_op jit(solution)/shard_map/ppermute | solution.py:480
  10.4 5.2 %collective-permute-start.2 = (bf16[256,128]{1,0:T(8,128)(2,1)S(1)}, bf16[256,128]{1,0:T(8,128)(2,1)S(1)}, u32[]{:S(2)}, u32[]{:S(2)}) collective-permute-start(bf16[256,128]{1,0:T(8,128)(2,1)S(1)} %add.14), channel_id=1, source_target_pairs={{0,2},{1,3},{2,0},{3,1},{4,5},{5,4},{6,7},{7,6},{8,10},{9,11},{10,... | collective-permute-start | bytes 196616 | tf_op jit(solution)/shard_map/ppermute | solution.py:480
  15.7 4.6 %collective-permute-start.5 = (bf16[256,128]{1,0:T(8,128)(2,1)S(1)}, bf16[256,128]{1,0:T(8,128)(2,1)S(1)}, u32[]{:S(2)}, u32[]{:S(2)}) collective-permute-start(bf16[256,128]{1,0:T(8,128)(2,1)S(1)} %add.15.query_ref), channel_id=1, source_target_pairs={{0,4},{4,0},{1,5},{5,1},{2,6},{6,2},{3,7},{7,3},{8,12},{12,8},{9,1... | collective-permute-start | bytes 196616 | tf_op jit(solution)/shard_map/ppermute | solution.py:469
  18.5 5.2 %collective-permute-start.3 = (f16[288,128]{1,0:T(8,128)(2,1)S(1)}, f16[288,128]{1,0:T(8,128)(2,1)S(1)}, u32[]{:S(2)}, u32[]{:S(2)}) collective-permute-start(f16[288,128]{1,0:T(8,128)(2,1)S(1)} %convert_element_type.36), channel_id=1, source_target_pairs={{0,1},{1,0},{2,3},{3,2},{4,6},{5,7},{6,4},{7,5},{8,9},{9,8},{10,11... | collective-permute-start | bytes 221192 | tf_op jit(solution)/shard_map/ppermute | solution.py:480
  23.0 8.2 %copy-start.4 = (f32[1,128]{1,0:T(1,128)S(1)}, f32[1,128]{1,0:T(1,128)}, u32[]{:S(2)}) copy-start(f32[1,128]{1,0:T(1,128)} %decay_ref.3) | copy-start | bytes 1540
  23.0 12.9 %copy-start.2 = (bf16[128,128]{1,0:T(8,128)(2,1)S(1)}, bf16[128,128]{1,0:T(8,128)(2,1)}, u32[]{:S(2)}) copy-start(bf16[128,128]{1,0:T(8,128)(2,1)} %pw_ref.1) | copy-start | bytes 98308
  23.0 12.9 %copy-start.3 = (f32[3,128]{1,0:T(4,128)S(1)}, f32[3,128]{1,0:T(4,128)}, u32[]{:S(2)}) copy-start(f32[3,128]{1,0:T(4,128)} %dw_ref.1) | copy-start | bytes 4612
  23.0 12.9 %copy-start.5 = (f32[2,128]{1,0:T(2,128)S(1)}, f32[2,128]{1,0:T(2,128)}, u32[]{:S(2)}) copy-start(f32[2,128]{1,0:T(2,128)} %ow_ref.1) | copy-start | bytes 3076
  23.1 5.5 %collective-permute-start.6 = (f16[288,128]{1,0:T(8,128)(2,1)S(1)}, f16[288,128]{1,0:T(8,128)(2,1)S(1)}, u32[]{:S(2)}, u32[]{:S(2)}) collective-permute-start(f16[288,128]{1,0:T(8,128)(2,1)S(1)} %convert_element_type.42), channel_id=1, source_target_pairs={{0,1},{1,0},{2,3},{3,2},{4,6},{5,7},{6,4},{7,5},{8,9},{9,8},{10,11... | collective-permute-start | bytes 221192 | tf_op jit(solution)/shard_map/ppermute | solution.py:480
  24.0 7.2 %collective-permute-start.4 = (f16[288,128]{1,0:T(8,128)(2,1)S(1)}, f16[288,128]{1,0:T(8,128)(2,1)S(1)}, u32[]{:S(2)}, u32[]{:S(2)}) collective-permute-start(f16[288,128]{1,0:T(8,128)(2,1)S(1)} %convert_element_type.39), channel_id=1, source_target_pairs={{0,2},{1,3},{2,0},{3,1},{4,5},{5,4},{6,7},{7,6},{8,10},{9,11},{10,... | collective-permute-start | bytes 221192 | tf_op jit(solution)/shard_map/ppermute | solution.py:480
  28.9 5.4 %collective-permute-start.7 = (f16[288,128]{1,0:T(8,128)(2,1)S(1)}, f16[288,128]{1,0:T(8,128)(2,1)S(1)}, u32[]{:S(2)}, u32[]{:S(2)}) collective-permute-start(f16[288,128]{1,0:T(8,128)(2,1)S(1)} %convert_element_type.45), channel_id=1, source_target_pairs={{0,2},{1,3},{2,0},{3,1},{4,5},{5,4},{6,7},{7,6},{8,10},{9,11},{10,... | collective-permute-start | bytes 221192 | tf_op jit(solution)/shard_map/ppermute | solution.py:480
  31.5 3.2 %collective-permute-start.8 = (bf16[272,128]{1,0:T(8,128)(2,1)S(1)}, bf16[272,128]{1,0:T(8,128)(2,1)S(1)}, u32[]{:S(2)}, u32[]{:S(2)}) collective-permute-start(bf16[272,128]{1,0:T(8,128)(2,1)S(1)} %get-tuple-element.11.near_mine), channel_id=1, source_target_pairs={{0,4},{4,0},{1,5},{5,1},{2,6},{6,2},{3,7},{7,3},{8,12},{12,8},{9,1... | collective-permute-start | bytes 208904 | tf_op jit(solution)/shard_map/ppermute | solution.py:469
  34.6 1.3 %collective-permute-start.9 = (bf16[272,128]{1,0:T(8,128)(2,1)S(1)}, bf16[272,128]{1,0:T(8,128)(2,1)S(1)}, u32[]{:S(2)}, u32[]{:S(2)}) collective-permute-start(bf16[272,128]{1,0:T(8,128)(2,1)S(1)} %get-tuple-element.12.far_mine), channel_id=1, source_target_pairs={{0,4},{4,0},{1,5},{5,1},{2,6},{6,2},{3,7},{7,3},{8,12},{12,8},{9,1... | collective-permute-start | bytes 208904 | tf_op jit(solution)/shard_map/ppermute | solution.py:469

commit v11 on v10

--- a/solution.py
+++ b/solution.py
@@ -245,7 +245,7 @@
     factor = math.log2(math.e) / math.sqrt(channels)
     query = query_ref[...]
     first_row = (lax.axis_index("space") * rows_here).astype(F32)
-    chunk = pick_chunk(positions, 2560)
+    chunk = pick_chunk(positions, 3840)
 
     def score(base):
         keys = map_ref[base : base + chunk, :]

time: 37.3 us -> 39.2 us (1.051)
  Pallas kernels: 10.1 us -> 11.5 us
  waiting for transfers between devices: 11.2 us -> 12.3 us
  starting transfers between devices: 13 us -> 12.5 us
    pallas_call x2, Pallas kernels: 5.27 us -> 6.64 us  [blocks_of(): call(functools.partial(half_kernel, rows_here, height, map_width), block,...]
    ppermute x6, waiting for transfers between devices: 9.85 us -> 10.9 us  [space_swap(): return lax.ppermute(value, ('tm', 'space'), pairs)]
    ppermute x6, starting transfers between devices: 12.1 us -> 11.7 us  [space_swap(): return lax.ppermute(value, ('tm', 'space'), pairs)]
  transfers between devices with their start and end apart: 10 -> 10, of which waited for: 7 -> 6; matrix products, arithmetic and copies ran while one was open for 0% -> 0% of each run, Pallas kernels for 22% -> 25%
where the time goes in v11:
time: 39.2 us; the launch traced here: 39 us
  starting transfers between devices  12.5 us (32%)
  waiting for transfers between devices  12.3 us (31%)
  Pallas kernels  11.5 us (29%)
  local copies, waits for them, and re-layouts  1.58 us (4%)
  other arithmetic  0.93 us (2%)
    ppermute x6, starting transfers between devices, space_swap(): return lax.ppermute(value, ('tm', 'space'), pairs)  11.7 us
    ppermute x6, waiting for transfers between devices, space_swap(): return lax.ppermute(value, ('tm', 'space'), pairs)  10.9 us
    pallas_call x2, Pallas kernels, blocks_of(): call(functools.partial(half_kernel, rows_here, height, map_width), block,...  6.64 us
    unnamed x12, local copies, waits for them, and re-layouts  1.58 us
    pallas_call x2, Pallas kernels, pick(): call(functools.partial(pick_kernel, core_flip), jax.ShapeDtypeStruct((hal...  1.5 us
    ppermute x4, waiting for transfers between devices, core_swap(): return lax.ppermute(value, 'tm', [(0, 1), (1, 0)])  1.39 us
    pallas_call x1, Pallas kernels, local_pair(): call(functools.partial(coord_kernel, map_width), jax.ShapeDtypeStruct((po...  1.19 us
    pallas_call x1, Pallas kernels, local_pair(): call(track_kernel, jax.ShapeDtypeStruct((1, n_out, queries), F32), 9, flo...  1.16 us
  transfers between devices with their start and end apart: 10, of which 6 were waited for; matrix products, arithmetic and copies ran while one was open for 0% of the time, Pallas kernels for 25%

profile of v11, /device:TPU:0, one launch (start us, length us, event | category | flops | bytes accessed | tf_op | source)
XLA Modules:
  0.0 39.0 jit_solution(7704739078871967105)
XLA Ops:
  0.0 0.7 %add_select_fusion = s32[512]{0:T(512)S(1)} fusion(s32[512]{0:T(512)} %param.11, s32[512]{0:T(512)} %param.10, s32[512]{0:T(512)} %param.9, s32[]{:T(128)S(6)} %mul.9, s32[]{:T(128)S(6)} %axis_index.23), kind=kLoop, calls=%fused_computation | loop fusion | flops 4608 | bytes 8200 | tf_op jit(solution)/shard_map/jit(_where)/select_n | solution.py:496
  0.7 0.0 copy-start
  0.7 1.5 %copy-done = bf16[1,32,240,128]{3,2,1,0:T(8,128)(2,1)S(1)} copy-done((bf16[1,32,240,128]{3,2,1,0:T(8,128)(2,1)S(1)}, bf16[1,32,240,128]{3,2,1,0:T(8,128)(2,1)}, u32[]{:S(2)}) %copy-start) | copy-done | bytes 1966104
  2.3 0.8 %shard_map.83 = bf16[256,128]{1,0:T(8,128)(2,1)S(1)} custom-call(s32[1,512]{1,0:T(1,128)S(1)} %bitcast.6, bf16[7680,128]{1,0:T(8,128)(2,1)S(1)} %bitcast.2), custom_call_target="tpu_custom_call" | custom-call | flops 503316480 | bytes 1966080 | tf_op jit(solution)/shard_map/pallas_call | solution.py:499
  3.0 0.0 copy-start.1
  3.0 0.5 %collective-permute-start = (bf16[256,128]{1,0:T(8,128)(2,1)S(1)}, bf16[256,128]{1,0:T(8,128)(2,1)S(1)}, u32[]{:S(2)}, u32[]{:S(2)}) collective-permute-start(bf16[256,128]{1,0:T(8,128)(2,1)S(1)} %shard_map.83), channel_id=1, source_target_pairs={{0,4},{4,0},{1,5},{5,1},{2,6},{6,2},{3,7},{7,3},{8,12},{12,8},{9,1... | collective-permute-start | bytes 196616 | tf_op jit(solution)/shard_map/ppermute | solution.py:469
  3.6 0.8 %shard_map.82 = bf16[256,128]{1,0:T(8,128)(2,1)S(1)} custom-call(s32[1,512]{1,0:T(1,128)S(1)} %bitcast.7, bf16[7680,128]{1,0:T(8,128)(2,1)S(1)} %bitcast.3), custom_call_target="tpu_custom_call" | custom-call | flops 503316480 | bytes 1966080 | tf_op jit(solution)/shard_map/pallas_call | solution.py:499
  4.3 0.1 collective-permute-done
  4.5 3.0 %collective-permute-start.1 = (bf16[256,128]{1,0:T(8,128)(2,1)S(1)}, bf16[256,128]{1,0:T(8,128)(2,1)S(1)}, u32[]{:S(2)}, u32[]{:S(2)}) collective-permute-start(bf16[256,128]{1,0:T(8,128)(2,1)S(1)} %add.13), channel_id=1, source_target_pairs={{0,1},{1,0},{2,3},{3,2},{4,6},{5,7},{6,4},{7,5},{8,9},{9,8},{10,11... | collective-permute-start | bytes 196616 | tf_op jit(solution)/shard_map/ppermute | solution.py:480
  7.5 2.9 %collective-permute-done.1 = bf16[256,128]{1,0:T(8,128)(2,1)S(1)} collective-permute-done((bf16[256,128]{1,0:T(8,128)(2,1)S(1)}, bf16[256,128]{1,0:T(8,128)(2,1)S(1)}, u32[]{:S(2)}, u32[]{:S(2)}) %collective-permute-start.1) | collective-permute-done | bytes 65568 | tf_op jit(solution)/shard_map/ppermute | solution.py:480
  10.4 2.4 %collective-permute-start.2 = (bf16[256,128]{1,0:T(8,128)(2,1)S(1)}, bf16[256,128]{1,0:T(8,128)(2,1)S(1)}, u32[]{:S(2)}, u32[]{:S(2)}) collective-permute-start(bf16[256,128]{1,0:T(8,128)(2,1)S(1)} %add.14), channel_id=1, source_target_pairs={{0,2},{1,3},{2,0},{3,1},{4,5},{5,4},{6,7},{7,6},{8,10},{9,11},{10,... | collective-permute-start | bytes 196616 | tf_op jit(solution)/shard_map/ppermute | solution.py:480
  12.8 1.2 %shard_map.84.coord_ref = bf16[7680,128]{1,0:T(8,128)(2,1)S(1)} custom-call(s32[1,512]{1,0:T(1,128)S(1)} %bitcast.8), custom_call_target="tpu_custom_call" | custom-call | flops 7864320 | bytes 1966080 | tf_op jit(solution)/shard_map/pallas_call | solution.py:509
  14.0 1.6 %collective-permute-done.2 = bf16[256,128]{1,0:T(8,128)(2,1)S(1)} collective-permute-done((bf16[256,128]{1,0:T(8,128)(2,1)S(1)}, bf16[256,128]{1,0:T(8,128)(2,1)S(1)}, u32[]{:S(2)}, u32[]{:S(2)}) %collective-permute-start.2) | collective-permute-done | bytes 65568 | tf_op jit(solution)/shard_map/ppermute | solution.py:480
  15.7 0.1 collective-permute-start.5
  15.8 0.0 copy-done.1
  15.8 3.3 %shard_map.85 = f32[288,128]{1,0:T(8,128)S(1)} custom-call(bf16[256,128]{1,0:T(8,128)(2,1)S(1)} %add.15.query_ref, bf16[7680,128]{1,0:T(8,128)(2,1)S(1)} %bitcast.4, bf16[7680,128]{1,0:T(8,128)(2,1)S(1)} %shard_map.84.coord_ref), custom_call_target="tpu_custom_call" | custom-call | flops 1509949440 | bytes 3932160 | tf_op jit(solution)/shard_map/pallas_call | solution.py:526
  19.1 1.9 %collective-permute-start.3 = (f16[288,128]{1,0:T(8,128)(2,1)S(1)}, f16[288,128]{1,0:T(8,128)(2,1)S(1)}, u32[]{:S(2)}, u32[]{:S(2)}) collective-permute-start(f16[288,128]{1,0:T(8,128)(2,1)S(1)} %convert_element_type.36), channel_id=1, source_target_pairs={{0,1},{1,0},{2,3},{3,2},{4,6},{5,7},{6,4},{7,5},{8,9},{9,8},{10,11... | collective-permute-start | bytes 221192 | tf_op jit(solution)/shard_map/ppermute | solution.py:480
  21.0 0.0 collective-permute-done.5.query_ref
  21.0 3.3 %shard_map.88 = f32[288,128]{1,0:T(8,128)S(1)} custom-call(bf16[256,128]{1,0:T(8,128)(2,1)S(1)} %collective-permute-done.5.query_ref, bf16[7680,128]{1,0:T(8,128)(2,1)S(1)} %bitcast.5, bf16[7680,128]{1,0:T(8,128)(2,1)S(1)} %shard_map.84.coord_ref), custom_call_target="tpu_custom_call" | custom-call | flops 1509949440 | bytes 3932160 | tf_op jit(solution)/shard_map/pallas_call | solution.py:526
  24.4 0.0 copy-start.4
  24.4 0.0 copy-start.2
  24.4 0.0 copy-start.3
  24.4 0.0 copy-start.5
  24.4 0.3 collective-permute-start.6
  24.7 0.0 collective-permute-done.3
  24.8 0.3 shard_map.86
  25.0 2.6 %collective-permute-start.4 = (f16[288,128]{1,0:T(8,128)(2,1)S(1)}, f16[288,128]{1,0:T(8,128)(2,1)S(1)}, u32[]{:S(2)}, u32[]{:S(2)}) collective-permute-start(f16[288,128]{1,0:T(8,128)(2,1)S(1)} %convert_element_type.39), channel_id=1, source_target_pairs={{0,2},{1,3},{2,0},{3,1},{4,5},{5,4},{6,7},{7,6},{8,10},{9,11},{10,... | collective-permute-start | bytes 221192 | tf_op jit(solution)/shard_map/ppermute | solution.py:480
  27.6 3.1 %collective-permute-done.6 = f16[288,128]{1,0:T(8,128)(2,1)S(1)} collective-permute-done((f16[288,128]{1,0:T(8,128)(2,1)S(1)}, f16[288,128]{1,0:T(8,128)(2,1)S(1)}, u32[]{:S(2)}, u32[]{:S(2)}) %collective-permute-start.6) | collective-permute-done | bytes 73760 | tf_op jit(solution)/shard_map/ppermute | solution.py:480
  30.7 0.3 shard_map.89
  31.0 1.6 %collective-permute-start.7 = (f16[288,128]{1,0:T(8,128)(2,1)S(1)}, f16[288,128]{1,0:T(8,128)(2,1)S(1)}, u32[]{:S(2)}, u32[]{:S(2)}) collective-permute-start(f16[288,128]{1,0:T(8,128)(2,1)S(1)} %convert_element_type.45), channel_id=1, source_target_pairs={{0,2},{1,3},{2,0},{3,1},{4,5},{5,4},{6,7},{7,6},{8,10},{9,11},{10,... | collective-permute-start | bytes 221192 | tf_op jit(solution)/shard_map/ppermute | solution.py:480
  32.6 0.0 collective-permute-done.4
  32.6 0.0 copy-done.4
  32.6 0.3 shard_map.87
  32.9 0.2 collective-permute-start.8
  33.0 3.2 %collective-permute-done.7 = f16[288,128]{1,0:T(8,128)(2,1)S(1)} collective-permute-done((f16[288,128]{1,0:T(8,128)(2,1)S(1)}, f16[288,128]{1,0:T(8,128)(2,1)S(1)}, u32[]{:S(2)}, u32[]{:S(2)}) %collective-permute-start.7) | collective-permute-done | bytes 73760 | tf_op jit(solution)/shard_map/ppermute | solution.py:480
  36.3 0.3 shard_map.90
  36.5 0.1 collective-permute-start.9
  36.6 0.0 collective-permute-done.8.near_came
  36.6 1.2 %collective-permute-done.9.far_came = bf16[272,128]{1,0:T(8,128)(2,1)S(1)} collective-permute-done((bf16[272,128]{1,0:T(8,128)(2,1)S(1)}, bf16[272,128]{1,0:T(8,128)(2,1)S(1)}, u32[]{:S(2)}, u32[]{:S(2)}) %collective-permute-start.9) | collective-permute-done | bytes 69664 | tf_op jit(solution)/shard_map/ppermute | solution.py:469
  37.9 0.0 copy-done.2
  37.9 0.0 copy-done.3
  37.9 0.0 copy-done.5
  37.9 1.2 %shard_map.91 = f32[1,2,512]{2,1,0:T(2,128)} custom-call(f32[3,128]{1,0:T(4,128)S(1)} %copy-done.3, bf16[128,128]{1,0:T(8,128)(2,1)S(1)} %copy-done.2, f32[2,128]{1,0:T(2,128)S(1)} %copy-done.5, f32[2,256]{1,0:T(2,128)S(1)} %get-tuple-element.9.near_place, f32[2,256]{1,0:T(2,128)S(1)} %get-tuple-element.10.far_place, ...), custom_call_target="tpu_custom_call" | custom-call | flops 67108864 | bytes 524288 | tf_op jit(solution)/shard_map/pallas_call | solution.py:569
  (15 shorter events, 0.2 us)
Async XLA Ops:
  0.7 1.5 %copy-start = (bf16[1,32,240,128]{3,2,1,0:T(8,128)(2,1)S(1)}, bf16[1,32,240,128]{3,2,1,0:T(8,128)(2,1)}, u32[]{:S(2)}) copy-start(bf16[1,32,240,128]{3,2,1,0:T(8,128)(2,1)} %param.8) | copy-start | bytes 5898244
  3.0 12.8 %copy-start.1 = (bf16[1,32,240,128]{3,2,1,0:T(8,128)(2,1)S(1)}, bf16[1,32,240,128]{3,2,1,0:T(8,128)(2,1)}, u32[]{:S(2)}) copy-start(bf16[1,32,240,128]{3,2,1,0:T(8,128)(2,1)} %param.8) | copy-start | bytes 5898244
  3.0 1.4 %collective-permute-start = (bf16[256,128]{1,0:T(8,128)(2,1)S(1)}, bf16[256,128]{1,0:T(8,128)(2,1)S(1)}, u32[]{:S(2)}, u32[]{:S(2)}) collective-permute-start(bf16[256,128]{1,0:T(8,128)(2,1)S(1)} %shard_map.83), channel_id=1, source_target_pairs={{0,4},{4,0},{1,5},{5,1},{2,6},{6,2},{3,7},{7,3},{8,12},{12,8},{9,1... | collective-permute-start | bytes 196616 | tf_op jit(solution)/shard_map/ppermute | solution.py:469
  4.5 5.9 %collective-permute-start.1 = (bf16[256,128]{1,0:T(8,128)(2,1)S(1)}, bf16[256,128]{1,0:T(8,128)(2,1)S(1)}, u32[]{:S(2)}, u32[]{:S(2)}) collective-permute-start(bf16[256,128]{1,0:T(8,128)(2,1)S(1)} %add.13), channel_id=1, source_target_pairs={{0,1},{1,0},{2,3},{3,2},{4,6},{5,7},{6,4},{7,5},{8,9},{9,8},{10,11... | collective-permute-start | bytes 196616 | tf_op jit(solution)/shard_map/ppermute | solution.py:480
  10.4 5.2 %collective-permute-start.2 = (bf16[256,128]{1,0:T(8,128)(2,1)S(1)}, bf16[256,128]{1,0:T(8,128)(2,1)S(1)}, u32[]{:S(2)}, u32[]{:S(2)}) collective-permute-start(bf16[256,128]{1,0:T(8,128)(2,1)S(1)} %add.14), channel_id=1, source_target_pairs={{0,2},{1,3},{2,0},{3,1},{4,5},{5,4},{6,7},{7,6},{8,10},{9,11},{10,... | collective-permute-start | bytes 196616 | tf_op jit(solution)/shard_map/ppermute | solution.py:480
  15.7 5.3 %collective-permute-start.5 = (bf16[256,128]{1,0:T(8,128)(2,1)S(1)}, bf16[256,128]{1,0:T(8,128)(2,1)S(1)}, u32[]{:S(2)}, u32[]{:S(2)}) collective-permute-start(bf16[256,128]{1,0:T(8,128)(2,1)S(1)} %add.15.query_ref), channel_id=1, source_target_pairs={{0,4},{4,0},{1,5},{5,1},{2,6},{6,2},{3,7},{7,3},{8,12},{12,8},{9,1... | collective-permute-start | bytes 196616 | tf_op jit(solution)/shard_map/ppermute | solution.py:469
  19.1 5.6 %collective-permute-start.3 = (f16[288,128]{1,0:T(8,128)(2,1)S(1)}, f16[288,128]{1,0:T(8,128)(2,1)S(1)}, u32[]{:S(2)}, u32[]{:S(2)}) collective-permute-start(f16[288,128]{1,0:T(8,128)(2,1)S(1)} %convert_element_type.36), channel_id=1, source_target_pairs={{0,1},{1,0},{2,3},{3,2},{4,6},{5,7},{6,4},{7,5},{8,9},{9,8},{10,11... | collective-permute-start | bytes 221192 | tf_op jit(solution)/shard_map/ppermute | solution.py:480
  24.4 8.2 %copy-start.4 = (f32[1,128]{1,0:T(1,128)S(1)}, f32[1,128]{1,0:T(1,128)}, u32[]{:S(2)}) copy-start(f32[1,128]{1,0:T(1,128)} %decay_ref.3) | copy-start | bytes 1540
  24.4 13.5 %copy-start.2 = (bf16[128,128]{1,0:T(8,128)(2,1)S(1)}, bf16[128,128]{1,0:T(8,128)(2,1)}, u32[]{:S(2)}) copy-start(bf16[128,128]{1,0:T(8,128)(2,1)} %pw_ref.1) | copy-start | bytes 98308
  24.4 13.5 %copy-start.3 = (f32[3,128]{1,0:T(4,128)S(1)}, f32[3,128]{1,0:T(4,128)}, u32[]{:S(2)}) copy-start(f32[3,128]{1,0:T(4,128)} %dw_ref.1) | copy-start | bytes 4612
  24.4 13.5 %copy-start.5 = (f32[2,128]{1,0:T(2,128)S(1)}, f32[2,128]{1,0:T(2,128)}, u32[]{:S(2)}) copy-start(f32[2,128]{1,0:T(2,128)} %ow_ref.1) | copy-start | bytes 3076
  24.4 6.2 %collective-permute-start.6 = (f16[288,128]{1,0:T(8,128)(2,1)S(1)}, f16[288,128]{1,0:T(8,128)(2,1)S(1)}, u32[]{:S(2)}, u32[]{:S(2)}) collective-permute-start(f16[288,128]{1,0:T(8,128)(2,1)S(1)} %convert_element_type.42), channel_id=1, source_target_pairs={{0,1},{1,0},{2,3},{3,2},{4,6},{5,7},{6,4},{7,5},{8,9},{9,8},{10,11... | collective-permute-start | bytes 221192 | tf_op jit(solution)/shard_map/ppermute | solution.py:480
  25.0 7.5 %collective-permute-start.4 = (f16[288,128]{1,0:T(8,128)(2,1)S(1)}, f16[288,128]{1,0:T(8,128)(2,1)S(1)}, u32[]{:S(2)}, u32[]{:S(2)}) collective-permute-start(f16[288,128]{1,0:T(8,128)(2,1)S(1)} %convert_element_type.39), channel_id=1, source_target_pairs={{0,2},{1,3},{2,0},{3,1},{4,5},{5,4},{6,7},{7,6},{8,10},{9,11},{10,... | collective-permute-start | bytes 221192 | tf_op jit(solution)/shard_map/ppermute | solution.py:480
  31.0 5.3 %collective-permute-start.7 = (f16[288,128]{1,0:T(8,128)(2,1)S(1)}, f16[288,128]{1,0:T(8,128)(2,1)S(1)}, u32[]{:S(2)}, u32[]{:S(2)}) collective-permute-start(f16[288,128]{1,0:T(8,128)(2,1)S(1)} %convert_element_type.45), channel_id=1, source_target_pairs={{0,2},{1,3},{2,0},{3,1},{4,5},{5,4},{6,7},{7,6},{8,10},{9,11},{10,... | collective-permute-start | bytes 221192 | tf_op jit(solution)/shard_map/ppermute | solution.py:480
  32.9 3.8 %collective-permute-start.8 = (bf16[272,128]{1,0:T(8,128)(2,1)S(1)}, bf16[272,128]{1,0:T(8,128)(2,1)S(1)}, u32[]{:S(2)}, u32[]{:S(2)}) collective-permute-start(bf16[272,128]{1,0:T(8,128)(2,1)S(1)} %get-tuple-element.11.near_mine), channel_id=1, source_target_pairs={{0,4},{4,0},{1,5},{5,1},{2,6},{6,2},{3,7},{7,3},{8,12},{12,8},{9,1... | collective-permute-start | bytes 208904 | tf_op jit(solution)/shard_map/ppermute | solution.py:469
  36.5 1.3 %collective-permute-start.9 = (bf16[272,128]{1,0:T(8,128)(2,1)S(1)}, bf16[272,128]{1,0:T(8,128)(2,1)S(1)}, u32[]{:S(2)}, u32[]{:S(2)}) collective-permute-start(bf16[272,128]{1,0:T(8,128)(2,1)S(1)} %get-tuple-element.12.far_mine), channel_id=1, source_target_pairs={{0,4},{4,0},{1,5},{5,1},{2,6},{6,2},{3,7},{7,3},{8,12},{12,8},{9,1... | collective-permute-start | bytes 208904 | tf_op jit(solution)/shard_map/ppermute | solution.py:469
